TPU v7x, 128 devices: a whole 4x4x4 slice. The times are simulated.
128 devices in a mesh: slab: 4 (over y), energy: 32 (over x, z, core).
Axes of the slice: x: 4, y: 4, z: 4, core: 2. Of those that a mesh axis runs over, the one named last changes fastest.
Arguments:
- g_lesser: float32 [2, 512, 131072], P(None, 'energy', 'slab'), may hold values from -6 to 6
- g_greater: float32 [2, 512, 131072], P(None, 'energy', 'slab'), may hold values from -6 to 6
- live_columns: int32 [131072], P('slab'), may hold values from 0 to 32767, as said below
- live_count: int32 [4], P('slab'), may hold values from 8192 to 16384, as said below
- mirror: int32 [131072], P('slab'), may hold values from 0 to 32767, as said below
Outputs:
- polar_lesser: float32 [2, 512, 131072], P(None, 'energy', 'slab')
Inputs may be any that keep to these rules, and one draw needn't show every extreme that they name: `live_columns`: each slab's 32768 entries are a permutation of the slab's columns 0 .. 32767; the first live_count entries name its live pairs. `live_count`: A slab and its mirror-image slab (the one at the same place counted from the other end) hold equal counts; some slab holds exactly 16384 live pairs in every draw. Between a slab and its mirror-image slab the map is a bijection that is its own inverse and takes live pairs to live pairs.
All inputs are finite; a program needn't handle non-finite values.
Results may differ from a plain program's by a relative error of at most 0.0003.
Values sent between devices are 32-bit elements; how exact they have to be, the bound alone decides.
No kernel may reach another device: no remote copies, remote signals or barrier semaphores. Data moves between devices by JAX's collectives and lax.ppermute only.
A program may use at most 192 MiB of HBM per device.

v0:
```python
import math

import jax
import jax.numpy as jnp
from jax import lax
from jax.sharding import PartitionSpec as P

GROUPS = 4


def from_partner(value, axis, distance):
    mask = 2**distance
    pairs = [(source, source ^ mask) for source in range(lax.axis_size(axis))]
    return lax.ppermute(value, axis, pairs)


def precise(left, right):
    return jnp.dot(left, right, precision=lax.Precision.HIGHEST, preferred_element_type=jnp.float32)


def twiddle(row_count, col_count, length):
    phase_turns = (
        jnp.arange(row_count, dtype=jnp.int32)[:, None]
        * jnp.arange(col_count, dtype=jnp.int32)[None, :]
        % length
    )
    angles = phase_turns.astype(jnp.float32) * (2.0 * math.pi / length)
    return (jnp.cos(angles), jnp.sin(angles))


def pair_major(array):
    column_count = array.shape[-1]
    return jnp.transpose(array.reshape(-1, column_count))


def energy_major(rows, lead_shape):
    return jnp.transpose(rows).reshape(lead_shape + (rows.shape[0],))


def pick_pairs(array, index):
    rows = jnp.take(pair_major(array), index, axis=0)
    return energy_major(rows, array.shape[:-1])


def transform_pairs(pieces):
    energies = pieces.shape[1]
    count_items = pieces.shape[3]
    item_width = pieces.shape[4]
    length = 2 * energies
    span = count_items * item_width
    columns = pieces.reshape(2, energies, 2 * span)
    cosine, sine_part = twiddle(length, energies, length)
    matrix = jnp.concatenate(
        [jnp.concatenate([cosine, sine_part], 1), jnp.concatenate([-sine_part, cosine], 1)], 0
    )
    spectrum = precise(matrix, columns.reshape(2 * energies, 2 * span)).reshape(2, length, 2 * span)
    spectrum_re = spectrum[0]
    spectrum_im = spectrum[1]
    spectrum_re = spectrum_re.reshape(length, 2, span)
    spectrum_im = spectrum_im.reshape(length, 2, span)
    own_re = spectrum_re[:, 0]
    own_im = spectrum_im[:, 0]
    mirror_re = spectrum_re[:, 1]
    mirror_im = spectrum_im[:, 1]
    prod_re = own_re * mirror_re + own_im * mirror_im
    prod_im = own_im * mirror_re - own_re * mirror_im
    back_cos, back_sin = twiddle(energies, length, length)
    factor = 1.0 / (length * math.sqrt(energies))
    matrix_back = (
        jnp.concatenate(
            [jnp.concatenate([back_sin, back_cos], 1), jnp.concatenate([-back_cos, back_sin], 1)], 0
        )
        * factor
    )
    polarized = precise(matrix_back, jnp.concatenate([prod_re, prod_im], 0))
    polarized = polarized.reshape(2, energies, count_items, item_width)
    return lax.all_to_all(polarized, "energy", split_axis=1, concat_axis=3, tiled=True)


def correlate(own_rows, mirror_rows):
    energies_dev = own_rows.shape[1]
    capacity = own_rows.shape[2]
    conj_sign = jnp.array([1.0, -1.0], jnp.float32)[:, None, None]
    stacked = jnp.stack([own_rows, mirror_rows * conj_sign], axis=2)
    stacked = stacked.reshape(2, energies_dev, 2, GROUPS, capacity // GROUPS)
    returned = transform_pairs(
        lax.all_to_all(stacked, "energy", split_axis=4, concat_axis=1, tiled=True)
    )
    return returned.reshape(2, energies_dev, capacity)


def local(g_lesser, g_greater, live_columns, live_count, mirror):
    slab_total = lax.axis_size("slab")
    slot_count = g_lesser.shape[2]
    position = (
        jnp.zeros((slot_count,), jnp.int32)
        .at[live_columns]
        .set(jnp.arange(slot_count, dtype=jnp.int32))
    )
    is_live = position < live_count[0]
    partner = g_greater
    for bit_index in range(slab_total.bit_length() - 1):
        partner = from_partner(partner, "slab", bit_index)
    mirrored = pick_pairs(partner, mirror)
    spread_out = correlate(g_lesser, mirrored)
    return jnp.where(is_live[None, None, :], spread_out, jnp.zeros_like(spread_out))


def solution(mesh):
    return jax.shard_map(
        local,
        mesh=mesh,
        in_specs=(
            P(None, "energy", "slab"),
            P(None, "energy", "slab"),
            P("slab"),
            P("slab"),
            P("slab"),
        ),
        out_specs=P(None, "energy", "slab"),
        check_vma=False,
    )
```

profile of v0, /device:TPU:1, one launch (start us, length us, event | category | flops | bytes accessed | tf_op | source)
XLA Modules:
  0.0 1021.3 jit_solution(10088011886243546471)
XLA Ops:
  0.0 0.0 copy-start.1
  0.0 2.1 collective-permute-start
  2.1 90.2 %collective-permute-done = f32[2,16,32768]{2,1,0:T(8,128)} collective-permute-done((f32[2,16,32768]{2,1,0:T(8,128)}, f32[2,16,32768]{2,1,0:T(8,128)}, u32[]{:S(2)}, u32[]{:S(2)}) %collective-permute-start) | collective-permute-done | bytes 4194336 | tf_op jit(solution)/shard_map/ppermute | solution.py:14
  92.3 3.2 collective-permute-start.1
  95.5 6.2 stack.7
  101.7 0.0 copy-done.1
  101.8 83.2 %collective-permute-done.1 = f32[2,16,32768]{2,1,0:T(8,128)} collective-permute-done((f32[2,16,32768]{2,1,0:T(8,128)}, f32[2,16,32768]{2,1,0:T(8,128)}, u32[]{:S(2)}, u32[]{:S(2)}) %collective-permute-start.1) | collective-permute-done | bytes 4194336 | tf_op jit(solution)/shard_map/ppermute | solution.py:14
  185.0 10.4 %copy.20 = f32[32,32768]{0,1:T(8,128)} copy(f32[32,32768]{1,0:T(8,128)} %bitcast.1) | data formatting | bytes 8388608 | tf_op jit(solution)/shard_map/reshape | solution.py:33
  195.3 114.2 %gather_fusion = f32[32768,32]{1,0:T(8,128)} fusion(f32[32768,32]{1,0:T(8,128)} %bitcast.23, s32[32768]{0:T(1024)S(1)} %fusion.37), kind=kCustom, calls=%fused_computation | custom fusion | bytes 8519680 | tf_op jit(solution)/shard_map/jit(_take)/gather | solution.py:41
  309.5 19.1 %select_bitcast_fusion = f32[32,32768]{0,1:T(8,128)} fusion(f32[32768,32]{1,0:T(8,128)} %gather_fusion, pred[32768]{0:T(1024)(128)(4,1)S(1)} %compare_and_fusion), kind=kLoop, calls=%fused_computation.2 | loop fusion | flops 1048576 | bytes 8421376 | tf_op jit(solution)/shard_map/jit(_take)/select_n | solution.py:41
  328.6 11.6 %copy.21 = f32[32,32768]{1,0:T(8,128)} copy(f32[32,32768]{0,1:T(8,128)} %select_bitcast_fusion) | data formatting | bytes 8388608 | tf_op jit(solution)/shard_map/jit(_take)/select_n | solution.py:41
  340.2 0.0 copy-start.3
  340.2 6.2 reshape.48
  346.4 0.0 copy-done.3
  346.4 0.0 copy-start
  346.4 5.7 broadcast_multiply_fusion
  352.1 0.0 copy-done
  352.1 8.4 pad_maximum_fusion
  360.5 46.7 %copy.22 = f32[2,16,2,4,8192]{1,3,2,0,4:T(4,128)} copy(f32[2,16,2,4,8192]{4,3,1,0,2:T(4,128)} %pad_maximum_fusion) | data formatting | bytes 16777216 | tf_op jit(solution)/shard_map/stack | solution.py:84
  407.2 55.0 %reshape.71 = f32[32,1,65536]{2,1,0:T(1,128)} reshape(f32[8192,2,2,4,16]{4,3,2,1,0:T(4,128)} %bitcast.18) | data formatting | bytes 16777216
  462.2 10.8 %all-to-all-start = ((f32[32,1,65536]{2,1,0:T(1,128)}), f32[32,1,65536]{2,1,0:T(1,128)}, u32[]{:S(2)}, u32[]{:S(2)}) async-start(f32[32,1,65536]{2,1,0:T(1,128)} %reshape.71), calls=%async_computation | async-start | bytes 16777216 | tf_op jit(solution)/shard_map/all_to_all | solution.py:87
  473.0 9.0 fusion.31
  482.0 8.6 fusion.36
  490.5 9.1 fusion.33
  499.7 8.5 fusion.35
  508.2 73.3 %all-to-all-done = f32[32,1,65536]{2,1,0:T(1,128)} async-done(((f32[32,1,65536]{2,1,0:T(1,128)}), f32[32,1,65536]{2,1,0:T(1,128)}, u32[]{:S(2)}, u32[]{:S(2)}) %all-to-all-start) | async-done | bytes 8388640 | tf_op jit(solution)/shard_map/all_to_all | solution.py:87
  581.5 0.6 broadcast.59
  582.1 25.2 %reduce = f32[32,65536]{1,0:T(8,128)} reduce(f32[32,1,65536]{2,1,0:T(1,128)} %all-to-all-done, f32[]{:T(128)} %broadcast.59), dimensions={1}, to_apply=%all_to_all.22.reduce_sub_computation | reduce | bytes 16777220 | tf_op jit(solution)/shard_map/all_to_all | solution.py:87
  607.3 76.4 %reshape.72 = f32[8192,2,2,4,16]{4,3,2,1,0:T(4,128)} reshape(f32[32,65536]{1,0:T(8,128)} %reduce) | data formatting | bytes 16777216
  683.7 52.4 %copy.23 = f32[2,16,2,4,32,256]{5,3,2,1,4,0:T(4,128)} copy(f32[2,16,2,4,32,256]{1,3,2,0,5,4:T(4,128)} %bitcast.4) | data formatting | bytes 16777216 | tf_op jit(solution)/shard_map/all_to_all | solution.py:87
  736.1 10.8 %reshape_reshape.3 = f32[1024,2048]{1,0:T(8,128)} reshape(f32[2,32,16,2,4,256]{5,4,3,2,1,0:T(4,128)} %bitcast.24) | data formatting | bytes 16777216 | tf_op jit(solution)/shard_map/reshape;reshape | solution.py:56
  746.8 62.5 %fusion.7 = f32[2048,2048]{0,1:T(8,128)} fusion(f32[1024,2048]{1,0:T(8,128)} %reshape_reshape.3, f32[1024,512]{1,0:T(8,128)} %get-tuple-element.10, f32[1024,512]{1,0:T(8,128)} %fusion.36, f32[1024,512]{1,0:T(8,128)S(1)} %get-tuple-element.9), kind=kOutput, calls=%fused_computation.11 | convolution fusion | flops 51545899008 | bytes 31457280 | tf_op jit(solution)/shard_map/dot_general | solution.py:18
  809.3 6.7 fusion.43
  816.1 2.4 add_bitcast_fusion
  818.5 33.6 %fusion = f32[1024,1024]{1,0:T(8,128)} fusion(f32[512,1024]{1,0:T(8,128)} %get-tuple-element.12, f32[512,1024]{1,0:T(8,128)} %fusion.35, f32[512,1024]{1,0:T(8,128)} %get-tuple-element.11, f32[1024,1024]{0,1:T(8,128)S(1)} %get-tuple-element.6, f32[1024,1024]{0,1:T(8,128)S(1)} %get-tuple-element.5), kind=kOutput, calls=%fused_computation.4 | convolution fusion | flops 25780289536 | bytes 18874368 | tf_op jit(solution)/shard_map/dot_general | solution.py:18
  852.1 5.6 reshape.49
  857.8 4.9 copy.24
  862.7 0.0 copy-start.2
  862.7 21.2 %all-to-all-start.1 = ((f32[2,512,4,256]{3,2,0,1:T(4,128)}), f32[2,512,4,256]{3,2,0,1:T(4,128)}, u32[]{:S(2)}, u32[]{:S(2)}) async-start(f32[2,512,4,256]{3,2,0,1:T(4,128)} %copy.24), calls=%async_computation.1 | async-start | bytes 8388608 | tf_op jit(solution)/shard_map/all_to_all | solution.py:77
  884.5 0.0 copy-done.2
  884.6 120.1 %scatter_custom_fusion = s32[32768]{0:T(1024)S(1)} fusion(s32[32768]{0:T(1024)S(1)} %compare_select_fusion.1, s32[32768]{0:T(1024)S(1)} %iota.19, s32[]{:T(128)} %constant.40.clone.1), kind=kCustom, calls=%fused_computation.57 | custom fusion | bytes 131076 | tf_op jit(solution)/shard_map/scatter | solution.py:98
  1004.7 0.0 all-to-all-done.1
  1004.7 6.6 copy.25
  1011.3 4.9 reshape.50
  1016.3 4.5 broadcast_select_fusion
  (5 shorter events, 0.1 us)
Async XLA Ops:
  0.0 101.7 %copy-start.1 = (s32[32768]{0:T(1024)S(1)}, s32[32768]{0:T(1024)}, u32[]{:S(2)}) copy-start(s32[32768]{0:T(1024)} %param.10) | copy-start | bytes 393220
  0.0 92.3 %collective-permute-start = (f32[2,16,32768]{2,1,0:T(8,128)}, f32[2,16,32768]{2,1,0:T(8,128)}, u32[]{:S(2)}, u32[]{:S(2)}) collective-permute-start(f32[2,16,32768]{2,1,0:T(8,128)} %param.7), channel_id=1, source_target_pairs={{0,32},{32,0},{64,96},{96,64},{1,33},{33,1},{65,97},{97,65},{2,34}... | collective-permute-start | bytes 12582920 | tf_op jit(solution)/shard_map/ppermute | solution.py:14
  92.3 92.7 %collective-permute-start.1 = (f32[2,16,32768]{2,1,0:T(8,128)}, f32[2,16,32768]{2,1,0:T(8,128)}, u32[]{:S(2)}, u32[]{:S(2)}) collective-permute-start(f32[2,16,32768]{2,1,0:T(8,128)} %collective-permute-done), channel_id=1, source_target_pairs={{0,64},{32,96},{64,0},{96,32},{1,65},{33,97},{65,1},{97,33},{2,66}... | collective-permute-start | bytes 12582920 | tf_op jit(solution)/shard_map/ppermute | solution.py:14
  340.2 6.2 copy-start.3
  346.4 5.7 copy-start
  462.2 119.4 %all-to-all-start = ((f32[32,1,65536]{2,1,0:T(1,128)}), f32[32,1,65536]{2,1,0:T(1,128)}, u32[]{:S(2)}, u32[]{:S(2)}) async-start(f32[32,1,65536]{2,1,0:T(1,128)} %reshape.71), calls=%async_computation | async-start | bytes 16777216 | tf_op jit(solution)/shard_map/all_to_all | solution.py:87
  862.7 21.9 %copy-start.2 = (s32[32768]{0:T(1024)S(1)}, s32[32768]{0:T(1024)}, u32[]{:S(2)}) copy-start(s32[32768]{0:T(1024)} %param.8) | copy-start | bytes 393220
  862.7 142.0 %all-to-all-start.1 = ((f32[2,512,4,256]{3,2,0,1:T(4,128)}), f32[2,512,4,256]{3,2,0,1:T(4,128)}, u32[]{:S(2)}, u32[]{:S(2)}) async-start(f32[2,512,4,256]{3,2,0,1:T(4,128)} %copy.24), calls=%async_computation.1 | async-start | bytes 8388608 | tf_op jit(solution)/shard_map/all_to_all | solution.py:77
where the time goes:
time: 1030 us; the launch traced here: 1020 us
  local copies, waits for them, and re-layouts  539 us (52%)
  waiting for transfers between devices  247 us (24%)
  other arithmetic  101 us (10%)
  matrix products  96.1 us (9%)
  starting transfers between devices  37.3 us (4%)
    ppermute x2, waiting for transfers between devices, from_partner(): return lax.ppermute(value, axis, pairs)  173 us
    unnamed x10, local copies, waits for them, and re-layouts  131 us
    scatter x1, local copies, waits for them, and re-layouts, local(): position = jnp.zeros((slot_count,), jnp.int32).at[live_columns].set(jnp.a...  120 us
    gather x1, local copies, waits for them, and re-layouts, pick_pairs(): rows = jnp.take(pair_major(array), index, axis=0)  114 us
    dot_general x2, matrix products, precise(): jnp.dot(left, right, precision=lax.Precision.HIGHEST, preferred_element_t...  96.1 us
    all_to_all x1, waiting for transfers between devices, correlate(): lax.all_to_all(stacked, 'energy', split_axis=4, concat_axis=1, tiled=True)  73.3 us
    all_to_all x2, local copies, waits for them, and re-layouts, correlate(): lax.all_to_all(stacked, 'energy', split_axis=4, concat_axis=1, tiled=True)  53 us
    another operation x2, local copies, waits for them, and re-layouts, correlate(): stacked = jnp.stack([own_rows, mirror_rows * conj_sign], axis=2)  52.9 us
  transfers between devices with their start and end apart: 4, of which 3 were waited for; matrix products, arithmetic and copies ran while one was open for 16% of the time, Pallas kernels for 0%

commit v1 on v0

v1 whole, which is shorter than its diff:
```python
import functools
import math

import jax
import jax.numpy as jnp
import ml_dtypes
import numpy as np
from jax import lax
from jax.experimental import pallas as pl
from jax.experimental.pallas import tpu as pltpu

F32 = jnp.float32
BF16 = jnp.bfloat16
SLOTS = 32768
LIVE = 16384
ENERGIES = 512
PARTS = 32
WIDTHS = (256, 256)
VMEM_BYTES = 40 << 20
SMEM = pl.BlockSpec(memory_space=pltpu.SMEM)
VMEM = pl.BlockSpec(memory_space=pltpu.VMEM)
UNROLL = 32


def params():
    return pltpu.CompilerParams(vmem_limit_bytes=VMEM_BYTES)


def rows_kernel(a_low, b_low, a_high, b_high, rows):
    for j in range(a_low.shape[-1] // 128):
        s = slice(j * 128, (j + 1) * 128)
        block = [ref[:, :, s].reshape(32, 128) for ref in (a_low, b_low, a_high, b_high)]
        rows[s, :] = jnp.concatenate(block, 0).T


def column_rows(a, b, block=2048):
    steps = LIVE // block
    low = pl.BlockSpec((2, 16, block), lambda i: (0, 0, i))
    high = pl.BlockSpec((2, 16, block), lambda i: (0, 0, i + steps))
    return pl.pallas_call(
        rows_kernel,
        grid=(steps,),
        in_specs=[low, low, high, high],
        out_specs=pl.BlockSpec((block, 128), lambda i: (i, 0)),
        out_shape=jax.ShapeDtypeStruct((LIVE, 128), F32),
        compiler_params=params(),
        name="column_rows",
    )(a, b, a, b)


def gather_kernel(count, order, table, rows, out, packed, *, base, width):
    half = lax.broadcasted_iota(jnp.int32, (1, 128), 1) >> 6

    def step(k, _):
        first = pl.multiple_of(k * UNROLL, UNROLL)
        cols = [table[order[first + u]] for u in range(UNROLL)]
        picked = [rows[pl.ds(c & (LIVE - 1), 1), :] for c in cols]
        for u in range(UNROLL):
            mine = (jnp.full((1, 128), cols[u], jnp.int32) >> 14) == half
            packed[pl.ds(first + u, 1), :] = jnp.where(mine, picked[u], 0.0)
        return 0

    lax.fori_loop(0, PARTS * width // UNROLL, step, 0)
    lane = lax.broadcasted_iota(jnp.int32, (1, 128), 1)

    def turn(j, _):
        for w in range(width // 128):
            first = pl.multiple_of(j * width + w * 128, 128)
            block = packed[pl.ds(first, 128), :].T
            block = block[:64] + block[64:]
            out[j, :, w * 128 : (w + 1) * 128] = jnp.where(lane + first + base < count[0], block, 0.0)
        return 0

    lax.fori_loop(0, PARTS, turn, 0)


def gather(count, order, table, rows, base, width):
    items = PARTS * width
    return pl.pallas_call(
        functools.partial(gather_kernel, base=base, width=width),
        in_specs=[SMEM, SMEM, SMEM, VMEM],
        out_specs=VMEM,
        out_shape=jax.ShapeDtypeStruct((PARTS, 64, width), F32),
        scratch_shapes=[pltpu.VMEM((items, 128), F32)],
        compiler_params=params(),
        cost_estimate=pl.CostEstimate(flops=items * 2000, bytes_accessed=items * 4000, transcendentals=0),
        name="gather",
    )(count, order, table, rows)


def columns_kernel(order, table, out):
    def step(k, _):
        first = pl.multiple_of(k * UNROLL, UNROLL)
        cols = [table[order[first + u]] for u in range(UNROLL)]
        for u in range(UNROLL):
            out[first + u] = cols[u]
        return 0

    lax.fori_loop(0, LIVE // UNROLL, step, 0)


def columns_in_order(order, table):
    return pl.pallas_call(
        columns_kernel,
        in_specs=[SMEM, SMEM],
        out_specs=SMEM,
        out_shape=jax.ShapeDtypeStruct((LIVE,), jnp.int32),
        cost_estimate=pl.CostEstimate(flops=LIVE * 1000, bytes_accessed=LIVE * 2000, transcendentals=0),
        name="columns_in_order",
    )(order, table)


def tables():
    n = np.arange(256)
    angle = 2.0 * np.pi * ((n[:, None] * n[None, :]) % 256) / 256.0
    matrix = np.concatenate([np.cos(angle), np.sin(angle)], 0).astype(np.float32)
    high = matrix.astype(ml_dtypes.bfloat16)
    low = (matrix - high.astype(np.float32)).astype(ml_dtypes.bfloat16)
    matrix = np.concatenate([high, high, low], 1)
    phase = 2.0 * np.pi * np.arange(1, 4)[:, None] * n[None, :] / 1024.0
    turn = np.stack([np.cos(phase), np.sin(phase)], 1).astype(np.float32)
    return matrix, np.repeat(turn[:, :, :, None], 128, 3)


def split(values):
    high = values.astype(BF16)
    low = (values - high.astype(F32)).astype(BF16)
    return jnp.concatenate([high, low, high], 0)


def correlate_kernel(matrix, turn, a_ref, b_ref, out):
    scale = 1.0 / (1024.0 * math.sqrt(ENERGIES))

    def tile(w, _):
        lanes = pl.ds(pl.multiple_of(w * 128, 128), 128)

        def halves(ref, part):
            values = ref[:, part * 16 : part * 16 + 16, lanes].reshape(ENERGIES, 128)
            return values[:256], values[256:]

        ar0, ar1 = halves(a_ref, 0)
        ai0, ai1 = halves(a_ref, 1)
        br0, br1 = halves(b_ref, 0)
        bi0, bi1 = halves(b_ref, 1)
        low_re = low_im = high_re = high_im = None
        for r in range(4):
            if r == 0:
                ur, ui, vr, vi = ar0 + ar1, ai0 + ai1, br0 + br1, bi0 + bi1
            elif r == 1:
                ur, ui, vr, vi = ar0 + ai1, ai0 - ar1, br0 - bi1, bi0 + br1
            elif r == 2:
                ur, ui, vr, vi = ar0 - ar1, ai0 - ai1, br0 - br1, bi0 - bi1
            else:
                ur, ui, vr, vi = ar0 - ai1, ai0 + ar1, br0 + bi1, bi0 - br1
            if r:
                c, s = turn[r - 1, 0], turn[r - 1, 1]
                ur, ui = ur * c + ui * s, ui * c - ur * s
                vr, vi = vr * c - vi * s, vi * c + vr * s
            spec = jnp.dot(
                matrix[...],
                split(jnp.concatenate([ur, ui, vr, vi], 1)),
                preferred_element_type=F32,
            )
            cos, sin = spec[:256], spec[256:]
            a_re = cos[:, :128] + sin[:, 128:256]
            a_im = cos[:, 128:256] - sin[:, :128]
            b_re = cos[:, 256:384] - sin[:, 384:]
            b_im = cos[:, 384:] + sin[:, 256:384]
            p_re = a_re * b_re - a_im * b_im
            p_im = a_re * b_im + a_im * b_re
            back = jnp.dot(
                matrix[...], split(jnp.concatenate([p_re, p_im], 1)), preferred_element_type=F32
            )
            q_re = back[:256, :128] - back[256:, 128:]
            q_im = back[:256, 128:] + back[256:, :128]
            if r:
                q_re, q_im = q_re * c - q_im * s, q_re * s + q_im * c
            if r == 0:
                low_re, low_im, high_re, high_im = q_re, q_im, q_re, q_im
            else:
                low_re, low_im = low_re + q_re, low_im + q_im
                if r == 1:
                    high_re, high_im = high_re - q_im, high_im + q_re
                elif r == 2:
                    high_re, high_im = high_re - q_re, high_im - q_im
                else:
                    high_re, high_im = high_re + q_im, high_im - q_re
        out[:16, :16, lanes] = (low_im * scale).reshape(16, 16, 128)
        out[16:, :16, lanes] = (high_im * scale).reshape(16, 16, 128)
        out[:16, 16:, lanes] = (low_re * -scale).reshape(16, 16, 128)
        out[16:, 16:, lanes] = (high_re * -scale).reshape(16, 16, 128)
        return 0

    lax.fori_loop(0, a_ref.shape[-1] // 128, tile, 0)


def correlate(matrix, turn, a, b):
    width = a.shape[-1]
    return pl.pallas_call(
        correlate_kernel,
        in_specs=[VMEM] * 4,
        out_specs=VMEM,
        out_shape=jax.ShapeDtypeStruct((PARTS, 32, width), F32),
        compiler_params=params(),
        cost_estimate=pl.CostEstimate(
            flops=width * 2 * 4 * 512 * 768 * 6, bytes_accessed=width * 12288, transcendentals=0
        ),
        name="correlate",
    )(matrix, turn, a, b)


def scatter_kernel(*refs, width, first_chunk):
    if first_chunk:
        where, values, out, rows = refs
        out[...] = jnp.zeros_like(out)
    else:
        where, values, before, out, rows = refs
        out[...] = before[...]
    group = lax.broadcasted_iota(jnp.int32, (1, 128), 1) >> 5

    def turn(j, _):
        for w in range(width // 128):
            first = pl.multiple_of(j * width + w * 128, 128)
            block = values[j, :, w * 128 : (w + 1) * 128]
            rows[pl.ds(first, 128), :] = jnp.concatenate([block] * 4, 0).T
        return 0

    lax.fori_loop(0, PARTS, turn, 0)

    def step(k, _):
        first = pl.multiple_of(k * UNROLL, UNROLL)
        places = [where[first + u] for u in range(UNROLL)]
        picked = [rows[pl.ds(first + u, 1), :] for u in range(UNROLL)]
        for u in range(UNROLL):
            mine = (jnp.full((1, 128), places[u], jnp.int32) >> 13) == group
            pltpu.store(out.at[pl.ds(places[u] & 8191, 1), :], picked[u], mask=mine)
        return 0

    lax.fori_loop(0, PARTS * width // UNROLL, step, 0)


def scatter(where, values, before):
    width = values.shape[-1]
    items = PARTS * width
    operands = (where, values) if before is None else (where, values, before)
    return pl.pallas_call(
        functools.partial(scatter_kernel, width=width, first_chunk=before is None),
        in_specs=[SMEM] + [VMEM] * (len(operands) - 1),
        out_specs=VMEM,
        out_shape=jax.ShapeDtypeStruct((SLOTS // 4, 128), F32),
        scratch_shapes=[pltpu.VMEM((items, 128), F32)],
        compiler_params=params(),
        cost_estimate=pl.CostEstimate(flops=items * 1000, bytes_accessed=items * 2500, transcendentals=0),
        name="scatter",
    )(*operands)


def slots_kernel(rows, out):
    for q in range(rows.shape[0] // 128):
        block = rows[q * 128 : (q + 1) * 128, :].T
        for g in range(4):
            s = slice(q * 512 + g * 128, q * 512 + (g + 1) * 128)
            out[:, :, s] = block[g * 32 : (g + 1) * 32].reshape(2, 16, 128)


def to_slots(rows, block=1024):
    return pl.pallas_call(
        slots_kernel,
        grid=(SLOTS // 4 // block,),
        in_specs=[pl.BlockSpec((block, 128), lambda i: (i, 0))],
        out_specs=pl.BlockSpec((2, 16, 4 * block), lambda i: (0, 0, i)),
        out_shape=jax.ShapeDtypeStruct((2, 16, SLOTS), F32),
        compiler_params=params(),
        name="to_slots",
    )(rows)


def local(g_lesser, g_greater, live_columns, live_count, mirror):
    slabs = lax.axis_size("slab")
    across = [(s, slabs - 1 - s) for s in range(slabs)]
    is_upper = lax.axis_index("slab") >= slabs // 2
    own = jnp.concatenate([live_columns[:LIVE], mirror])
    other = lax.ppermute(own, "slab", across)
    order = jnp.where(is_upper, other[:LIVE], live_columns[:LIVE])
    table = jnp.where(is_upper, other[LIVE:], jnp.arange(SLOTS, dtype=jnp.int32))
    matrix, turn = tables()
    matrix, turn = jnp.asarray(matrix), jnp.asarray(turn)

    rows = column_rows(g_lesser, g_greater)
    bases = np.cumsum((0,) + WIDTHS) * PARTS
    polar = []
    for k, width in enumerate(WIDTHS):
        base = int(bases[k])
        picked = gather(live_count, order[base : base + PARTS * width], table, rows, base, width)
        arrived = lax.all_to_all(picked, "energy", 0, 0, tiled=True)
        mirrored = lax.ppermute(arrived[:, 32:], "slab", across)
        result = correlate(matrix, turn, arrived[:, :32], mirrored)
        polar.append(lax.all_to_all(result, "energy", 0, 0, tiled=True))
    cols = columns_in_order(order, table)
    where = (cols >> 9 << 7) | (cols & 127) | ((cols >> 7 & 3) << 13)
    slots = None
    for k, width in enumerate(WIDTHS):
        base = int(bases[k])
        slots = scatter(where[base : base + PARTS * width], polar[k], slots)
    return to_slots(slots)


def solution(mesh):
    spec = jax.P(None, "energy", "slab")
    return jax.shard_map(
        local,
        mesh=mesh,
        in_specs=(spec, spec, jax.P("slab"), jax.P("slab"), jax.P("slab")),
        out_specs=spec,
        check_vma=False,
    )
```

time: 1030 us -> 236 us (0.23)
  local copies, waits for them, and re-layouts: 539 us -> 26.2 us
  waiting for transfers between devices: 247 us -> 36.5 us
  Pallas kernels: 0 us -> 141 us
  other arithmetic: 101 us -> 1.8 us
  matrix products: 96.1 us -> 0 us
    ppermute x2 -> x3, waiting for transfers between devices: 173 us -> 6.81 us  [the longest x2 6.81 us: local(): mirrored = lax.ppermute(arrived[:, 32:], 'slab', across)]
    pallas_call x0 -> x9, Pallas kernels: none -> 141 us  [the longest x2 41.9 us: gather(): pl.pallas_call(functools.partial(gather_kernel, base=base, width=width),...]
    scatter x1 -> x0, local copies, waits for them, and re-layouts: 120 us -> none  [local(): position = jnp.zeros((slot_count,), jnp.int32).at[live_columns].set(jnp.a...]
    gather x1 -> x0, local copies, waits for them, and re-layouts: 114 us -> none  [pick_pairs(): rows = jnp.take(pair_major(array), index, axis=0)]
    unnamed x10 -> x26, local copies, waits for them, and re-layouts: 131 us -> 19.9 us
    dot_general x2 -> x0, matrix products: 96.1 us -> none  [precise(): jnp.dot(left, right, precision=lax.Precision.HIGHEST, preferred_element_t...]
    another operation x3 -> x0, local copies, waits for them, and re-layouts: 63.7 us -> none  [the longest x2 52.9 us: correlate(): stacked = jnp.stack([own_rows, mirror_rows * conj_sign], axis=2)]
    all_to_all x3 -> x0, local copies, waits for them, and re-layouts: 59.6 us -> none  [the longest x2 53 us: correlate(): lax.all_to_all(stacked, 'energy', split_axis=4, concat_axis=1, tiled=True)]
  transfers between devices with their start and end apart: 4 -> 7, of which waited for: 3 -> 3; matrix products, arithmetic and copies ran while one was open for 16% -> 3% of each run, Pallas kernels for 0% -> 43%
where the time goes in v1:
time: 236 us; the launch traced here: 235 us
  Pallas kernels  141 us (60%)
  waiting for transfers between devices  36.5 us (15%)
  starting transfers between devices  29 us (12%)
  local copies, waits for them, and re-layouts  26.2 us (11%)
    pallas_call x2, Pallas kernels, gather(): pl.pallas_call(functools.partial(gather_kernel, base=base, width=width),...  41.9 us
    pallas_call x1, Pallas kernels, columns_in_order(): pl.pallas_call(columns_kernel, in_specs=[SMEM, SMEM], out_specs=SMEM, out...  40.8 us
    all_to_all x2, waiting for transfers between devices, local(): arrived = lax.all_to_all(picked, 'energy', 0, 0, tiled=True)  29.7 us
    pallas_call x2, Pallas kernels, scatter(): pl.pallas_call(functools.partial(scatter_kernel, width=width, first_chunk...  28.5 us
    unnamed x26, local copies, waits for them, and re-layouts  19.9 us
    pallas_call x2, Pallas kernels, correlate(): pl.pallas_call(correlate_kernel, in_specs=[VMEM] * 4, out_specs=VMEM, out...  19.5 us
    all_to_all x2, starting transfers between devices, local(): arrived = lax.all_to_all(picked, 'energy', 0, 0, tiled=True)  14.1 us
    all_to_all x2, starting transfers between devices, local(): polar.append(lax.all_to_all(result, 'energy', 0, 0, tiled=True))  11.2 us
  transfers between devices with their start and end apart: 7, of which 3 were waited for; matrix products, arithmetic and copies ran while one was open for 3% of the time, Pallas kernels for 43%

profile of v1, /device:TPU:1, one launch (start us, length us, event | category | flops | bytes accessed | tf_op | source)
XLA Modules:
  0.0 235.3 jit_solution(5968127191975580746)
XLA Ops:
  0.0 0.8 slice.34
  0.8 0.9 pad_add_fusion
  1.8 3.6 %collective-permute-start = (s32[49152]{0:T(1024)S(1)}, s32[49152]{0:T(1024)S(1)}, u32[]{:S(2)}, u32[]{:S(2)}) collective-permute-start(s32[49152]{0:T(1024)S(1)} %pad_add_fusion), channel_id=1, source_target_pairs={{0,96},{32,64},{64,32},{96,0},{1,97},{33,65},{65,33},{97,1},{2,98}... | collective-permute-start | bytes 589832 | tf_op jit(solution)/shard_map/ppermute | solution.py:283
  6.1 0.0 copy-start.4
  6.1 2.2 copy-done.4
  8.3 0.0 copy-start.5
  8.3 2.2 copy-done.5
  10.4 0.0 copy-start.12
  10.4 6.2 %column_rows.1.rows = f32[16384,128]{1,0:T(8,128)} custom-call(f32[2,16,32768]{2,1,0:T(8,128)S(1)} %copy-done.4, f32[2,16,32768]{2,1,0:T(8,128)S(1)} %copy-done.5, f32[2,16,32768]{2,1,0:T(8,128)S(1)} %copy-done.4, f32[2,16,32768]{2,1,0:T(8,128)S(1)} %copy-done.5), custom_call_target="tpu_custom_call" | custom-call | tf_op jit(solution)/shard_map/column_rows/pallas_call | solution.py:40
  16.6 0.0 collective-permute-done
  16.6 0.0 copy-done.12
  16.6 0.0 copy-start.11
  16.7 0.0 copy-start.6
  16.7 0.0 copy-start
  16.7 3.4 %copy-done = f32[16384,128]{1,0:T(8,128)S(1)} copy-done((f32[16384,128]{1,0:T(8,128)S(1)}, f32[16384,128]{1,0:T(8,128)}, u32[]{:S(2)}) %copy-start) | copy-done | bytes 8388632
  20.1 20.9 %gather.3 = f32[32,64,256]{2,1,0:T(8,128)} custom-call(s32[1]{0:T(128)S(6)} %copy.8.count, s32[8192]{0:T(1024)S(1)} %get-tuple-element.9.order, s32[32768]{0:T(1024)S(1)} %slice_select_fusion.table, f32[16384,128]{1,0:T(8,128)S(1)} %copy-done), custom_call_target="tpu_custom_call" | custom-call | flops 16384000 | bytes 32768000 | tf_op jit(solution)/shard_map/gather/pallas_call | solution.py:79
  41.1 0.0 copy-done.11
  41.1 8.9 %all-to-all-start.2 = ((f32[32,64,256]{2,1,0:T(8,128)}), f32[32,64,256]{2,1,0:T(8,128)}, u32[]{:S(2)}, u32[]{:S(2)}) async-start(f32[32,64,256]{2,1,0:T(8,128)} %gather.3), calls=%async_computation.2 | async-start | bytes 4194304 | tf_op jit(solution)/shard_map/all_to_all | solution.py:295
  50.0 0.0 copy-done.6
  50.0 0.0 copy-start.1
  50.0 3.4 %copy-done.1 = f32[16384,128]{1,0:T(8,128)S(1)} copy-done((f32[16384,128]{1,0:T(8,128)S(1)}, f32[16384,128]{1,0:T(8,128)}, u32[]{:S(2)}) %copy-start.1) | copy-done | bytes 8388632
  53.4 21.0 %gather.2 = f32[32,64,256]{2,1,0:T(8,128)} custom-call(s32[1]{0:T(128)S(6)} %copy.8.count, s32[8192]{0:T(1024)S(1)} %get-tuple-element.10.order, s32[32768]{0:T(1024)S(1)} %slice_select_fusion.table, f32[16384,128]{1,0:T(8,128)S(1)} %copy-done.1), custom_call_target="tpu_custom_call" | custom-call | flops 16384000 | bytes 32768000 | tf_op jit(solution)/shard_map/gather/pallas_call | solution.py:79
  74.4 4.0 %all-to-all-done.2 = f32[32,64,256]{2,1,0:T(8,128)} async-done(((f32[32,64,256]{2,1,0:T(8,128)}), f32[32,64,256]{2,1,0:T(8,128)}, u32[]{:S(2)}, u32[]{:S(2)}) %all-to-all-start.2) | async-done | bytes 2097184 | tf_op jit(solution)/shard_map/all_to_all | solution.py:295
  78.3 5.2 %all-to-all-start = ((f32[32,64,256]{2,1,0:T(8,128)}), f32[32,64,256]{2,1,0:T(8,128)}, u32[]{:S(2)}, u32[]{:S(2)}) async-start(f32[32,64,256]{2,1,0:T(8,128)} %gather.2), calls=%async_computation | async-start | bytes 4194304 | tf_op jit(solution)/shard_map/all_to_all | solution.py:295
  83.6 2.7 %fusion = (f32[32,32,256]{2,1,0:T(8,128)}, f32[32,32,256]{2,1,0:T(8,128)S(1)}) fusion(f32[32,64,256]{2,1,0:T(8,128)} %all-to-all-done.2), kind=kLoop, calls=%fused_computation.4 | loop fusion | bytes 4194304 | tf_op jit(solution)/shard_map/slice | solution.py:296
  86.3 0.0 collective-permute-start.2
  86.3 25.7 %all-to-all-done = f32[32,64,256]{2,1,0:T(8,128)} async-done(((f32[32,64,256]{2,1,0:T(8,128)}), f32[32,64,256]{2,1,0:T(8,128)}, u32[]{:S(2)}, u32[]{:S(2)}) %all-to-all-start) | async-done | bytes 2097184 | tf_op jit(solution)/shard_map/all_to_all | solution.py:295
  112.0 2.7 %fusion.1 = (f32[32,32,256]{2,1,0:T(8,128)}, f32[32,32,256]{2,1,0:T(8,128)S(1)}) fusion(f32[32,64,256]{2,1,0:T(8,128)} %all-to-all-done), kind=kLoop, calls=%fused_computation.5 | loop fusion | bytes 4194304 | tf_op jit(solution)/shard_map/slice | solution.py:296
  114.7 0.0 collective-permute-start.1
  114.7 0.0 collective-permute-done.2.b_ref
  114.7 0.0 copy-start.7
  114.7 1.1 copy-done.7
  115.8 0.0 copy-start.9
  115.8 1.1 copy-done.9
  117.0 10.3 %correlate.3 = f32[32,32,256]{2,1,0:T(8,128)} custom-call(bf16[512,768]{1,0:T(8,128)(2,1)S(1)} %copy-done.9, f32[3,2,256,128]{3,2,1,0:T(8,128)S(1)} %copy-done.7, f32[32,32,256]{2,1,0:T(8,128)S(1)} %get-tuple-element.6.a_ref, f32[32,32,256]{2,1,0:T(8,128)} %collective-permute-done.2.b_ref), custom_call_target="tpu_custom_call" | custom-call | flops 4831838208 | bytes 3145728 | tf_op jit(solution)/shard_map/correlate/pallas_call | solution.py:199
  127.3 5.8 %all-to-all-start.3 = ((f32[32,32,256]{2,1,0:T(8,128)}), f32[32,32,256]{2,1,0:T(8,128)S(1)}, u32[]{:S(2)}, u32[]{:S(2)}) async-start(f32[32,32,256]{2,1,0:T(8,128)} %correlate.3), calls=%async_computation.3 | async-start | bytes 2097152 | tf_op jit(solution)/shard_map/all_to_all | solution.py:298
  133.1 6.8 %collective-permute-done.1.b_ref = f32[32,32,256]{2,1,0:T(8,128)S(1)} collective-permute-done((f32[32,32,256]{2,1,0:T(8,128)}, f32[32,32,256]{2,1,0:T(8,128)S(1)}, u32[]{:S(2)}, u32[]{:S(2)}) %collective-permute-start.1) | collective-permute-done | bytes 1048608 | tf_op jit(solution)/shard_map/ppermute | solution.py:296
  139.9 0.0 copy-start.8
  139.9 1.1 copy-done.8
  141.1 0.0 copy-start.10
  141.1 1.1 copy-done.10
  142.2 9.1 %correlate.2 = f32[32,32,256]{2,1,0:T(8,128)} custom-call(bf16[512,768]{1,0:T(8,128)(2,1)S(1)} %copy-done.10, f32[3,2,256,128]{3,2,1,0:T(8,128)S(1)} %copy-done.8, f32[32,32,256]{2,1,0:T(8,128)S(1)} %get-tuple-element.8.a_ref, f32[32,32,256]{2,1,0:T(8,128)S(1)} %collective-permute-done.1.b_ref), custom_call_target="tpu_custom_call" | custom-call | flops 4831838208 | bytes 3145728 | tf_op jit(solution)/shard_map/correlate/pallas_call | solution.py:199
  151.3 0.0 all-to-all-done.3.refs_1_
  151.4 5.3 %all-to-all-start.1 = ((f32[32,32,256]{2,1,0:T(8,128)}), f32[32,32,256]{2,1,0:T(8,128)S(1)}, u32[]{:S(2)}, u32[]{:S(2)}) async-start(f32[32,32,256]{2,1,0:T(8,128)} %correlate.2), calls=%async_computation.1 | async-start | bytes 2097152 | tf_op jit(solution)/shard_map/all_to_all | solution.py:298
  156.7 40.8 %columns_in_order.1 = s32[16384]{0:T(1024)} custom-call(s32[16384]{0:T(1024)} %copy-done.11, s32[32768]{0:T(1024)} %copy-done.6), custom_call_target="tpu_custom_call" | custom-call | flops 16384000 | bytes 32768000 | tf_op jit(solution)/shard_map/columns_in_order/pallas_call | solution.py:103
  197.5 0.9 shift-left_or_fusion
  198.4 14.2 %scatter.2.refs_2_ = f32[8192,128]{1,0:T(8,128)S(1)} custom-call(s32[8192]{0:T(1024)S(1)} %get-tuple-element.11.refs_0_, f32[32,32,256]{2,1,0:T(8,128)S(1)} %all-to-all-done.3.refs_1_), custom_call_target="tpu_custom_call" | custom-call | flops 8192000 | bytes 20480000 | tf_op jit(solution)/shard_map/scatter/pallas_call | solution.py:246
  212.6 0.0 copy-start.2
  212.6 2.0 copy-done.2
  214.6 0.0 all-to-all-done.1.refs_1_
  214.6 0.0 copy-start.3
  214.6 2.2 copy-done.3
  216.8 14.2 %scatter.3.rows = f32[8192,128]{1,0:T(8,128)S(1)} custom-call(s32[8192]{0:T(1024)S(1)} %get-tuple-element.12.refs_0_, f32[32,32,256]{2,1,0:T(8,128)S(1)} %all-to-all-done.1.refs_1_, f32[8192,128]{1,0:T(8,128)S(1)} %copy-done.3), custom_call_target="tpu_custom_call" | custom-call | flops 8192000 | bytes 20480000 | tf_op jit(solution)/shard_map/scatter/pallas_call | solution.py:246
  231.1 4.2 %to_slots.1 = f32[2,16,32768]{2,1,0:T(8,128)} custom-call(f32[8192,128]{1,0:T(8,128)S(1)} %scatter.3.rows), custom_call_target="tpu_custom_call" | custom-call | tf_op jit(solution)/shard_map/to_slots/pallas_call | solution.py:267
  (4 shorter events, 0.0 us)
Async XLA Ops:
  1.8 14.8 %collective-permute-start = (s32[49152]{0:T(1024)S(1)}, s32[49152]{0:T(1024)S(1)}, u32[]{:S(2)}, u32[]{:S(2)}) collective-permute-start(s32[49152]{0:T(1024)S(1)} %pad_add_fusion), channel_id=1, source_target_pairs={{0,96},{32,64},{64,32},{96,0},{1,97},{33,65},{65,33},{97,1},{2,98}... | collective-permute-start | bytes 589832 | tf_op jit(solution)/shard_map/ppermute | solution.py:283
  6.1 2.2 copy-start.4
  8.3 2.2 copy-start.5
  10.4 6.2 %copy-start.12 = (s32[32768]{0:T(1024)S(1)}, s32[32768]{0:T(1024)}, u32[]{:S(2)}) copy-start(s32[32768]{0:T(1024)} %param.9) | copy-start | bytes 393220
  16.6 24.4 %copy-start.11 = (s32[16384]{0:T(1024)}, s32[16384]{0:T(1024)S(1)}, u32[]{:S(2)}) copy-start(s32[16384]{0:T(1024)S(1)} %slice_select_fusion.1.order) | copy-start | bytes 196612
  16.7 33.3 %copy-start.6 = (s32[32768]{0:T(1024)}, s32[32768]{0:T(1024)S(1)}, u32[]{:S(2)}) copy-start(s32[32768]{0:T(1024)S(1)} %slice_select_fusion.table) | copy-start | bytes 393220
  16.7 3.4 %copy-start = (f32[16384,128]{1,0:T(8,128)S(1)}, f32[16384,128]{1,0:T(8,128)}, u32[]{:S(2)}) copy-start(f32[16384,128]{1,0:T(8,128)} %column_rows.1.rows) | copy-start | bytes 25165828
  41.1 37.3 %all-to-all-start.2 = ((f32[32,64,256]{2,1,0:T(8,128)}), f32[32,64,256]{2,1,0:T(8,128)}, u32[]{:S(2)}, u32[]{:S(2)}) async-start(f32[32,64,256]{2,1,0:T(8,128)} %gather.3), calls=%async_computation.2 | async-start | bytes 4194304 | tf_op jit(solution)/shard_map/all_to_all | solution.py:295
  50.0 3.4 %copy-start.1 = (f32[16384,128]{1,0:T(8,128)S(1)}, f32[16384,128]{1,0:T(8,128)}, u32[]{:S(2)}) copy-start(f32[16384,128]{1,0:T(8,128)} %column_rows.1.rows) | copy-start | bytes 25165828
  78.3 33.6 %all-to-all-start = ((f32[32,64,256]{2,1,0:T(8,128)}), f32[32,64,256]{2,1,0:T(8,128)}, u32[]{:S(2)}, u32[]{:S(2)}) async-start(f32[32,64,256]{2,1,0:T(8,128)} %gather.2), calls=%async_computation | async-start | bytes 4194304 | tf_op jit(solution)/shard_map/all_to_all | solution.py:295
  86.3 28.4 %collective-permute-start.2 = (f32[32,32,256]{2,1,0:T(8,128)}, f32[32,32,256]{2,1,0:T(8,128)}, u32[]{:S(2)}, u32[]{:S(2)}) collective-permute-start(f32[32,32,256]{2,1,0:T(8,128)} %get-tuple-element.5), channel_id=1, source_target_pairs={{0,96},{32,64},{64,32},{96,0},{1,97},{33,65},{65,33},{97,1},{2,98}... | collective-permute-start | bytes 3145736 | tf_op jit(solution)/shard_map/ppermute | solution.py:296
  114.7 25.2 %collective-permute-start.1 = (f32[32,32,256]{2,1,0:T(8,128)}, f32[32,32,256]{2,1,0:T(8,128)S(1)}, u32[]{:S(2)}, u32[]{:S(2)}) collective-permute-start(f32[32,32,256]{2,1,0:T(8,128)} %get-tuple-element.7), channel_id=1, source_target_pairs={{0,96},{32,64},{64,32},{96,0},{1,97},{33,65},{65,33},{97,1},{2,98}... | collective-permute-start | bytes 3145736 | tf_op jit(solution)/shard_map/ppermute | solution.py:296
  114.7 1.1 copy-start.7
  115.8 1.1 copy-start.9
  127.3 24.1 %all-to-all-start.3 = ((f32[32,32,256]{2,1,0:T(8,128)}), f32[32,32,256]{2,1,0:T(8,128)S(1)}, u32[]{:S(2)}, u32[]{:S(2)}) async-start(f32[32,32,256]{2,1,0:T(8,128)} %correlate.3), calls=%async_computation.3 | async-start | bytes 2097152 | tf_op jit(solution)/shard_map/all_to_all | solution.py:298
  139.9 1.1 copy-start.8
  141.1 1.1 copy-start.10
  151.4 63.3 %all-to-all-start.1 = ((f32[32,32,256]{2,1,0:T(8,128)}), f32[32,32,256]{2,1,0:T(8,128)S(1)}, u32[]{:S(2)}, u32[]{:S(2)}) async-start(f32[32,32,256]{2,1,0:T(8,128)} %correlate.2), calls=%async_computation.1 | async-start | bytes 2097152 | tf_op jit(solution)/shard_map/all_to_all | solution.py:298
  212.6 2.0 copy-start.2
  214.6 2.2 copy-start.3

commit v2 on v1

v2 whole, which is shorter than its diff:
```python
import functools
import math

import jax
import jax.numpy as jnp
import ml_dtypes
import numpy as np
from jax import lax
from jax.experimental import pallas as pl
from jax.experimental.pallas import tpu as pltpu

F32 = jnp.float32
BF16 = jnp.bfloat16
SLOTS = 32768
LIVE = 16384
ENERGIES = 512
PARTS = 32
WIDTHS = (256, 256)
VMEM_BYTES = 60 << 20
SMEM = pl.BlockSpec(memory_space=pltpu.SMEM)
VMEM = pl.BlockSpec(memory_space=pltpu.VMEM)
ANY = pl.BlockSpec(memory_space=pl.ANY)
UNROLL = 32


def params(limit=VMEM_BYTES):
    return pltpu.CompilerParams(vmem_limit_bytes=limit)


def cost(flops, bytes_accessed):
    return pl.CostEstimate(flops=flops, bytes_accessed=bytes_accessed, transcendentals=0)


def rows_kernel(a_low, b_low, a_high, b_high, rows):
    first_half = lax.broadcasted_iota(jnp.int32, (128, 128), 1) < 64
    for j in range(a_low.shape[-1] // 128):
        s = slice(j * 128, (j + 1) * 128)
        block = [ref[:, :, s].reshape(32, 128) for ref in (a_low, b_low, a_high, b_high)]
        block = jnp.concatenate(block, 0).T
        rows[0, s, :] = jnp.where(first_half, block, 0.0)
        rows[1, s, :] = jnp.where(first_half, 0.0, block)


def column_rows(a, b, block=1024):
    steps = LIVE // block
    low = pl.BlockSpec((2, 16, block), lambda i: (0, 0, i))
    high = pl.BlockSpec((2, 16, block), lambda i: (0, 0, i + steps))
    rows = pl.pallas_call(
        rows_kernel,
        grid=(steps,),
        in_specs=[low, low, high, high],
        out_specs=pl.BlockSpec((2, block, 128), lambda i: (0, i, 0)),
        out_shape=jax.ShapeDtypeStruct((2, LIVE, 128), F32),
        compiler_params=params(),
        cost_estimate=cost(1 << 20, 24 << 20),
        name="column_rows",
    )(a, b, a, b)
    return rows.reshape(SLOTS, 128)


def gather_kernel(count, order, table, rows, out, *rest, base, width):
    places, even, odd = rest if len(rest) == 3 else (None, *rest)
    per = width // 128
    lane = lax.broadcasted_iota(jnp.int32, (1, 128), 1)

    def fill(block, packed):
        for k in range(0, 128, UNROLL):
            first = pl.multiple_of(block * 128 + k, UNROLL)
            cols = [table[order[first + u]] for u in range(UNROLL)]
            if places is not None:
                for u in range(UNROLL):
                    places[first + u] = cols[u]
            for u in range(UNROLL):
                packed[k + u : k + u + 1, :] = rows[pl.ds(cols[u], 1), :]

    def turn(j, w, packed):
        block = packed[...].T
        live = lane + (j * width + w * 128 + base) < count[0]
        out[j, :, w * 128 : (w + 1) * 128] = jnp.where(live, block[:64] + block[64:], 0.0)

    fill(0, even)
    bufs = (even, odd)

    def step(k, _):
        for h in range(2):
            for w in range(per):
                now = h * per + w
                turn(2 * k + h, w, bufs[now % 2])
                fill(jnp.minimum(2 * k * per + now + 1, PARTS * per - 1), bufs[(now + 1) % 2])
        return 0

    lax.fori_loop(0, PARTS // 2, step, 0)


def gather(count, order, table, rows, base, width, with_places):
    items = PARTS * width
    out_shape = [jax.ShapeDtypeStruct((PARTS, 64, width), F32)]
    out_specs = [VMEM]
    if with_places:
        out_shape.append(jax.ShapeDtypeStruct((items,), jnp.int32))
        out_specs.append(SMEM)
    return pl.pallas_call(
        functools.partial(gather_kernel, base=base, width=width),
        in_specs=[SMEM, SMEM, SMEM, VMEM],
        out_specs=out_specs,
        out_shape=out_shape,
        scratch_shapes=[pltpu.VMEM((128, 128), F32)] * 2,
        compiler_params=params(),
        cost_estimate=cost(items * 2000, items * 5000),
        name="gather",
    )(count, order, table, rows)


def columns_kernel(order, table, _, out):
    def step(k, _):
        for v in range(0, UNROLL, 8):
            first = pl.multiple_of(k * UNROLL + v, 8)
            cols = [table[order[first + u]] for u in range(8)]
            for u in range(8):
                out[first + u] = cols[u]
        return 0

    lax.fori_loop(0, out.shape[0] // UNROLL, step, 0)


def columns_in_order(order, table, after):
    items = order.shape[0]
    return pl.pallas_call(
        columns_kernel,
        in_specs=[SMEM, SMEM, ANY],
        out_specs=SMEM,
        out_shape=jax.ShapeDtypeStruct((items,), jnp.int32),
        compiler_params=params(2 << 20),
        cost_estimate=cost(items * 2000, items * 5000),
        name="columns_in_order",
    )(order, table, after)


def tables():
    n = np.arange(256)
    angle = 2.0 * np.pi * ((n[:, None] * n[None, :]) % 256) / 256.0
    matrix = np.concatenate([np.cos(angle), np.sin(angle)], 0).astype(np.float32)
    high = matrix.astype(ml_dtypes.bfloat16)
    low = (matrix - high.astype(np.float32)).astype(ml_dtypes.bfloat16)
    matrix = np.concatenate([high, high, low], 1)
    phase = 2.0 * np.pi * np.arange(1, 4)[:, None] * n[None, :] / 1024.0
    turn = np.stack([np.cos(phase), np.sin(phase)], 1).astype(np.float32)
    return matrix, np.repeat(turn[:, :, :, None], 128, 3)


def split(values):
    high = values.astype(BF16)
    low = (values - high.astype(F32)).astype(BF16)
    return jnp.concatenate([high, low, high], 0)


def correlate_kernel(matrix, turn, a_ref, b_ref, *rest):
    out = rest[-1]
    scale = 1.0 / (1024.0 * math.sqrt(ENERGIES))

    def tile(w, _):
        lanes = pl.ds(pl.multiple_of(w * 128, 128), 128)

        def halves(ref, part):
            values = ref[:, part * 16 : part * 16 + 16, lanes].reshape(ENERGIES, 128)
            return values[:256], values[256:]

        ar0, ar1 = halves(a_ref, 0)
        ai0, ai1 = halves(a_ref, 1)
        br0, br1 = halves(b_ref, 0)
        bi0, bi1 = halves(b_ref, 1)
        low_re = low_im = high_re = high_im = None
        for r in range(4):
            if r == 0:
                ur, ui, vr, vi = ar0 + ar1, ai0 + ai1, br0 + br1, bi0 + bi1
            elif r == 1:
                ur, ui, vr, vi = ar0 + ai1, ai0 - ar1, br0 - bi1, bi0 + br1
            elif r == 2:
                ur, ui, vr, vi = ar0 - ar1, ai0 - ai1, br0 - br1, bi0 - bi1
            else:
                ur, ui, vr, vi = ar0 - ai1, ai0 + ar1, br0 + bi1, bi0 - br1
            if r:
                c, s = turn[r - 1, 0], turn[r - 1, 1]
                ur, ui = ur * c + ui * s, ui * c - ur * s
                vr, vi = vr * c - vi * s, vi * c + vr * s
            spec = jnp.dot(
                matrix[...],
                split(jnp.concatenate([ur, ui, vr, vi], 1)),
                preferred_element_type=F32,
            )
            cos, sin = spec[:256], spec[256:]
            a_re = cos[:, :128] + sin[:, 128:256]
            a_im = cos[:, 128:256] - sin[:, :128]
            b_re = cos[:, 256:384] - sin[:, 384:]
            b_im = cos[:, 384:] + sin[:, 256:384]
            p_re = a_re * b_re - a_im * b_im
            p_im = a_re * b_im + a_im * b_re
            back = jnp.dot(
                matrix[...], split(jnp.concatenate([p_re, p_im], 1)), preferred_element_type=F32
            )
            q_re = back[:256, :128] - back[256:, 128:]
            q_im = back[:256, 128:] + back[256:, :128]
            if r:
                q_re, q_im = q_re * c - q_im * s, q_re * s + q_im * c
            if r == 0:
                low_re, low_im, high_re, high_im = q_re, q_im, q_re, q_im
            else:
                low_re, low_im = low_re + q_re, low_im + q_im
                if r == 1:
                    high_re, high_im = high_re - q_im, high_im + q_re
                elif r == 2:
                    high_re, high_im = high_re - q_re, high_im - q_im
                else:
                    high_re, high_im = high_re + q_im, high_im - q_re
        out[:16, :16, lanes] = (low_im * scale).reshape(16, 16, 128)
        out[16:, :16, lanes] = (high_im * scale).reshape(16, 16, 128)
        out[:16, 16:, lanes] = (low_re * -scale).reshape(16, 16, 128)
        out[16:, 16:, lanes] = (high_re * -scale).reshape(16, 16, 128)
        return 0

    lax.fori_loop(0, a_ref.shape[-1] // 128, tile, 0)


def correlate(matrix, turn, a, b, *after):
    width = a.shape[-1]
    return pl.pallas_call(
        correlate_kernel,
        in_specs=[VMEM] * 4 + [ANY] * len(after),
        out_specs=VMEM,
        out_shape=jax.ShapeDtypeStruct((PARTS, 32, width), F32),
        compiler_params=params(24 << 20),
        cost_estimate=cost(width * 2 * 4 * 512 * 768 * 6, width * 12288),
        name="correlate",
    )(matrix, turn, a, b, *after)


def greater_kernel(both, _, out, sem):
    copy = pltpu.make_async_copy(both.at[:, 32:, :], out, sem)
    copy.start()
    copy.wait()


def greater_part(both, after):
    shape = (PARTS, 32, both.shape[-1])
    return pl.pallas_call(
        greater_kernel,
        in_specs=[ANY, ANY],
        out_specs=ANY,
        out_shape=jax.ShapeDtypeStruct(shape, F32),
        scratch_shapes=[pltpu.SemaphoreType.DMA],
        compiler_params=params(1 << 20),
        cost_estimate=cost(1 << 20, 4 << 20),
        name="greater_part",
    )(both, after)


def scatter_rows(row_of, column, values, out, even, odd, width):
    per = width // 128

    def turn(block, packed):
        j, w = block // per, block % per
        lanes = pl.ds(pl.multiple_of(w * 128, 128), 128)
        group = (column[pl.ds(block, 1), :] >> 7) & 3
        data = values[j, :, lanes]
        packed[...] = jnp.concatenate([jnp.where(group == g, data, 0.0) for g in range(4)], 0).T

    def spread(block, packed):
        for k in range(0, 128, UNROLL):
            first = pl.multiple_of(block * 128 + k, UNROLL)
            rows = [row_of[first + u] for u in range(UNROLL)]
            for u in range(UNROLL):
                row = packed[k + u : k + u + 1, :]
                pltpu.store(out.at[pl.ds(rows[u], 1), :], row, mask=row != 0.0)

    turn(0, even)

    def step(k, _):
        turn(2 * k + 1, odd)
        spread(2 * k, even)
        turn(jnp.minimum(2 * k + 2, PARTS * per - 1), even)
        spread(2 * k + 1, odd)
        return 0

    lax.fori_loop(0, PARTS * per // 2, step, 0)


def scatter_first_kernel(row_of, column, values, out, even, odd, slots, sem):
    slots[...] = jnp.zeros_like(slots)
    scatter_rows(row_of, column, values, slots, even, odd, values.shape[-1])
    save = pltpu.make_async_copy(slots, out.at[0], sem)
    save.start()
    save.wait()


def scatter_last_kernel(row_of, column, values, before, out, even, odd, slots, staged, in_sem, out_sem):
    load = pltpu.make_async_copy(before.at[0], slots, in_sem)
    load.start()
    load.wait()
    scatter_rows(row_of, column, values, slots, even, odd, values.shape[-1])
    pieces = out_sem.shape[0]
    span = SLOTS // pieces
    copies = []
    for p in range(pieces):
        for q in range(p * span // 512, (p + 1) * span // 512):
            block = slots[q * 128 : (q + 1) * 128, :].T
            for g in range(4):
                s = slice(q * 512 + g * 128, q * 512 + (g + 1) * 128)
                staged[:, :, s] = block[g * 32 : (g + 1) * 32].reshape(2, 16, 128)
        piece = slice(p * span, (p + 1) * span)
        copies.append(pltpu.make_async_copy(staged.at[:, :, piece], out.at[:, :, piece], out_sem.at[p]))
        copies[-1].start()
    for copy in copies:
        copy.wait()


def scatter(columns, values, before):
    width = values.shape[-1]
    items = PARTS * width
    row_of = (columns >> 9 << 7) | (columns & 127)
    column = columns.reshape(items // 128, 128)
    first = before is None
    scratch = [
        pltpu.VMEM((128, 128), F32),
        pltpu.VMEM((128, 128), F32),
        pltpu.VMEM((SLOTS // 4, 128), F32),
    ]
    if first:
        scratch += [pltpu.SemaphoreType.DMA]
    else:
        scratch += [
            pltpu.VMEM((2, 16, SLOTS), F32),
            pltpu.SemaphoreType.DMA,
            pltpu.SemaphoreType.DMA((8,)),
        ]
    return pl.pallas_call(
        scatter_first_kernel if first else scatter_last_kernel,
        in_specs=[SMEM, VMEM, VMEM] + ([] if first else [ANY]),
        out_specs=ANY,
        out_shape=jax.ShapeDtypeStruct((6, SLOTS // 4, 128) if first else (2, 16, SLOTS), F32),
        scratch_shapes=scratch,
        compiler_params=params(44 << 20),
        cost_estimate=cost(items * 1000, items * 4000),
        name="scatter",
    )(row_of, column, values, *(() if first else (before,)))


def local(g_lesser, g_greater, live_columns, live_count, mirror):
    slabs = lax.axis_size("slab")
    across = [(s, slabs - 1 - s) for s in range(slabs)]
    is_upper = lax.axis_index("slab") >= slabs // 2
    other_mirror = lax.ppermute(mirror, "slab", across)
    other_live = lax.ppermute(live_columns[:LIVE], "slab", across)
    order = jnp.where(is_upper, other_live, live_columns[:LIVE])
    table = jnp.where(is_upper, other_mirror, jnp.arange(SLOTS, dtype=jnp.int32))
    matrix, turn = tables()
    matrix, turn = jnp.asarray(matrix), jnp.asarray(turn)

    rows = column_rows(g_lesser, g_greater)
    half = WIDTHS[0]
    orders = [order[: PARTS * half], order[PARTS * half :]]
    (picked0,) = gather(live_count, orders[0], table, rows, 0, half, False)
    picked1, columns1 = gather(live_count, orders[1], table, rows, PARTS * half, WIDTHS[1], True)
    columns0 = columns_in_order(orders[0], table, picked1)

    def swap(values):
        return lax.all_to_all(values, "energy", 0, 0, tiled=True)

    def mirrored(values, after):
        return lax.ppermute(greater_part(values, after), "slab", across)

    arrived0 = swap(picked0)
    arrived1 = swap(picked1)
    result0 = correlate(matrix, turn, arrived0, mirrored(arrived0, picked1), columns0)
    result1 = correlate(matrix, turn, arrived1, mirrored(arrived1, result0))
    polar0 = swap(result0)
    polar1 = swap(result1)
    slots = scatter(columns0, polar0, None)
    return scatter(columns1, polar1, slots)


def solution(mesh):
    spec = jax.P(None, "energy", "slab")
    return jax.shard_map(
        local,
        mesh=mesh,
        in_specs=(spec, spec, jax.P("slab"), jax.P("slab"), jax.P("slab")),
        out_specs=spec,
        check_vma=False,
    )
```

time: 236 us -> 203 us (0.86)
  local copies, waits for them, and re-layouts: 26.2 us -> 3.78 us
  Pallas kernels: 141 us -> 128 us
  starting transfers between devices: 29 us -> 41.2 us
  waiting for transfers between devices: 36.5 us -> 26.9 us
    all_to_all x4, waiting for transfers between devices: 29.7 us -> 7.68 us  [swap(): return lax.all_to_all(values, 'energy', 0, 0, tiled=True)]
    pallas_call x6 -> x7, Pallas kernels: 92.9 us -> 71.5 us  [the longest x2 30.1 us: scatter(): pl.pallas_call(scatter_first_kernel if first else scatter_last_kernel, in...]
    unnamed x26 -> x18, local copies, waits for them, and re-layouts: 19.9 us -> 2.3 us
    ppermute x3 -> x4, waiting for transfers between devices: 6.81 us -> 19.2 us  [the longest x2 19.2 us: mirrored(): return lax.ppermute(greater_part(values, after), 'slab', across)]
    pallas_call x1, Pallas kernels: 6.16 us -> 14.8 us  [column_rows(): pl.pallas_call(rows_kernel, grid=(steps,), in_specs=[low, low, high, high...]
    all_to_all x4, starting transfers between devices: 25.3 us -> 32.2 us  [swap(): return lax.all_to_all(values, 'energy', 0, 0, tiled=True)]
    ppermute x3 -> x4, starting transfers between devices: 3.65 us -> 9.08 us  [the longest x2 5.48 us: mirrored(): return lax.ppermute(greater_part(values, after), 'slab', across)]
    slice x5 -> x2, local copies, waits for them, and re-layouts: 6.32 us -> 1.48 us  [the longest x1 0.84 us: local(): other_live = lax.ppermute(live_columns[:LIVE], 'slab', across)]
  transfers between devices with their start and end apart: 7 -> 8, of which waited for: 3 -> 4; matrix products, arithmetic and copies ran while one was open for 3% -> 0% of each run, Pallas kernels for 43% -> 46%
where the time goes in v2:
time: 203 us; the launch traced here: 201 us
  Pallas kernels  128 us (63%)
  starting transfers between devices  41.2 us (20%)
  waiting for transfers between devices  26.9 us (13%)
  local copies, waits for them, and re-layouts  3.78 us (2%)
    pallas_call x2, Pallas kernels, gather(): pl.pallas_call(functools.partial(gather_kernel, base=base, width=width),...  41.6 us
    all_to_all x4, starting transfers between devices, swap(): return lax.all_to_all(values, 'energy', 0, 0, tiled=True)  32.2 us
    pallas_call x2, Pallas kernels, scatter(): pl.pallas_call(scatter_first_kernel if first else scatter_last_kernel, in...  30.1 us
    pallas_call x2, Pallas kernels, correlate(): pl.pallas_call(correlate_kernel, in_specs=[VMEM] * 4 + [ANY] * len(after)...  21.4 us
    ppermute x2, waiting for transfers between devices, mirrored(): return lax.ppermute(greater_part(values, after), 'slab', across)  19.2 us
    pallas_call x1, Pallas kernels, columns_in_order(): pl.pallas_call(columns_kernel, in_specs=[SMEM, SMEM, ANY], out_specs=SMEM...  17.4 us
    pallas_call x1, Pallas kernels, column_rows(): pl.pallas_call(rows_kernel, grid=(steps,), in_specs=[low, low, high, high...  14.8 us
    all_to_all x4, waiting for transfers between devices, swap(): return lax.all_to_all(values, 'energy', 0, 0, tiled=True)  7.68 us
  transfers between devices with their start and end apart: 8, of which 4 were waited for; matrix products, arithmetic and copies ran while one was open for 0% of the time, Pallas kernels for 46%

profile of v2, /device:TPU:1, one launch (start us, length us, event | category | flops | bytes accessed | tf_op | source)
XLA Modules:
  0.0 201.4 jit_solution(7519581629128175982)
XLA Ops:
  0.0 0.8 slice.10
  0.8 3.6 %collective-permute-start = (s32[16384]{0:T(1024)S(1)}, s32[16384]{0:T(1024)S(1)}, u32[]{:S(2)}, u32[]{:S(2)}) collective-permute-start(s32[16384]{0:T(1024)S(1)} %slice.10), channel_id=1, source_target_pairs={{0,96},{32,64},{64,32},{96,0},{1,97},{33,65},{65,33},{97,1},{2,98}... | collective-permute-start | bytes 196616 | tf_op jit(solution)/shard_map/ppermute | solution.py:352
  4.4 0.0 collective-permute-start.1
  5.1 0.0 copy-start.8
  5.1 14.8 %column_rows.1 = f32[2,16384,128]{2,1,0:T(8,128)} custom-call(f32[2,16,32768]{2,1,0:T(8,128)} %a_high.1, f32[2,16,32768]{2,1,0:T(8,128)} %b_high.1, f32[2,16,32768]{2,1,0:T(8,128)} %a_high.1, f32[2,16,32768]{2,1,0:T(8,128)} %b_high.1), custom_call_target="tpu_custom_call" | custom-call | flops 1048576 | bytes 25165824 | tf_op jit(solution)/shard_map/column_rows/pallas_call | solution.py:48
  19.9 0.0 collective-permute-done
  19.9 0.0 copy-done.8
  20.0 0.6 fusion
  20.6 0.0 collective-permute-done.1
  20.6 0.7 iota_select_fusion.table
  21.3 18.0 %gather.3 = f32[32,64,256]{2,1,0:T(8,128)} custom-call(s32[1]{0:T(128)S(6)} %copy.8.count, s32[8192]{0:T(1024)} %get-tuple-element.9.order, s32[32768]{0:T(1024)} %iota_select_fusion.table, f32[32768,128]{1,0:T(8,128)} %bitcast.5), custom_call_target="tpu_custom_call" | custom-call | flops 16384000 | bytes 40960000 | tf_op jit(solution)/shard_map/gather/pallas_call | solution.py:102
  39.3 9.1 %all-to-all-start.1 = ((f32[32,64,256]{2,1,0:T(8,128)}), f32[32,64,256]{2,1,0:T(8,128)}, u32[]{:S(2)}, u32[]{:S(2)}) async-start(f32[32,64,256]{2,1,0:T(8,128)} %gather.3), calls=%async_computation.1 | async-start | bytes 4194304 | tf_op jit(solution)/shard_map/all_to_all | solution.py:366
  48.4 23.6 %gather.2 = (f32[32,64,256]{2,1,0:T(8,128)}, s32[8192]{0:T(1024)}) custom-call(s32[1]{0:T(128)S(6)} %copy.8.count, s32[8192]{0:T(1024)} %get-tuple-element.10.order, s32[32768]{0:T(1024)} %iota_select_fusion.table, f32[32768,128]{1,0:T(8,128)} %bitcast.6), custom_call_target="tpu_custom_call" | custom-call | flops 16384000 | bytes 40960000 | tf_op jit(solution)/shard_map/gather/pallas_call | solution.py:102
  72.1 0.0 copy-start
  72.1 4.7 %all-to-all-done.1.both.a_ref = f32[32,64,256]{2,1,0:T(8,128)} async-done(((f32[32,64,256]{2,1,0:T(8,128)}), f32[32,64,256]{2,1,0:T(8,128)}, u32[]{:S(2)}, u32[]{:S(2)}) %all-to-all-start.1) | async-done | bytes 2097184 | tf_op jit(solution)/shard_map/all_to_all | solution.py:366
  76.8 0.0 copy-start.1
  76.8 0.0 copy-start.2
  76.8 5.3 %all-to-all-start = ((f32[32,64,256]{2,1,0:T(8,128)}), f32[32,64,256]{2,1,0:T(8,128)}, u32[]{:S(2)}, u32[]{:S(2)}) async-start(f32[32,64,256]{2,1,0:T(8,128)} %get-tuple-element.8._), calls=%async_computation | async-start | bytes 4194304 | tf_op jit(solution)/shard_map/all_to_all | solution.py:366
  82.1 0.0 copy-done
  82.1 0.0 copy-start.4
  82.1 0.0 copy-start.6
  82.2 1.4 greater_part.2
  83.5 2.8 %collective-permute-start.2 = (f32[32,32,256]{2,1,0:T(8,128)S(1)}, f32[32,32,256]{2,1,0:T(8,128)S(1)}, u32[]{:S(2)}, u32[]{:S(2)}) collective-permute-start(f32[32,32,256]{2,1,0:T(8,128)S(1)} %greater_part.2), channel_id=1, source_target_pairs={{0,96},{32,64},{64,32},{96,0},{1,97},{33,65},{65,33},{97,1},{2,98}... | collective-permute-start | bytes 3145736 | tf_op jit(solution)/shard_map/ppermute | solution.py:369
  86.3 0.0 copy-done.1
  86.3 0.0 copy-done.2
  86.3 17.4 %columns_in_order.1.rest_0_ = s32[8192]{0:T(1024)S(1)} custom-call(s32[8192]{0:T(1024)S(1)} %copy-done.2, s32[32768]{0:T(1024)S(1)} %copy-done.1, f32[32,64,256]{2,1,0:T(8,128)S(1)} %copy-done), custom_call_target="tpu_custom_call" | custom-call | flops 16384000 | bytes 40960000 | tf_op jit(solution)/shard_map/columns_in_order/pallas_call | solution.py:128
  103.8 5.6 %collective-permute-done.2.b_ref = f32[32,32,256]{2,1,0:T(8,128)S(1)} collective-permute-done((f32[32,32,256]{2,1,0:T(8,128)S(1)}, f32[32,32,256]{2,1,0:T(8,128)S(1)}, u32[]{:S(2)}, u32[]{:S(2)}) %collective-permute-start.2) | collective-permute-done | bytes 1048608 | tf_op jit(solution)/shard_map/ppermute | solution.py:369
  109.4 0.0 copy-done.4
  109.4 0.0 copy-done.6
  109.4 10.7 %correlate.2._ = f32[32,32,256]{2,1,0:T(8,128)} custom-call(bf16[512,768]{1,0:T(8,128)(2,1)S(1)} %copy-done.6, f32[3,2,256,128]{3,2,1,0:T(8,128)S(1)} %copy-done.4, f32[32,64,256]{2,1,0:T(8,128)} %all-to-all-done.1.both.a_ref, f32[32,32,256]{2,1,0:T(8,128)S(1)} %collective-permute-done.2.b_ref, s32[8192]{0:T(1024)S(1)} %columns_in_order.1.rest_0_), custom_call_target="tpu_custom_call" | custom-call | flops 4831838208 | bytes 3145728 | tf_op jit(solution)/shard_map/correlate/pallas_call | solution.py:226
  120.1 0.0 all-to-all-done.both.a_ref
  120.1 1.2 greater_part.3
  121.3 2.7 %collective-permute-start.3 = (f32[32,32,256]{2,1,0:T(8,128)S(1)}, f32[32,32,256]{2,1,0:T(8,128)S(1)}, u32[]{:S(2)}, u32[]{:S(2)}) collective-permute-start(f32[32,32,256]{2,1,0:T(8,128)S(1)} %greater_part.3), channel_id=1, source_target_pairs={{0,96},{32,64},{64,32},{96,0},{1,97},{33,65},{65,33},{97,1},{2,98}... | collective-permute-start | bytes 3145736 | tf_op jit(solution)/shard_map/ppermute | solution.py:369
  124.0 8.6 %all-to-all-start.3 = ((f32[32,32,256]{2,1,0:T(8,128)}), f32[32,32,256]{2,1,0:T(8,128)S(1)}, u32[]{:S(2)}, u32[]{:S(2)}) async-start(f32[32,32,256]{2,1,0:T(8,128)} %correlate.2._), calls=%async_computation.3 | async-start | bytes 2097152 | tf_op jit(solution)/shard_map/all_to_all | solution.py:366
  132.6 0.0 copy-start.3
  132.6 13.6 %collective-permute-done.3.b_ref = f32[32,32,256]{2,1,0:T(8,128)S(1)} collective-permute-done((f32[32,32,256]{2,1,0:T(8,128)S(1)}, f32[32,32,256]{2,1,0:T(8,128)S(1)}, u32[]{:S(2)}, u32[]{:S(2)}) %collective-permute-start.3) | collective-permute-done | bytes 1048608 | tf_op jit(solution)/shard_map/ppermute | solution.py:369
  146.2 0.0 copy-start.5
  146.2 1.1 copy-done.5
  147.3 0.0 copy-start.7
  147.3 1.1 copy-done.7
  148.5 10.7 %correlate.3 = f32[32,32,256]{2,1,0:T(8,128)} custom-call(bf16[512,768]{1,0:T(8,128)(2,1)S(1)} %copy-done.7, f32[3,2,256,128]{3,2,1,0:T(8,128)S(1)} %copy-done.5, f32[32,64,256]{2,1,0:T(8,128)} %all-to-all-done.both.a_ref, f32[32,32,256]{2,1,0:T(8,128)S(1)} %collective-permute-done.3.b_ref), custom_call_target="tpu_custom_call" | custom-call | flops 4831838208 | bytes 3145728 | tf_op jit(solution)/shard_map/correlate/pallas_call | solution.py:226
  159.2 0.0 all-to-all-done.3.values
  159.2 9.1 %all-to-all-start.2 = ((f32[32,32,256]{2,1,0:T(8,128)}), f32[32,32,256]{2,1,0:T(8,128)S(1)}, u32[]{:S(2)}, u32[]{:S(2)}) async-start(f32[32,32,256]{2,1,0:T(8,128)} %correlate.3), calls=%async_computation.2 | async-start | bytes 2097152 | tf_op jit(solution)/shard_map/all_to_all | solution.py:366
  168.3 0.0 copy-done.3
  168.3 13.9 %scatter.2.before = f32[6,8192,128]{2,1,0:T(8,128)} custom-call(s32[8192]{0:T(1024)S(1)} %and_or_fusion.row_of, s32[64,128]{1,0:T(8,128)S(1)} %bitcast.3, f32[32,32,256]{2,1,0:T(8,128)S(1)} %all-to-all-done.3.values), custom_call_target="tpu_custom_call" | custom-call | flops 8192000 | bytes 32768000 | tf_op jit(solution)/shard_map/scatter/pallas_call | solution.py:335
  182.2 3.0 %all-to-all-done.2.values = f32[32,32,256]{2,1,0:T(8,128)S(1)} async-done(((f32[32,32,256]{2,1,0:T(8,128)}), f32[32,32,256]{2,1,0:T(8,128)S(1)}, u32[]{:S(2)}, u32[]{:S(2)}) %all-to-all-start.2) | async-done | bytes 1048608 | tf_op jit(solution)/shard_map/all_to_all | solution.py:366
  185.2 16.2 %scatter.3 = f32[2,16,32768]{2,1,0:T(8,128)} custom-call(s32[8192]{0:T(1024)S(1)} %and_or_fusion.1.row_of, s32[64,128]{1,0:T(8,128)S(1)} %bitcast.4, f32[32,32,256]{2,1,0:T(8,128)S(1)} %all-to-all-done.2.values, f32[6,8192,128]{2,1,0:T(8,128)} %scatter.2.before), custom_call_target="tpu_custom_call" | custom-call | flops 8192000 | bytes 32768000 | tf_op jit(solution)/shard_map/scatter/pallas_call | solution.py:335
  (3 shorter events, 0.0 us)
Async XLA Ops:
  0.8 19.1 %collective-permute-start = (s32[16384]{0:T(1024)S(1)}, s32[16384]{0:T(1024)S(1)}, u32[]{:S(2)}, u32[]{:S(2)}) collective-permute-start(s32[16384]{0:T(1024)S(1)} %slice.10), channel_id=1, source_target_pairs={{0,96},{32,64},{64,32},{96,0},{1,97},{33,65},{65,33},{97,1},{2,98}... | collective-permute-start | bytes 196616 | tf_op jit(solution)/shard_map/ppermute | solution.py:352
  4.4 16.2 %collective-permute-start.1 = (s32[32768]{0:T(1024)}, s32[32768]{0:T(1024)S(1)}, u32[]{:S(2)}, u32[]{:S(2)}) collective-permute-start(s32[32768]{0:T(1024)} %param.11), channel_id=1, source_target_pairs={{0,96},{32,64},{64,32},{96,0},{1,97},{33,65},{65,33},{97,1},{2,98}... | collective-permute-start | bytes 393224 | tf_op jit(solution)/shard_map/ppermute | solution.py:351
  5.1 14.8 %copy-start.8 = (s32[32768]{0:T(1024)S(1)}, s32[32768]{0:T(1024)}, u32[]{:S(2)}) copy-start(s32[32768]{0:T(1024)} %param.9) | copy-start | bytes 393220
  39.3 37.5 %all-to-all-start.1 = ((f32[32,64,256]{2,1,0:T(8,128)}), f32[32,64,256]{2,1,0:T(8,128)}, u32[]{:S(2)}, u32[]{:S(2)}) async-start(f32[32,64,256]{2,1,0:T(8,128)} %gather.3), calls=%async_computation.1 | async-start | bytes 4194304 | tf_op jit(solution)/shard_map/all_to_all | solution.py:366
  72.1 10.1 %copy-start = (f32[32,64,256]{2,1,0:T(8,128)S(1)}, f32[32,64,256]{2,1,0:T(8,128)}, u32[]{:S(2)}) copy-start(f32[32,64,256]{2,1,0:T(8,128)} %get-tuple-element.8._) | copy-start | bytes 6291460
  76.8 9.6 %copy-start.1 = (s32[32768]{0:T(1024)S(1)}, s32[32768]{0:T(1024)}, u32[]{:S(2)}) copy-start(s32[32768]{0:T(1024)} %iota_select_fusion.table) | copy-start | bytes 393220
  76.8 9.6 %copy-start.2 = (s32[8192]{0:T(1024)S(1)}, s32[8192]{0:T(1024)}, u32[]{:S(2)}) copy-start(s32[8192]{0:T(1024)} %get-tuple-element.9.order) | copy-start | bytes 98308
  76.8 43.3 %all-to-all-start = ((f32[32,64,256]{2,1,0:T(8,128)}), f32[32,64,256]{2,1,0:T(8,128)}, u32[]{:S(2)}, u32[]{:S(2)}) async-start(f32[32,64,256]{2,1,0:T(8,128)} %get-tuple-element.8._), calls=%async_computation | async-start | bytes 4194304 | tf_op jit(solution)/shard_map/all_to_all | solution.py:366
  82.1 27.2 %copy-start.4 = (f32[3,2,256,128]{3,2,1,0:T(8,128)S(1)}, f32[3,2,256,128]{3,2,1,0:T(8,128)}, u32[]{:S(2)}) copy-start(f32[3,2,256,128]{3,2,1,0:T(8,128)} %constant.19.clone.turn) | copy-start | bytes 2359300
  82.1 27.2 %copy-start.6 = (bf16[512,768]{1,0:T(8,128)(2,1)S(1)}, bf16[512,768]{1,0:T(8,128)(2,1)}, u32[]{:S(2)}) copy-start(bf16[512,768]{1,0:T(8,128)(2,1)} %constant.18.clone.matrix) | copy-start | bytes 2359300
  83.5 25.9 %collective-permute-start.2 = (f32[32,32,256]{2,1,0:T(8,128)S(1)}, f32[32,32,256]{2,1,0:T(8,128)S(1)}, u32[]{:S(2)}, u32[]{:S(2)}) collective-permute-start(f32[32,32,256]{2,1,0:T(8,128)S(1)} %greater_part.2), channel_id=1, source_target_pairs={{0,96},{32,64},{64,32},{96,0},{1,97},{33,65},{65,33},{97,1},{2,98}... | collective-permute-start | bytes 3145736 | tf_op jit(solution)/shard_map/ppermute | solution.py:369
  121.3 24.9 %collective-permute-start.3 = (f32[32,32,256]{2,1,0:T(8,128)S(1)}, f32[32,32,256]{2,1,0:T(8,128)S(1)}, u32[]{:S(2)}, u32[]{:S(2)}) collective-permute-start(f32[32,32,256]{2,1,0:T(8,128)S(1)} %greater_part.3), channel_id=1, source_target_pairs={{0,96},{32,64},{64,32},{96,0},{1,97},{33,65},{65,33},{97,1},{2,98}... | collective-permute-start | bytes 3145736 | tf_op jit(solution)/shard_map/ppermute | solution.py:369
  124.0 35.2 %all-to-all-start.3 = ((f32[32,32,256]{2,1,0:T(8,128)}), f32[32,32,256]{2,1,0:T(8,128)S(1)}, u32[]{:S(2)}, u32[]{:S(2)}) async-start(f32[32,32,256]{2,1,0:T(8,128)} %correlate.2._), calls=%async_computation.3 | async-start | bytes 2097152 | tf_op jit(solution)/shard_map/all_to_all | solution.py:366
  132.6 35.7 %copy-start.3 = (s32[8192]{0:T(1024)S(1)}, s32[8192]{0:T(1024)}, u32[]{:S(2)}) copy-start(s32[8192]{0:T(1024)} %get-tuple-element.7) | copy-start | bytes 98308
  146.2 1.1 copy-start.5
  147.3 1.1 copy-start.7
  159.2 26.0 %all-to-all-start.2 = ((f32[32,32,256]{2,1,0:T(8,128)}), f32[32,32,256]{2,1,0:T(8,128)S(1)}, u32[]{:S(2)}, u32[]{:S(2)}) async-start(f32[32,32,256]{2,1,0:T(8,128)} %correlate.3), calls=%async_computation.2 | async-start | bytes 2097152 | tf_op jit(solution)/shard_map/all_to_all | solution.py:366

commit v3 on v2

v3 whole, which is shorter than its diff:
```python
import functools
import math

import jax
import jax.numpy as jnp
import ml_dtypes
import numpy as np
from jax import lax
from jax.experimental import pallas as pl
from jax.experimental.pallas import tpu as pltpu

F32 = jnp.float32
BF16 = jnp.bfloat16
SLOTS = 32768
LIVE = 16384
ENERGIES = 512
PARTS = 32
WIDTHS = (256, 256)
VMEM_BYTES = 60 << 20
SMEM = pl.BlockSpec(memory_space=pltpu.SMEM)
VMEM = pl.BlockSpec(memory_space=pltpu.VMEM)
ANY = pl.BlockSpec(memory_space=pl.ANY)
UNROLL = 32
BATCH = 4
TILE = 256


def params(limit=VMEM_BYTES):
    return pltpu.CompilerParams(vmem_limit_bytes=limit)


def cost(flops, bytes_accessed):
    return pl.CostEstimate(flops=flops, bytes_accessed=bytes_accessed, transcendentals=0)


def rows_kernel(a_low, b_low, a_high, b_high, rows):
    for j in range(a_low.shape[-1] // 128):
        s = slice(j * 128, (j + 1) * 128)
        block = [ref[:, :, s].reshape(32, 128) for ref in (a_low, b_low, a_high, b_high)]
        rows[s, :] = jnp.concatenate(block, 0).T


def column_rows(a, b, block=4096):
    steps = LIVE // block
    low = pl.BlockSpec((2, 16, block), lambda i: (0, 0, i))
    high = pl.BlockSpec((2, 16, block), lambda i: (0, 0, i + steps))
    return pl.pallas_call(
        rows_kernel,
        grid=(steps,),
        in_specs=[low, low, high, high],
        out_specs=pl.BlockSpec((block, 128), lambda i: (i, 0)),
        out_shape=jax.ShapeDtypeStruct((LIVE, 128), F32),
        compiler_params=params(),
        cost_estimate=cost(1 << 20, 24 << 20),
        name="column_rows",
    )(a, b, a, b)


def gather_kernel(count, order_in, map_in, rows, out, places, packed, order, mapped, table, sems, row_sems, *, base):
    width = out.shape[-1]
    per = width // 128
    copies = [
        pltpu.make_async_copy(map_in, mapped, sems.at[0]),
        pltpu.make_async_copy(order_in, order, sems.at[1]),
    ]
    parts = row_sems.shape[0]
    span = LIVE // parts
    loads = []
    for p in range(parts):
        s = pl.ds(p * span, span)
        loads.append(pltpu.make_async_copy(rows.at[s, :], table.at[s, :], row_sems.at[p]))
    for copy in copies + loads:
        copy.start()
    step = 2048
    first_half = lax.broadcasted_iota(jnp.int32, (8, 128), 1) < 64
    number = lax.broadcasted_iota(jnp.int32, (8, 128), 0).astype(F32)
    for p in range(parts):
        loads[p].wait()

        def widen(k, _):
            first = pl.multiple_of(p * span + k * step, step)
            offset = number + first.astype(F32)
            for r in range(0, step, 8):
                both = table[pl.ds(first + r, 8), :]
                high = pltpu.roll(both, 64, 1)
                column = offset + float(r)
                table[pl.ds(first + r, 8), :] = jnp.where(first_half, both, column)
                table[pl.ds(first + r + LIVE, 8), :] = jnp.where(first_half, high, column + float(LIVE))
            return 0

        lax.fori_loop(0, span // step, widen, 0)
    for copy in copies:
        copy.wait()
    lane = lax.broadcasted_iota(jnp.int32, (1, 128), 1)

    def batch(k, _):
        for r in range(0, BATCH * 128, UNROLL):
            first = pl.multiple_of(k * (BATCH * 128) + r, UNROLL)
            cols = [mapped[order[first + u]] for u in range(UNROLL)]
            for u in range(UNROLL):
                packed[r + u : r + u + 1, :] = table[pl.ds(cols[u], 1), :]
        blocks = [packed[b * 128 : (b + 1) * 128, :].T for b in range(BATCH)]
        for b in range(BATCH):
            block = k * BATCH + b
            w = b % per * 128
            live = lane + (block * 128 + base) < count[0]
            out[block // per, :, w : w + 128] = jnp.where(live, blocks[b][:64], 0.0)
            places[pl.ds(block, 1), :] = blocks[b][64:65].astype(jnp.int32)
        return 0

    lax.fori_loop(0, PARTS * per // BATCH, batch, 0)


def gather(count, order, table, rows, base, width):
    items = PARTS * width
    return pl.pallas_call(
        functools.partial(gather_kernel, base=base),
        in_specs=[SMEM, ANY, ANY, ANY],
        out_specs=[VMEM, VMEM],
        out_shape=[
            jax.ShapeDtypeStruct((PARTS, 64, width), F32),
            jax.ShapeDtypeStruct((items // 128, 128), jnp.int32),
        ],
        scratch_shapes=[
            pltpu.VMEM((BATCH * 128, 128), F32),
            pltpu.SMEM((items,), jnp.int32),
            pltpu.SMEM((SLOTS,), jnp.int32),
            pltpu.VMEM((SLOTS, 128), F32),
            pltpu.SemaphoreType.DMA((2,)),
            pltpu.SemaphoreType.DMA((4,)),
        ],
        compiler_params=params(),
        cost_estimate=cost(items * 2000, items * 5000),
        name="gather",
    )(count, order, table, rows)


def tables():
    n = np.arange(256)
    angle = 2.0 * np.pi * ((n[:, None] * n[None, :]) % 256) / 256.0
    matrix = np.concatenate([np.cos(angle), np.sin(angle)], 0).astype(np.float32)
    high = matrix.astype(ml_dtypes.bfloat16)
    low = (matrix - high.astype(np.float32)).astype(ml_dtypes.bfloat16)
    matrix = np.concatenate([high, high, low], 1)
    phase = 2.0 * np.pi * np.arange(1, 4)[:, None] * n[None, :] / 1024.0
    turn = np.stack([np.cos(phase), np.sin(phase)], 1).astype(np.float32)
    return matrix, np.repeat(turn[:, :, :, None], 128, 3)


def split(values):
    high = values.astype(BF16)
    low = (values - high.astype(F32)).astype(BF16)
    return jnp.concatenate([high, low, high], 0)


def halves(ref, part, lanes):
    values = ref[:, part * 16 : part * 16 + 16, lanes].reshape(ENERGIES, -1)
    return values[:256], values[256:]


def turned(turn, r, lanes):
    repeat = (lanes.stop - lanes.start) // 128
    return [jnp.concatenate([turn[r - 1, part]] * repeat, 1) for part in range(2)]


def product(matrix, re, im):
    both = jnp.dot(matrix[...], split(jnp.concatenate([re, im], 1)), preferred_element_type=F32)
    half = re.shape[1]
    return both[:256, :half], both[:256, half:], both[256:, :half], both[256:, half:]


def lesser_kernel(matrix, turn, both, spectrum):
    for w in range(0, both.shape[-1], TILE):
        lanes = slice(w, w + TILE)
        re0, re1 = halves(both, 0, lanes)
        im0, im1 = halves(both, 1, lanes)
        for r in range(4):
            re = (re0 + re1, re0 + im1, re0 - re1, re0 - im1)[r]
            im = (im0 + im1, im0 - re1, im0 - im1, im0 + re1)[r]
            if r:
                c, s = turned(turn, r, lanes)
                re, im = re * c + im * s, im * c - re * s
            cos_re, cos_im, sin_re, sin_im = product(matrix, re, im)
            spectrum[r, 0, :, lanes] = cos_re + sin_im
            spectrum[r, 1, :, lanes] = cos_im - sin_re


def lesser_spectrum(matrix, turn, both):
    width = both.shape[-1]
    return pl.pallas_call(
        lesser_kernel,
        in_specs=[VMEM] * 3,
        out_specs=VMEM,
        out_shape=jax.ShapeDtypeStruct((4, 2, 256, width), F32),
        compiler_params=params(),
        cost_estimate=cost(width * 2 * 4 * 512 * 768 * 2, width * 12288),
        name="lesser_spectrum",
    )(matrix, turn, both)


def correlate_kernel(matrix, turn, spectrum, b_ref, out):
    scale = 1.0 / (1024.0 * math.sqrt(ENERGIES))
    for w in range(0, b_ref.shape[-1], TILE):
        lanes = slice(w, w + TILE)
        re0, re1 = halves(b_ref, 0, lanes)
        im0, im1 = halves(b_ref, 1, lanes)
        low_re = low_im = high_re = high_im = None
        for r in range(4):
            re = (re0 + re1, re0 - im1, re0 - re1, re0 + im1)[r]
            im = (im0 + im1, im0 + re1, im0 - im1, im0 - re1)[r]
            if r:
                c, s = turned(turn, r, lanes)
                re, im = re * c - im * s, im * c + re * s
            cos_re, cos_im, sin_re, sin_im = product(matrix, re, im)
            b_re, b_im = cos_re - sin_im, cos_im + sin_re
            a_re, a_im = spectrum[r, 0, :, lanes], spectrum[r, 1, :, lanes]
            cos_re, cos_im, sin_re, sin_im = product(
                matrix, a_re * b_re - a_im * b_im, a_re * b_im + a_im * b_re
            )
            re, im = cos_re - sin_im, cos_im + sin_re
            if r:
                re, im = re * c - im * s, re * s + im * c
            if r == 0:
                low_re, low_im, high_re, high_im = re, im, re, im
            else:
                low_re, low_im = low_re + re, low_im + im
                if r == 1:
                    high_re, high_im = high_re - im, high_im + re
                elif r == 2:
                    high_re, high_im = high_re - re, high_im - im
                else:
                    high_re, high_im = high_re + im, high_im - re
        shape = (16, 16, TILE)
        out[:16, :16, lanes] = (low_im * scale).reshape(shape)
        out[16:, :16, lanes] = (high_im * scale).reshape(shape)
        out[:16, 16:, lanes] = (low_re * -scale).reshape(shape)
        out[16:, 16:, lanes] = (high_re * -scale).reshape(shape)


def correlate(matrix, turn, spectrum, b):
    width = b.shape[-1]
    return pl.pallas_call(
        correlate_kernel,
        in_specs=[VMEM] * 4,
        out_specs=VMEM,
        out_shape=jax.ShapeDtypeStruct((PARTS, 32, width), F32),
        compiler_params=params(),
        cost_estimate=cost(width * 2 * 4 * 512 * 768 * 4, width * 12288),
        name="correlate",
    )(matrix, turn, spectrum, b)


def scatter_rows(row_of, column, values, out, packed):
    per = values.shape[-1] // 128

    def batch(k, _):
        blocks = []
        for b in range(BATCH):
            block = k * BATCH + b
            w = b % per * 128
            group = (column[pl.ds(block, 1), :] >> 7) & 3
            data = values[block // per, :, w : w + 128]
            blocks.append(jnp.concatenate([jnp.where(group == g, data, 0.0) for g in range(4)], 0).T)
        for b in range(BATCH):
            packed[b * 128 : (b + 1) * 128, :] = blocks[b]
        for r in range(0, BATCH * 128, UNROLL):
            first = pl.multiple_of(k * (BATCH * 128) + r, UNROLL)
            rows = [row_of[first + u] for u in range(UNROLL)]
            for u in range(UNROLL):
                row = packed[r + u : r + u + 1, :]
                pltpu.store(out.at[pl.ds(rows[u], 1), :], row, mask=row != 0.0)
        return 0

    lax.fori_loop(0, PARTS * per // BATCH, batch, 0)


def scatter_first_kernel(row_of, column, values, out, packed, slots, sem):
    slots[...] = jnp.zeros_like(slots)
    scatter_rows(row_of, column, values, slots, packed)
    save = pltpu.make_async_copy(slots, out.at[0], sem)
    save.start()
    save.wait()


def scatter_last_kernel(row_of, column, values, before, out, packed, slots, earlier, staged, in_sem, out_sem):
    load = pltpu.make_async_copy(before.at[0], earlier, in_sem)
    load.start()
    slots[...] = jnp.zeros_like(slots)
    scatter_rows(row_of, column, values, slots, packed)
    load.wait()
    pieces = out_sem.shape[0]
    span = SLOTS // pieces
    copies = []
    for p in range(pieces):
        for q in range(p * span // 512, (p + 1) * span // 512):
            rows = slice(q * 128, (q + 1) * 128)
            block = (slots[rows, :] + earlier[rows, :]).T
            for g in range(4):
                s = slice(q * 512 + g * 128, q * 512 + (g + 1) * 128)
                staged[:, :, s] = block[g * 32 : (g + 1) * 32].reshape(2, 16, 128)
        piece = slice(p * span, (p + 1) * span)
        copies.append(pltpu.make_async_copy(staged.at[:, :, piece], out.at[:, :, piece], out_sem.at[p]))
        copies[-1].start()
    for copy in copies:
        copy.wait()


def scatter(columns, values, before):
    width = values.shape[-1]
    items = PARTS * width
    row_of = ((columns >> 9 << 7) | (columns & 127)).reshape(items)
    first = before is None
    scratch = [
        pltpu.VMEM((BATCH * 128, 128), F32),
        pltpu.VMEM((SLOTS // 4, 128), F32),
    ]
    if first:
        scratch += [pltpu.SemaphoreType.DMA]
    else:
        scratch += [
            pltpu.VMEM((SLOTS // 4, 128), F32),
            pltpu.VMEM((2, 16, SLOTS), F32),
            pltpu.SemaphoreType.DMA,
            pltpu.SemaphoreType.DMA((8,)),
        ]
    return pl.pallas_call(
        scatter_first_kernel if first else scatter_last_kernel,
        in_specs=[SMEM, VMEM, VMEM] + ([] if first else [ANY]),
        out_specs=ANY,
        out_shape=jax.ShapeDtypeStruct((6, SLOTS // 4, 128) if first else (2, 16, SLOTS), F32),
        scratch_shapes=scratch,
        compiler_params=params(44 << 20),
        cost_estimate=cost(items * 1000, items * 4000),
        name="scatter",
    )(row_of, columns, values, *(() if first else (before,)))


def local(g_lesser, g_greater, live_columns, live_count, mirror):
    slabs = lax.axis_size("slab")
    across = [(s, slabs - 1 - s) for s in range(slabs)]
    is_upper = lax.axis_index("slab") >= slabs // 2
    other_mirror = lax.ppermute(mirror, "slab", across)
    other_live = lax.ppermute(live_columns[:LIVE], "slab", across)
    order = jnp.where(is_upper, other_live, live_columns[:LIVE])
    table = jnp.where(is_upper, other_mirror, jnp.arange(SLOTS, dtype=jnp.int32))
    matrix, turn = tables()
    matrix, turn = jnp.asarray(matrix), jnp.asarray(turn)

    rows = column_rows(g_lesser, g_greater)
    half = WIDTHS[0]
    orders = [order[: PARTS * half], order[PARTS * half :]]
    picked0, columns0 = gather(live_count, orders[0], table, rows, 0, half)
    picked1, columns1 = gather(live_count, orders[1], table, rows, PARTS * half, WIDTHS[1])

    def swap(values):
        return lax.all_to_all(values, "energy", 0, 0, tiled=True)

    def mirrored(arrived):
        return lax.ppermute(arrived[:, 32:], "slab", across)

    arrived0 = swap(picked0)
    mirrored0 = mirrored(arrived0)
    arrived1 = swap(picked1)
    spectrum0 = lesser_spectrum(matrix, turn, arrived0)
    arrived1, spectrum0 = lax.optimization_barrier((arrived1, spectrum0))
    mirrored1 = mirrored(arrived1)
    polar0 = swap(correlate(matrix, turn, spectrum0, mirrored0))
    spectrum1 = lesser_spectrum(matrix, turn, arrived1)
    polar1 = swap(correlate(matrix, turn, spectrum1, mirrored1))
    slots = scatter(columns0, polar0, None)
    return scatter(columns1, polar1, slots)


def solution(mesh):
    spec = jax.P(None, "energy", "slab")
    return jax.shard_map(
        local,
        mesh=mesh,
        in_specs=(spec, spec, jax.P("slab"), jax.P("slab"), jax.P("slab")),
        out_specs=spec,
        check_vma=False,
    )
```

time: 203 us -> 174 us (0.86)
  Pallas kernels: 128 us -> 96.3 us
  waiting for transfers between devices: 26.9 us -> 36.4 us
  starting transfers between devices: 41.2 us -> 33.6 us
    all_to_all x4, waiting for transfers between devices: 7.68 us -> 32.6 us  [swap(): return lax.all_to_all(values, 'energy', 0, 0, tiled=True)]
    pallas_call x7 -> x6, Pallas kernels: 83.1 us -> 59.8 us  [the longest x2 33.1 us: gather(): pl.pallas_call(functools.partial(gather_kernel, base=base), in_specs=[SME...]
    ppermute x2, waiting for transfers between devices: 19.2 us -> 3.88 us  [mirrored(): return lax.ppermute(arrived[:, 32:], 'slab', across)]
    all_to_all x4, starting transfers between devices: 32.2 us -> 24.3 us  [swap(): return lax.all_to_all(values, 'energy', 0, 0, tiled=True)]
    pallas_call x1, Pallas kernels: 14.8 us -> 7.87 us  [column_rows(): pl.pallas_call(rows_kernel, grid=(steps,), in_specs=[low, low, high, high...]
    slice x0 -> x2, local copies, waits for them, and re-layouts: none -> 2.46 us  [mirrored(): return lax.ppermute(arrived[:, 32:], 'slab', across)]
  transfers between devices with their start and end apart: 8 -> 8, of which waited for: 4 -> 4; matrix products, arithmetic and copies ran while one was open for 0% -> 2% of each run, Pallas kernels for 46% -> 38%
where the time goes in v3:
time: 174 us; the launch traced here: 173 us
  Pallas kernels  96.3 us (55%)
  waiting for transfers between devices  36.4 us (21%)
  starting transfers between devices  33.6 us (19%)
  local copies, waits for them, and re-layouts  5.25 us (3%)
    pallas_call x2, Pallas kernels, gather(): pl.pallas_call(functools.partial(gather_kernel, base=base), in_specs=[SME...  33.1 us
    all_to_all x4, waiting for transfers between devices, swap(): return lax.all_to_all(values, 'energy', 0, 0, tiled=True)  32.6 us
    pallas_call x2, Pallas kernels, scatter(): pl.pallas_call(scatter_first_kernel if first else scatter_last_kernel, in...  28.6 us
    all_to_all x4, starting transfers between devices, swap(): return lax.all_to_all(values, 'energy', 0, 0, tiled=True)  24.3 us
    pallas_call x2, Pallas kernels, correlate(): pl.pallas_call(correlate_kernel, in_specs=[VMEM] * 4, out_specs=VMEM, out...  16.1 us
    pallas_call x2, Pallas kernels, lesser_spectrum(): pl.pallas_call(lesser_kernel, in_specs=[VMEM] * 3, out_specs=VMEM, out_sh...  10.6 us
    pallas_call x1, Pallas kernels, column_rows(): pl.pallas_call(rows_kernel, grid=(steps,), in_specs=[low, low, high, high...  7.87 us
    ppermute x2, starting transfers between devices, mirrored(): return lax.ppermute(arrived[:, 32:], 'slab', across)  5.74 us
  transfers between devices with their start and end apart: 8, of which 4 were waited for; matrix products, arithmetic and copies ran while one was open for 2% of the time, Pallas kernels for 38%

profile of v3, /device:TPU:1, one launch (start us, length us, event | category | flops | bytes accessed | tf_op | source)
XLA Modules:
  0.0 173.2 jit_solution(16793665349968928944)
XLA Ops:
  0.0 0.8 slice.16
  0.8 3.6 %collective-permute-start = (s32[16384]{0:T(1024)S(1)}, s32[16384]{0:T(1024)S(1)}, u32[]{:S(2)}, u32[]{:S(2)}) collective-permute-start(s32[16384]{0:T(1024)S(1)} %slice.16), channel_id=1, source_target_pairs={{0,96},{32,64},{64,32},{96,0},{1,97},{33,65},{65,33},{97,1},{2,98}... | collective-permute-start | bytes 196616 | tf_op jit(solution)/shard_map/ppermute | solution.py:343
  4.4 0.0 collective-permute-start.1
  5.1 0.0 copy-start.4
  5.1 7.9 %column_rows.1.rows = f32[16384,128]{1,0:T(8,128)} custom-call(f32[2,16,32768]{2,1,0:T(8,128)} %a_high.1, f32[2,16,32768]{2,1,0:T(8,128)} %b_high.1, f32[2,16,32768]{2,1,0:T(8,128)} %a_high.1, f32[2,16,32768]{2,1,0:T(8,128)} %b_high.1), custom_call_target="tpu_custom_call" | custom-call | flops 1048576 | bytes 25165824 | tf_op jit(solution)/shard_map/column_rows/pallas_call | solution.py:47
  13.0 0.0 collective-permute-done
  13.0 0.0 copy-done.4
  13.0 0.6 fusion
  13.6 0.0 collective-permute-done.1
  13.6 0.7 iota_select_fusion.map_in
  14.3 16.6 %gather.3 = (f32[32,64,256]{2,1,0:T(8,128)}, s32[64,128]{1,0:T(8,128)}) custom-call(s32[1]{0:T(128)S(6)} %copy.8.count, s32[8192]{0:T(1024)} %get-tuple-element.17.order_in, s32[32768]{0:T(1024)} %iota_select_fusion.map_in, f32[16384,128]{1,0:T(8,128)} %column_rows.1.rows), custom_call_target="tpu_custom_call" | custom-call | flops 16384000 | bytes 40960000 | tf_op jit(solution)/shard_map/gather/pallas_call | solution.py:116
  30.9 9.1 %all-to-all-start.1 = ((f32[32,64,256]{2,1,0:T(8,128)}), f32[32,64,256]{2,1,0:T(8,128)S(1)}, u32[]{:S(2)}, u32[]{:S(2)}) async-start(f32[32,64,256]{2,1,0:T(8,128)} %get-tuple-element.13), calls=%async_computation.1 | async-start | bytes 4194304 | tf_op jit(solution)/shard_map/all_to_all | solution.py:356
  40.0 16.5 %gather.2 = (f32[32,64,256]{2,1,0:T(8,128)}, s32[64,128]{1,0:T(8,128)}) custom-call(s32[1]{0:T(128)S(6)} %copy.8.count, s32[8192]{0:T(1024)} %get-tuple-element.18.order_in, s32[32768]{0:T(1024)} %iota_select_fusion.map_in, f32[16384,128]{1,0:T(8,128)} %column_rows.1.rows), custom_call_target="tpu_custom_call" | custom-call | flops 16384000 | bytes 40960000 | tf_op jit(solution)/shard_map/gather/pallas_call | solution.py:116
  56.5 11.8 %all-to-all-done.1.both = f32[32,64,256]{2,1,0:T(8,128)S(1)} async-done(((f32[32,64,256]{2,1,0:T(8,128)}), f32[32,64,256]{2,1,0:T(8,128)S(1)}, u32[]{:S(2)}, u32[]{:S(2)}) %all-to-all-start.1) | async-done | bytes 2097184 | tf_op jit(solution)/shard_map/all_to_all | solution.py:356
  68.3 0.0 copy-start.3
  68.3 1.3 copy-done.3
  69.6 4.5 %all-to-all-start = ((f32[32,64,256]{2,1,0:T(8,128)}), f32[32,64,256]{2,1,0:T(8,128)S(1)}, u32[]{:S(2)}, u32[]{:S(2)}) async-start(f32[32,64,256]{2,1,0:T(8,128)} %get-tuple-element.12), calls=%async_computation | async-start | bytes 4194304 | tf_op jit(solution)/shard_map/all_to_all | solution.py:356
  74.1 2.4 %slice.23 = f32[32,32,256]{2,1,0:T(8,128)} slice(f32[32,64,256]{2,1,0:T(8,128)} %copy-done.3), slice={[0:32], [32:64], [0:256]} | slice | bytes 2097152 | tf_op jit(solution)/shard_map/slice | solution.py:359
  76.5 2.7 %collective-permute-start.3 = (f32[32,32,256]{2,1,0:T(8,128)}, f32[32,32,256]{2,1,0:T(8,128)}, u32[]{:S(2)}, u32[]{:S(2)}) collective-permute-start(f32[32,32,256]{2,1,0:T(8,128)} %slice.23), channel_id=1, source_target_pairs={{0,96},{32,64},{64,32},{96,0},{1,97},{33,65},{65,33},{97,1},{2,98}... | collective-permute-start | bytes 3145736 | tf_op jit(solution)/shard_map/ppermute | solution.py:359
  79.2 5.3 %lesser_spectrum.2.spectrum = f32[4,2,256,256]{3,2,1,0:T(8,128)} custom-call(bf16[512,768]{1,0:T(8,128)(2,1)} %constant.18.clone.matrix, f32[3,2,256,128]{3,2,1,0:T(8,128)} %constant.19.clone.turn, f32[32,64,256]{2,1,0:T(8,128)} %copy-done.3), custom_call_target="tpu_custom_call" | custom-call | flops 1610612736 | bytes 3145728 | tf_op jit(solution)/shard_map/lesser_spectrum/pallas_call | solution.py:190
  84.5 18.0 %all-to-all-done.both = f32[32,64,256]{2,1,0:T(8,128)S(1)} async-done(((f32[32,64,256]{2,1,0:T(8,128)}), f32[32,64,256]{2,1,0:T(8,128)S(1)}, u32[]{:S(2)}, u32[]{:S(2)}) %all-to-all-start) | async-done | bytes 2097184 | tf_op jit(solution)/shard_map/all_to_all | solution.py:356
  102.5 0.0 copy-start.2
  102.5 0.1 slice.19
  102.6 3.0 %collective-permute-start.2 = (f32[32,32,256]{2,1,0:T(8,128)S(1)}, f32[32,32,256]{2,1,0:T(8,128)}, u32[]{:S(2)}, u32[]{:S(2)}) collective-permute-start(f32[32,32,256]{2,1,0:T(8,128)S(1)} %slice.19), channel_id=1, source_target_pairs={{0,96},{32,64},{64,32},{96,0},{1,97},{33,65},{65,33},{97,1},{2,98}... | collective-permute-start | bytes 3145736 | tf_op jit(solution)/shard_map/ppermute | solution.py:359
  105.6 0.0 collective-permute-done.3.b_ref
  105.6 8.1 %correlate.3 = f32[32,32,256]{2,1,0:T(8,128)} custom-call(bf16[512,768]{1,0:T(8,128)(2,1)} %constant.18.clone.matrix, f32[3,2,256,128]{3,2,1,0:T(8,128)} %constant.19.clone.turn, f32[4,2,256,256]{3,2,1,0:T(8,128)} %lesser_spectrum.2.spectrum, f32[32,32,256]{2,1,0:T(8,128)} %collective-permute-done.3.b_ref), custom_call_target="tpu_custom_call" | custom-call | flops 3221225472 | bytes 3145728 | tf_op jit(solution)/shard_map/correlate/pallas_call | solution.py:242
  113.7 0.0 copy-done.2
  113.7 5.3 %all-to-all-start.3 = ((f32[32,32,256]{2,1,0:T(8,128)}), f32[32,32,256]{2,1,0:T(8,128)S(1)}, u32[]{:S(2)}, u32[]{:S(2)}) async-start(f32[32,32,256]{2,1,0:T(8,128)} %correlate.3), calls=%async_computation.3 | async-start | bytes 2097152 | tf_op jit(solution)/shard_map/all_to_all | solution.py:356
  119.0 5.3 %lesser_spectrum.3.spectrum = f32[4,2,256,256]{3,2,1,0:T(8,128)} custom-call(bf16[512,768]{1,0:T(8,128)(2,1)} %constant.18.clone.matrix, f32[3,2,256,128]{3,2,1,0:T(8,128)} %constant.19.clone.turn, f32[32,64,256]{2,1,0:T(8,128)} %copy-done.2), custom_call_target="tpu_custom_call" | custom-call | flops 1610612736 | bytes 3145728 | tf_op jit(solution)/shard_map/lesser_spectrum/pallas_call | solution.py:190
  124.3 3.9 %collective-permute-done.2.b_ref = f32[32,32,256]{2,1,0:T(8,128)} collective-permute-done((f32[32,32,256]{2,1,0:T(8,128)S(1)}, f32[32,32,256]{2,1,0:T(8,128)}, u32[]{:S(2)}, u32[]{:S(2)}) %collective-permute-start.2) | collective-permute-done | bytes 1048608 | tf_op jit(solution)/shard_map/ppermute | solution.py:359
  128.2 8.0 %correlate.2 = f32[32,32,256]{2,1,0:T(8,128)} custom-call(bf16[512,768]{1,0:T(8,128)(2,1)} %constant.18.clone.matrix, f32[3,2,256,128]{3,2,1,0:T(8,128)} %constant.19.clone.turn, f32[4,2,256,256]{3,2,1,0:T(8,128)} %lesser_spectrum.3.spectrum, f32[32,32,256]{2,1,0:T(8,128)} %collective-permute-done.2.b_ref), custom_call_target="tpu_custom_call" | custom-call | flops 3221225472 | bytes 3145728 | tf_op jit(solution)/shard_map/correlate/pallas_call | solution.py:242
  136.2 0.0 copy-start
  136.2 0.0 copy-start.1
  136.2 0.0 all-to-all-done.3.values
  136.2 5.4 %all-to-all-start.2 = ((f32[32,32,256]{2,1,0:T(8,128)}), f32[32,32,256]{2,1,0:T(8,128)S(1)}, u32[]{:S(2)}, u32[]{:S(2)}) async-start(f32[32,32,256]{2,1,0:T(8,128)} %correlate.2), calls=%async_computation.2 | async-start | bytes 2097152 | tf_op jit(solution)/shard_map/all_to_all | solution.py:356
  141.6 0.0 copy-done
  141.7 0.0 copy-done.1
  141.7 14.1 %scatter.2.before = f32[6,8192,128]{2,1,0:T(8,128)} custom-call(s32[8192]{0:T(1024)S(1)} %or_bitcast_fusion.row_of, s32[64,128]{1,0:T(8,128)S(1)} %copy-done, f32[32,32,256]{2,1,0:T(8,128)S(1)} %all-to-all-done.3.values), custom_call_target="tpu_custom_call" | custom-call | flops 8192000 | bytes 32768000 | tf_op jit(solution)/shard_map/scatter/pallas_call | solution.py:326
  155.8 2.8 %all-to-all-done.2.values = f32[32,32,256]{2,1,0:T(8,128)S(1)} async-done(((f32[32,32,256]{2,1,0:T(8,128)}), f32[32,32,256]{2,1,0:T(8,128)S(1)}, u32[]{:S(2)}, u32[]{:S(2)}) %all-to-all-start.2) | async-done | bytes 1048608 | tf_op jit(solution)/shard_map/all_to_all | solution.py:356
  158.6 14.4 %scatter.3 = f32[2,16,32768]{2,1,0:T(8,128)} custom-call(s32[8192]{0:T(1024)S(1)} %or_bitcast_fusion.1.row_of, s32[64,128]{1,0:T(8,128)S(1)} %copy-done.1, f32[32,32,256]{2,1,0:T(8,128)S(1)} %all-to-all-done.2.values, f32[6,8192,128]{2,1,0:T(8,128)} %scatter.2.before), custom_call_target="tpu_custom_call" | custom-call | flops 8192000 | bytes 32768000 | tf_op jit(solution)/shard_map/scatter/pallas_call | solution.py:326
  (3 shorter events, 0.0 us)
Async XLA Ops:
  0.8 12.1 %collective-permute-start = (s32[16384]{0:T(1024)S(1)}, s32[16384]{0:T(1024)S(1)}, u32[]{:S(2)}, u32[]{:S(2)}) collective-permute-start(s32[16384]{0:T(1024)S(1)} %slice.16), channel_id=1, source_target_pairs={{0,96},{32,64},{64,32},{96,0},{1,97},{33,65},{65,33},{97,1},{2,98}... | collective-permute-start | bytes 196616 | tf_op jit(solution)/shard_map/ppermute | solution.py:343
  4.4 9.2 %collective-permute-start.1 = (s32[32768]{0:T(1024)}, s32[32768]{0:T(1024)S(1)}, u32[]{:S(2)}, u32[]{:S(2)}) collective-permute-start(s32[32768]{0:T(1024)} %param.11), channel_id=1, source_target_pairs={{0,96},{32,64},{64,32},{96,0},{1,97},{33,65},{65,33},{97,1},{2,98}... | collective-permute-start | bytes 393224 | tf_op jit(solution)/shard_map/ppermute | solution.py:342
  5.1 7.9 %copy-start.4 = (s32[32768]{0:T(1024)S(1)}, s32[32768]{0:T(1024)}, u32[]{:S(2)}) copy-start(s32[32768]{0:T(1024)} %param.9) | copy-start | bytes 393220
  30.9 37.4 %all-to-all-start.1 = ((f32[32,64,256]{2,1,0:T(8,128)}), f32[32,64,256]{2,1,0:T(8,128)S(1)}, u32[]{:S(2)}, u32[]{:S(2)}) async-start(f32[32,64,256]{2,1,0:T(8,128)} %get-tuple-element.13), calls=%async_computation.1 | async-start | bytes 4194304 | tf_op jit(solution)/shard_map/all_to_all | solution.py:356
  68.3 1.3 copy-start.3
  69.6 32.9 %all-to-all-start = ((f32[32,64,256]{2,1,0:T(8,128)}), f32[32,64,256]{2,1,0:T(8,128)S(1)}, u32[]{:S(2)}, u32[]{:S(2)}) async-start(f32[32,64,256]{2,1,0:T(8,128)} %get-tuple-element.12), calls=%async_computation | async-start | bytes 4194304 | tf_op jit(solution)/shard_map/all_to_all | solution.py:356
  76.5 29.1 %collective-permute-start.3 = (f32[32,32,256]{2,1,0:T(8,128)}, f32[32,32,256]{2,1,0:T(8,128)}, u32[]{:S(2)}, u32[]{:S(2)}) collective-permute-start(f32[32,32,256]{2,1,0:T(8,128)} %slice.23), channel_id=1, source_target_pairs={{0,96},{32,64},{64,32},{96,0},{1,97},{33,65},{65,33},{97,1},{2,98}... | collective-permute-start | bytes 3145736 | tf_op jit(solution)/shard_map/ppermute | solution.py:359
  102.5 11.2 %copy-start.2 = (f32[32,64,256]{2,1,0:T(8,128)}, f32[32,64,256]{2,1,0:T(8,128)S(1)}, u32[]{:S(2)}) copy-start(f32[32,64,256]{2,1,0:T(8,128)S(1)} %all-to-all-done.both) | copy-start | bytes 6291460
  102.6 25.5 %collective-permute-start.2 = (f32[32,32,256]{2,1,0:T(8,128)S(1)}, f32[32,32,256]{2,1,0:T(8,128)}, u32[]{:S(2)}, u32[]{:S(2)}) collective-permute-start(f32[32,32,256]{2,1,0:T(8,128)S(1)} %slice.19), channel_id=1, source_target_pairs={{0,96},{32,64},{64,32},{96,0},{1,97},{33,65},{65,33},{97,1},{2,98}... | collective-permute-start | bytes 3145736 | tf_op jit(solution)/shard_map/ppermute | solution.py:359
  113.7 22.5 %all-to-all-start.3 = ((f32[32,32,256]{2,1,0:T(8,128)}), f32[32,32,256]{2,1,0:T(8,128)S(1)}, u32[]{:S(2)}, u32[]{:S(2)}) async-start(f32[32,32,256]{2,1,0:T(8,128)} %correlate.3), calls=%async_computation.3 | async-start | bytes 2097152 | tf_op jit(solution)/shard_map/all_to_all | solution.py:356
  136.2 5.4 %copy-start = (s32[64,128]{1,0:T(8,128)S(1)}, s32[64,128]{1,0:T(8,128)}, u32[]{:S(2)}) copy-start(s32[64,128]{1,0:T(8,128)} %get-tuple-element.15.column) | copy-start | bytes 98308
  136.2 5.5 %copy-start.1 = (s32[64,128]{1,0:T(8,128)S(1)}, s32[64,128]{1,0:T(8,128)}, u32[]{:S(2)}) copy-start(s32[64,128]{1,0:T(8,128)} %get-tuple-element.11.column) | copy-start | bytes 98308
  136.2 22.4 %all-to-all-start.2 = ((f32[32,32,256]{2,1,0:T(8,128)}), f32[32,32,256]{2,1,0:T(8,128)S(1)}, u32[]{:S(2)}, u32[]{:S(2)}) async-start(f32[32,32,256]{2,1,0:T(8,128)} %correlate.2), calls=%async_computation.2 | async-start | bytes 2097152 | tf_op jit(solution)/shard_map/all_to_all | solution.py:356

commit v4 on v3

--- a/solution.py
+++ b/solution.py
@@ -56,20 +56,37 @@
     )(a, b, a, b)
 
 
-def gather_kernel(count, order_in, map_in, rows, out, places, packed, order, mapped, table, sems, row_sems, *, base):
+def gather_kernel(count, upper, own, other, identity, mirror, rows, out, places, *rest, base):
+    early, (packed, order, mapped, table, sems, row_sems) = rest[:-6], rest[-6:]
     width = out.shape[-1]
     per = width // 128
-    copies = [
-        pltpu.make_async_copy(map_in, mapped, sems.at[0]),
-        pltpu.make_async_copy(order_in, order, sems.at[1]),
+    here = pl.ds(base, PARTS * width)
+    lists = [
+        pltpu.make_async_copy(identity, mapped, sems.at[0]),
+        pltpu.make_async_copy(own.at[here], order, sems.at[1]),
     ]
+    other_lists = [
+        pltpu.make_async_copy(mirror, mapped, sems.at[0]),
+        pltpu.make_async_copy(other.at[here], order, sems.at[1]),
+    ]
+
+    @pl.when(upper[0] == 0)
+    def _():
+        for copy in lists:
+            copy.start()
+
+    @pl.when(upper[0] != 0)
+    def _():
+        for copy in other_lists:
+            copy.start()
+
     parts = row_sems.shape[0]
     span = LIVE // parts
     loads = []
     for p in range(parts):
         s = pl.ds(p * span, span)
         loads.append(pltpu.make_async_copy(rows.at[s, :], table.at[s, :], row_sems.at[p]))
-    for copy in copies + loads:
+    for copy in loads:
         copy.start()
     step = 2048
     first_half = lax.broadcasted_iota(jnp.int32, (8, 128), 1) < 64
@@ -89,7 +106,7 @@
             return 0
 
         lax.fori_loop(0, span // step, widen, 0)
-    for copy in copies:
+    for copy in lists:
         copy.wait()
     lane = lax.broadcasted_iota(jnp.int32, (1, 128), 1)
 
@@ -104,23 +121,27 @@
             block = k * BATCH + b
             w = b % per * 128
             live = lane + (block * 128 + base) < count[0]
-            out[block // per, :, w : w + 128] = jnp.where(live, blocks[b][:64], 0.0)
+            values = jnp.where(live, blocks[b][:64], 0.0)
+            out[block // per, :, w : w + 128] = values
+            if early and w == 0:
+                early[0][block // per] = values[32:]
             places[pl.ds(block, 1), :] = blocks[b][64:65].astype(jnp.int32)
         return 0
 
     lax.fori_loop(0, PARTS * per // BATCH, batch, 0)
 
 
-def gather(count, order, table, rows, base, width):
+def gather(lists, rows, base, width, early):
     items = PARTS * width
     return pl.pallas_call(
         functools.partial(gather_kernel, base=base),
-        in_specs=[SMEM, ANY, ANY, ANY],
-        out_specs=[VMEM, VMEM],
+        in_specs=[SMEM, SMEM, ANY, ANY, ANY, ANY, ANY],
+        out_specs=[VMEM] * (3 if early else 2),
         out_shape=[
             jax.ShapeDtypeStruct((PARTS, 64, width), F32),
             jax.ShapeDtypeStruct((items // 128, 128), jnp.int32),
-        ],
+            jax.ShapeDtypeStruct((PARTS, 32, 128), F32),
+        ][: 3 if early else 2],
         scratch_shapes=[
             pltpu.VMEM((BATCH * 128, 128), F32),
             pltpu.SMEM((items,), jnp.int32),
@@ -132,7 +153,27 @@
         compiler_params=params(),
         cost_estimate=cost(items * 2000, items * 5000),
         name="gather",
-    )(count, order, table, rows)
+    )(*lists, rows)
+
+
+def place_kernel(_, early, both, sem):
+    copy = pltpu.make_async_copy(early, both.at[:, 32:, :128], sem)
+    copy.start()
+    copy.wait()
+
+
+def place_early(both, early):
+    return pl.pallas_call(
+        place_kernel,
+        in_specs=[ANY, ANY],
+        out_specs=ANY,
+        out_shape=jax.ShapeDtypeStruct(both.shape, F32),
+        input_output_aliases={0: 0},
+        scratch_shapes=[pltpu.SemaphoreType.DMA],
+        compiler_params=params(),
+        cost_estimate=cost(1 << 20, 2 << 20),
+        name="place_early",
+    )(both, early)
 
 
 def tables():
@@ -169,9 +210,13 @@
     return both[:256, :half], both[:256, half:], both[256:, :half], both[256:, half:]
 
 
-def lesser_kernel(matrix, turn, both, spectrum):
-    for w in range(0, both.shape[-1], TILE):
-        lanes = slice(w, w + TILE)
+def lesser_kernel(matrix, turn, both_in, spectrum, both, sem):
+    load = pltpu.make_async_copy(both_in.at[:, :32, :], both, sem)
+    load.start()
+    load.wait()
+    tile = min(TILE, both.shape[-1])
+    for w in range(0, both.shape[-1], tile):
+        lanes = slice(w, w + tile)
         re0, re1 = halves(both, 0, lanes)
         im0, im1 = halves(both, 1, lanes)
         for r in range(4):
@@ -189,31 +234,45 @@
     width = both.shape[-1]
     return pl.pallas_call(
         lesser_kernel,
-        in_specs=[VMEM] * 3,
+        in_specs=[VMEM, VMEM, ANY],
         out_specs=VMEM,
         out_shape=jax.ShapeDtypeStruct((4, 2, 256, width), F32),
+        scratch_shapes=[pltpu.VMEM((PARTS, 32, width), F32), pltpu.SemaphoreType.DMA],
         compiler_params=params(),
         cost_estimate=cost(width * 2 * 4 * 512 * 768 * 2, width * 12288),
         name="lesser_spectrum",
     )(matrix, turn, both)
 
 
-def correlate_kernel(matrix, turn, spectrum, b_ref, out):
+def correlate_kernel(matrix_in, turn_in, spectrum_in, b_in, *rest, lanes):
+    result, matrix, turn, spectrum, b_ref, out, sems = rest[-7:]
+    b_lanes = slice(None) if b_in.shape[-1] == out.shape[-1] else lanes
+    loads = [
+        pltpu.make_async_copy(b_in.at[:, b_in.shape[1] - 32 :, b_lanes], b_ref, sems.at[0]),
+        pltpu.make_async_copy(matrix_in, matrix, sems.at[1]),
+        pltpu.make_async_copy(spectrum_in.at[:, :, :, lanes], spectrum, sems.at[2]),
+        pltpu.make_async_copy(turn_in, turn, sems.at[3]),
+    ]
+    for load in loads:
+        load.start()
+    for load in loads:
+        load.wait()
     scale = 1.0 / (1024.0 * math.sqrt(ENERGIES))
-    for w in range(0, b_ref.shape[-1], TILE):
-        lanes = slice(w, w + TILE)
-        re0, re1 = halves(b_ref, 0, lanes)
-        im0, im1 = halves(b_ref, 1, lanes)
+    tile = min(TILE, out.shape[-1])
+    for w in range(0, out.shape[-1], tile):
+        part = slice(w, w + tile)
+        re0, re1 = halves(b_ref, 0, part)
+        im0, im1 = halves(b_ref, 1, part)
         low_re = low_im = high_re = high_im = None
         for r in range(4):
             re = (re0 + re1, re0 - im1, re0 - re1, re0 + im1)[r]
             im = (im0 + im1, im0 + re1, im0 - im1, im0 - re1)[r]
             if r:
-                c, s = turned(turn, r, lanes)
+                c, s = turned(turn, r, part)
                 re, im = re * c - im * s, im * c + re * s
             cos_re, cos_im, sin_re, sin_im = product(matrix, re, im)
             b_re, b_im = cos_re - sin_im, cos_im + sin_re
-            a_re, a_im = spectrum[r, 0, :, lanes], spectrum[r, 1, :, lanes]
+            a_re, a_im = spectrum[r, 0, :, part], spectrum[r, 1, :, part]
             cos_re, cos_im, sin_re, sin_im = product(
                 matrix, a_re * b_re - a_im * b_im, a_re * b_im + a_im * b_re
             )
@@ -230,24 +289,38 @@
                     high_re, high_im = high_re - re, high_im - im
                 else:
                     high_re, high_im = high_re + im, high_im - re
-        shape = (16, 16, TILE)
-        out[:16, :16, lanes] = (low_im * scale).reshape(shape)
-        out[16:, :16, lanes] = (high_im * scale).reshape(shape)
-        out[:16, 16:, lanes] = (low_re * -scale).reshape(shape)
-        out[16:, 16:, lanes] = (high_re * -scale).reshape(shape)
-
-
-def correlate(matrix, turn, spectrum, b):
-    width = b.shape[-1]
-    return pl.pallas_call(
-        correlate_kernel,
-        in_specs=[VMEM] * 4,
-        out_specs=VMEM,
+        shape = (16, 16, tile)
+        out[:16, :16, part] = (low_im * scale).reshape(shape)
+        out[16:, :16, part] = (high_im * scale).reshape(shape)
+        out[:16, 16:, part] = (low_re * -scale).reshape(shape)
+        out[16:, 16:, part] = (high_re * -scale).reshape(shape)
+    save = pltpu.make_async_copy(out, result.at[:, :, lanes], sems.at[0])
+    save.start()
+    save.wait()
+
+
+def correlate(matrix, turn, spectrum, b, lanes, into=None):
+    width = spectrum.shape[-1]
+    part = lanes.stop - lanes.start
+    more = () if into is None else (into,)
+    return pl.pallas_call(
+        functools.partial(correlate_kernel, lanes=lanes),
+        in_specs=[ANY] * (4 + len(more)),
+        out_specs=ANY,
         out_shape=jax.ShapeDtypeStruct((PARTS, 32, width), F32),
+        input_output_aliases={4: 0} if more else {},
+        scratch_shapes=[
+            pltpu.VMEM(matrix.shape, BF16),
+            pltpu.VMEM(turn.shape, F32),
+            pltpu.VMEM((4, 2, 256, part), F32),
+            pltpu.VMEM((PARTS, 32, part), F32),
+            pltpu.VMEM((PARTS, 32, part), F32),
+            pltpu.SemaphoreType.DMA((4,)),
+        ],
         compiler_params=params(),
-        cost_estimate=cost(width * 2 * 4 * 512 * 768 * 4, width * 12288),
+        cost_estimate=cost(part * 2 * 4 * 512 * 768 * 4, part * 12288),
         name="correlate",
-    )(matrix, turn, spectrum, b)
+    )(matrix, turn, spectrum, b, *more)
 
 
 def scatter_rows(row_of, column, values, out, packed):
@@ -338,35 +411,38 @@
 def local(g_lesser, g_greater, live_columns, live_count, mirror):
     slabs = lax.axis_size("slab")
     across = [(s, slabs - 1 - s) for s in range(slabs)]
-    is_upper = lax.axis_index("slab") >= slabs // 2
+    upper = (lax.axis_index("slab") >= slabs // 2).astype(jnp.int32).reshape(1)
     other_mirror = lax.ppermute(mirror, "slab", across)
-    other_live = lax.ppermute(live_columns[:LIVE], "slab", across)
-    order = jnp.where(is_upper, other_live, live_columns[:LIVE])
-    table = jnp.where(is_upper, other_mirror, jnp.arange(SLOTS, dtype=jnp.int32))
+    other_live = lax.ppermute(live_columns, "slab", across)
+    identity = jnp.asarray(np.arange(SLOTS, dtype=np.int32))
+    lists = (live_count, upper, live_columns, other_live, identity, other_mirror)
     matrix, turn = tables()
     matrix, turn = jnp.asarray(matrix), jnp.asarray(turn)
-
-    rows = column_rows(g_lesser, g_greater)
-    half = WIDTHS[0]
-    orders = [order[: PARTS * half], order[PARTS * half :]]
-    picked0, columns0 = gather(live_count, orders[0], table, rows, 0, half)
-    picked1, columns1 = gather(live_count, orders[1], table, rows, PARTS * half, WIDTHS[1])
+    first, second = slice(0, 128), slice(128, 256)
 
     def swap(values):
         return lax.all_to_all(values, "energy", 0, 0, tiled=True)
 
-    def mirrored(arrived):
-        return lax.ppermute(arrived[:, 32:], "slab", across)
-
+    def cross(values):
+        return lax.ppermute(values, "slab", across)
+
+    rows = column_rows(g_lesser, g_greater)
+    picked0, columns0 = gather(lists, rows, 0, WIDTHS[0], False)
+    picked1, columns1, early = gather(lists, rows, PARTS * WIDTHS[0], WIDTHS[1], True)
+    early = cross(early)
     arrived0 = swap(picked0)
-    mirrored0 = mirrored(arrived0)
-    arrived1 = swap(picked1)
-    spectrum0 = lesser_spectrum(matrix, turn, arrived0)
-    arrived1, spectrum0 = lax.optimization_barrier((arrived1, spectrum0))
-    mirrored1 = mirrored(arrived1)
-    polar0 = swap(correlate(matrix, turn, spectrum0, mirrored0))
+    lesser0, greater0 = arrived0[:, :32], arrived0[:, 32:]
+    early, greater0 = lax.optimization_barrier((early, greater0))
+    mirrored0 = cross(greater0)
+    arrived1 = swap(place_early(picked1, early))
+    spectrum0 = lesser_spectrum(matrix, turn, lesser0)
+    result0 = correlate(matrix, turn, spectrum0, mirrored0, slice(0, 256))
+    arrived1, result0 = lax.optimization_barrier((arrived1, result0))
+    mirrored1 = cross(arrived1[:, 32:, second])
+    polar0 = swap(result0)
     spectrum1 = lesser_spectrum(matrix, turn, arrived1)
-    polar1 = swap(correlate(matrix, turn, spectrum1, mirrored1))
+    result1 = correlate(matrix, turn, spectrum1, arrived1, first)
+    polar1 = swap(correlate(matrix, turn, spectrum1, mirrored1, second, result1))
     slots = scatter(columns0, polar0, None)
     return scatter(columns1, polar1, slots)
 

time: 174 us -> 200 us (1.15)
  Pallas kernels: 96.3 us -> 117 us
  starting transfers between devices: 33.6 us -> 45.4 us
  waiting for transfers between devices: 36.4 us -> 31.9 us
    all_to_all x4, waiting for transfers between devices: 32.6 us -> 11.4 us  [swap(): return lax.all_to_all(values, 'energy', 0, 0, tiled=True)]
    pallas_call x4 -> x6, Pallas kernels: 26.7 us -> 46.8 us  [the longest x3 18.2 us: correlate(): pl.pallas_call(functools.partial(correlate_kernel, lanes=lanes), in_specs...]
    ppermute x3 -> x4, waiting for transfers between devices: 3.88 us -> 20.5 us  [the longest x3 20.5 us: cross(): return lax.ppermute(values, 'slab', across)]
    all_to_all x4, starting transfers between devices: 24.3 us -> 33.4 us  [swap(): return lax.all_to_all(values, 'energy', 0, 0, tiled=True)]
    ppermute x1, starting transfers between devices: 0.03 us -> 3.56 us  [local(): other_mirror = lax.ppermute(mirror, 'slab', across)]
    ppermute x3 -> x4, starting transfers between devices: 9.31 us -> 8.46 us  [the longest x3 8.42 us: cross(): return lax.ppermute(values, 'slab', across)]
  transfers between devices with their start and end apart: 8 -> 9, of which waited for: 4 -> 5; matrix products, arithmetic and copies ran while one was open for 2% -> 1% of each run, Pallas kernels for 38% -> 34%
where the time goes in v4:
time: 200 us
  Pallas kernels  117 us (58%)
  starting transfers between devices  45.4 us (23%)
  waiting for transfers between devices  31.9 us (16%)
  local copies, waits for them, and re-layouts  4.66 us (2%)
    pallas_call x2, Pallas kernels, gather(): pl.pallas_call(functools.partial(gather_kernel, base=base), in_specs=[SME...  33.4 us
    all_to_all x4, starting transfers between devices, swap(): return lax.all_to_all(values, 'energy', 0, 0, tiled=True)  33.4 us
    pallas_call x2, Pallas kernels, scatter(): pl.pallas_call(scatter_first_kernel if first else scatter_last_kernel, in...  28.5 us
    ppermute x3, waiting for transfers between devices, cross(): return lax.ppermute(values, 'slab', across)  20.5 us
    pallas_call x3, Pallas kernels, correlate(): pl.pallas_call(functools.partial(correlate_kernel, lanes=lanes), in_specs...  18.2 us
    pallas_call x1, Pallas kernels, place_early(): pl.pallas_call(place_kernel, in_specs=[ANY, ANY], out_specs=ANY, out_shap...  17 us
    pallas_call x2, Pallas kernels, lesser_spectrum(): pl.pallas_call(lesser_kernel, in_specs=[VMEM, VMEM, ANY], out_specs=VMEM,...  11.6 us
    all_to_all x4, waiting for transfers between devices, swap(): return lax.all_to_all(values, 'energy', 0, 0, tiled=True)  11.4 us
  transfers between devices with their start and end apart: 9, of which 5 were waited for; matrix products, arithmetic and copies ran while one was open for 1% of the time, Pallas kernels for 34%

profile of v4, /device:TPU:1, one launch (start us, length us, event | category | flops | bytes accessed | tf_op | source)
XLA Modules:
  0.0 199.7 jit_solution(4244768801875198650)
XLA Ops:
  0.0 3.6 %collective-permute-start.1 = (s32[32768]{0:T(1024)}, s32[32768]{0:T(1024)S(1)}, u32[]{:S(2)}, u32[]{:S(2)}) collective-permute-start(s32[32768]{0:T(1024)} %param.12), channel_id=1, source_target_pairs={{0,96},{32,64},{64,32},{96,0},{1,97},{33,65},{65,33},{97,1},{2,98}... | collective-permute-start | bytes 393224 | tf_op jit(solution)/shard_map/ppermute | solution.py:415
  3.6 0.0 collective-permute-start
  4.2 7.9 %column_rows.1.rows = f32[16384,128]{1,0:T(8,128)} custom-call(f32[2,16,32768]{2,1,0:T(8,128)} %a_high.1, f32[2,16,32768]{2,1,0:T(8,128)} %b_high.1, f32[2,16,32768]{2,1,0:T(8,128)} %a_high.1, f32[2,16,32768]{2,1,0:T(8,128)} %b_high.1), custom_call_target="tpu_custom_call" | custom-call | flops 1048576 | bytes 25165824 | tf_op jit(solution)/shard_map/column_rows/pallas_call | solution.py:47
  12.1 0.0 collective-permute-done.1.mirror
  12.1 0.0 copy-start.4
  12.1 0.0 collective-permute-done.other
  12.1 0.0 copy-start.5
  12.1 0.7 call_exported.0.identity
  12.9 0.0 copy-done.4
  12.9 0.0 copy-done.5
  12.9 16.6 %gather.3 = (f32[32,64,256]{2,1,0:T(8,128)}, s32[64,128]{1,0:T(8,128)}) custom-call(s32[1]{0:T(128)S(6)} %copy.13.count, s32[1]{0:T(128)} %bitcast.upper, s32[32768]{0:T(1024)} %own.3, s32[32768]{0:T(1024)} %copy-done.5, s32[32768]{0:T(1024)} %call_exported.0.identity, s32[32768]{0:T(1024)} %copy-done.4, f32[16384,128]{1,0:T(8,128)} %column_rows.1.rows), custom_call_target="tpu_custom_call" | custom-call | flops 16384000 | bytes 40960000 | tf_op jit(solution)/shard_map/gather/pallas_call | solution.py:136
  29.5 9.1 %all-to-all-start = ((f32[32,64,256]{2,1,0:T(8,128)}), f32[32,64,256]{2,1,0:T(8,128)S(1)}, u32[]{:S(2)}, u32[]{:S(2)}) async-start(f32[32,64,256]{2,1,0:T(8,128)} %get-tuple-element.17), calls=%async_computation | async-start | bytes 4194304 | tf_op jit(solution)/shard_map/all_to_all | solution.py:424
  38.6 16.8 %gather.2 = (f32[32,64,256]{2,1,0:T(8,128)}, s32[64,128]{1,0:T(8,128)}, f32[32,32,128]{2,1,0:T(8,128)}) custom-call(s32[1]{0:T(128)S(6)} %copy.13.count, s32[1]{0:T(128)} %bitcast.upper, s32[32768]{0:T(1024)} %own.3, s32[32768]{0:T(1024)} %copy-done.5, s32[32768]{0:T(1024)} %call_exported.0.identity, s32[32768]{0:T(1024)} %copy-done.4, ...), custom_call_target="tpu_custom_call" | custom-call | flops 16384000 | bytes 40960000 | tf_op jit(solution)/shard_map/gather/pallas_call | solution.py:136
  55.4 2.8 %collective-permute-start.2 = (f32[32,32,128]{2,1,0:T(8,128)}, f32[32,32,128]{2,1,0:T(8,128)S(1)}, u32[]{:S(2)}, u32[]{:S(2)}) collective-permute-start(f32[32,32,128]{2,1,0:T(8,128)} %get-tuple-element.16), channel_id=1, source_target_pairs={{0,96},{32,64},{64,32},{96,0},{1,97},{33,65},{65,33},{97,1},{2,98}... | collective-permute-start | bytes 1572872 | tf_op jit(solution)/shard_map/ppermute | solution.py:427
  58.2 8.7 %all-to-all-done = f32[32,64,256]{2,1,0:T(8,128)S(1)} async-done(((f32[32,64,256]{2,1,0:T(8,128)}), f32[32,64,256]{2,1,0:T(8,128)S(1)}, u32[]{:S(2)}, u32[]{:S(2)}) %all-to-all-start) | async-done | bytes 2097184 | tf_op jit(solution)/shard_map/all_to_all | solution.py:424
  66.9 1.5 fusion
  68.4 2.0 collective-permute-done.2.early
  70.4 0.0 copy-start.6
  70.4 0.8 copy-done.6
  71.2 17.0 %place_early.1 = f32[32,64,256]{2,1,0:T(8,128)} custom-call(f32[32,64,256]{2,1,0:T(8,128)} %get-tuple-element.15._, f32[32,32,128]{2,1,0:T(8,128)} %copy-done.6), custom_call_target="tpu_custom_call", output_to_operand_aliasing={{}: (0, {})} | custom-call | flops 1048576 | bytes 2097152 | tf_op jit(solution)/shard_map/place_early/pallas_call | solution.py:166
  88.2 0.0 copy-start.3
  88.2 8.1 %all-to-all-start.1 = ((f32[32,64,256]{2,1,0:T(8,128)}), f32[32,64,256]{2,1,0:T(8,128)S(1)}, u32[]{:S(2)}, u32[]{:S(2)}) async-start(f32[32,64,256]{2,1,0:T(8,128)} %place_early.1), calls=%async_computation.1 | async-start | bytes 4194304 | tf_op jit(solution)/shard_map/all_to_all | solution.py:424
  96.3 0.0 copy-done.3
  96.3 2.9 %collective-permute-start.3 = (f32[32,32,256]{2,1,0:T(8,128)S(1)}, f32[32,32,256]{2,1,0:T(8,128)}, u32[]{:S(2)}, u32[]{:S(2)}) collective-permute-start(f32[32,32,256]{2,1,0:T(8,128)S(1)} %copy-done.3), channel_id=1, source_target_pairs={{0,96},{32,64},{64,32},{96,0},{1,97},{33,65},{65,33},{97,1},{2,98}... | collective-permute-start | bytes 3145736 | tf_op jit(solution)/shard_map/ppermute | solution.py:427
  99.3 5.8 %lesser_spectrum.2.spectrum_in = f32[4,2,256,256]{3,2,1,0:T(8,128)} custom-call(bf16[512,768]{1,0:T(8,128)(2,1)} %constant.20.clone.matrix.matrix_in, f32[3,2,256,128]{3,2,1,0:T(8,128)} %constant.21.clone.turn.turn_in, f32[32,32,256]{2,1,0:T(8,128)} %get-tuple-element.23.both_in), custom_call_target="tpu_custom_call" | custom-call | flops 1610612736 | bytes 3145728 | tf_op jit(solution)/shard_map/lesser_spectrum/pallas_call | solution.py:235
  105.1 17.4 %collective-permute-done.3.b_in = f32[32,32,256]{2,1,0:T(8,128)} collective-permute-done((f32[32,32,256]{2,1,0:T(8,128)S(1)}, f32[32,32,256]{2,1,0:T(8,128)}, u32[]{:S(2)}, u32[]{:S(2)}) %collective-permute-start.3) | collective-permute-done | bytes 1048608 | tf_op jit(solution)/shard_map/ppermute | solution.py:427
  122.4 8.0 %correlate.3 = f32[32,32,256]{2,1,0:T(8,128)} custom-call(bf16[512,768]{1,0:T(8,128)(2,1)} %constant.20.clone.matrix.matrix_in, f32[3,2,256,128]{3,2,1,0:T(8,128)} %constant.21.clone.turn.turn_in, f32[4,2,256,256]{3,2,1,0:T(8,128)} %lesser_spectrum.2.spectrum_in, f32[32,32,256]{2,1,0:T(8,128)} %collective-permute-done.3.b_in), custom_call_target="tpu_custom_call" | custom-call | flops 3221225472 | bytes 3145728 | tf_op jit(solution)/shard_map/correlate/pallas_call | solution.py:306
  130.5 0.0 all-to-all-done.1.both_in.b_in
  130.5 0.0 copy-start.2
  130.5 8.1 %all-to-all-start.3 = ((f32[32,32,256]{2,1,0:T(8,128)}), f32[32,32,256]{2,1,0:T(8,128)S(1)}, u32[]{:S(2)}, u32[]{:S(2)}) async-start(f32[32,32,256]{2,1,0:T(8,128)} %correlate.3), calls=%async_computation.3 | async-start | bytes 2097152 | tf_op jit(solution)/shard_map/all_to_all | solution.py:424
  138.6 0.8 slice.11
  139.4 2.7 %collective-permute-start.4 = (f32[32,32,128]{2,1,0:T(8,128)}, f32[32,32,128]{2,1,0:T(8,128)S(1)}, u32[]{:S(2)}, u32[]{:S(2)}) collective-permute-start(f32[32,32,128]{2,1,0:T(8,128)} %slice.11), channel_id=1, source_target_pairs={{0,96},{32,64},{64,32},{96,0},{1,97},{33,65},{65,33},{97,1},{2,98}... | collective-permute-start | bytes 1572872 | tf_op jit(solution)/shard_map/ppermute | solution.py:427
  142.1 0.0 copy-done.2
  142.1 5.8 %lesser_spectrum.3.spectrum_in = f32[4,2,256,256]{3,2,1,0:T(8,128)} custom-call(bf16[512,768]{1,0:T(8,128)(2,1)} %constant.20.clone.matrix.matrix_in, f32[3,2,256,128]{3,2,1,0:T(8,128)} %constant.21.clone.turn.turn_in, f32[32,64,256]{2,1,0:T(8,128)} %copy-done.2), custom_call_target="tpu_custom_call" | custom-call | flops 1610612736 | bytes 3145728 | tf_op jit(solution)/shard_map/lesser_spectrum/pallas_call | solution.py:235
  147.9 5.1 %correlate.4.rest_0_ = f32[32,32,256]{2,1,0:T(8,128)} custom-call(bf16[512,768]{1,0:T(8,128)(2,1)} %constant.20.clone.matrix.matrix_in, f32[3,2,256,128]{3,2,1,0:T(8,128)} %constant.21.clone.turn.turn_in, f32[4,2,256,256]{3,2,1,0:T(8,128)} %lesser_spectrum.3.spectrum_in, f32[32,64,256]{2,1,0:T(8,128)} %copy-done.2), custom_call_target="tpu_custom_call" | custom-call | flops 1610612736 | bytes 1572864 | tf_op jit(solution)/shard_map/correlate/pallas_call | solution.py:306
  153.0 1.2 collective-permute-done.4.b_in
  154.1 0.0 copy-start.7
  154.1 0.8 copy-done.7
  154.9 5.1 %correlate.5 = f32[32,32,256]{2,1,0:T(8,128)} custom-call(bf16[512,768]{1,0:T(8,128)(2,1)} %constant.20.clone.matrix.matrix_in, f32[3,2,256,128]{3,2,1,0:T(8,128)} %constant.21.clone.turn.turn_in, f32[4,2,256,256]{3,2,1,0:T(8,128)} %lesser_spectrum.3.spectrum_in, f32[32,32,128]{2,1,0:T(8,128)} %copy-done.7, ...), custom_call_target="tpu_custom_call", output_to_operand_aliasing={{}: (4, {})} | custom-call | flops 1610612736 | bytes 1572864 | tf_op jit(solution)/shard_map/correlate/pallas_call | solution.py:306
  160.0 0.0 copy-start
  160.0 0.0 copy-start.1
  160.0 0.0 all-to-all-done.3.values
  160.0 8.1 %all-to-all-start.2 = ((f32[32,32,256]{2,1,0:T(8,128)}), f32[32,32,256]{2,1,0:T(8,128)S(1)}, u32[]{:S(2)}, u32[]{:S(2)}) async-start(f32[32,32,256]{2,1,0:T(8,128)} %correlate.5), calls=%async_computation.2 | async-start | bytes 2097152 | tf_op jit(solution)/shard_map/all_to_all | solution.py:424
  168.1 0.0 copy-done
  168.2 0.0 copy-done.1
  168.2 14.1 %scatter.2.before = f32[6,8192,128]{2,1,0:T(8,128)} custom-call(s32[8192]{0:T(1024)S(1)} %or_bitcast_fusion.row_of, s32[64,128]{1,0:T(8,128)S(1)} %copy-done, f32[32,32,256]{2,1,0:T(8,128)S(1)} %all-to-all-done.3.values), custom_call_target="tpu_custom_call" | custom-call | flops 8192000 | bytes 32768000 | tf_op jit(solution)/shard_map/scatter/pallas_call | solution.py:399
  182.3 2.7 %all-to-all-done.2.values = f32[32,32,256]{2,1,0:T(8,128)S(1)} async-done(((f32[32,32,256]{2,1,0:T(8,128)}), f32[32,32,256]{2,1,0:T(8,128)S(1)}, u32[]{:S(2)}, u32[]{:S(2)}) %all-to-all-start.2) | async-done | bytes 1048608 | tf_op jit(solution)/shard_map/all_to_all | solution.py:424
  185.0 14.4 %scatter.3 = f32[2,16,32768]{2,1,0:T(8,128)} custom-call(s32[8192]{0:T(1024)S(1)} %or_bitcast_fusion.1.row_of, s32[64,128]{1,0:T(8,128)S(1)} %copy-done.1, f32[32,32,256]{2,1,0:T(8,128)S(1)} %all-to-all-done.2.values, f32[6,8192,128]{2,1,0:T(8,128)} %scatter.2.before), custom_call_target="tpu_custom_call" | custom-call | flops 8192000 | bytes 32768000 | tf_op jit(solution)/shard_map/scatter/pallas_call | solution.py:399
  (2 shorter events, 0.0 us)
Async XLA Ops:
  0.0 12.1 %collective-permute-start.1 = (s32[32768]{0:T(1024)}, s32[32768]{0:T(1024)S(1)}, u32[]{:S(2)}, u32[]{:S(2)}) collective-permute-start(s32[32768]{0:T(1024)} %param.12), channel_id=1, source_target_pairs={{0,96},{32,64},{64,32},{96,0},{1,97},{33,65},{65,33},{97,1},{2,98}... | collective-permute-start | bytes 393224 | tf_op jit(solution)/shard_map/ppermute | solution.py:415
  3.6 8.6 %collective-permute-start = (s32[32768]{0:T(1024)}, s32[32768]{0:T(1024)S(1)}, u32[]{:S(2)}, u32[]{:S(2)}) collective-permute-start(s32[32768]{0:T(1024)} %own.3), channel_id=1, source_target_pairs={{0,96},{32,64},{64,32},{96,0},{1,97},{33,65},{65,33},{97,1},{2,98}... | collective-permute-start | bytes 393224 | tf_op jit(solution)/shard_map/ppermute | solution.py:416
  12.1 0.8 copy-start.4
  12.1 0.7 copy-start.5
  29.5 37.4 %all-to-all-start = ((f32[32,64,256]{2,1,0:T(8,128)}), f32[32,64,256]{2,1,0:T(8,128)S(1)}, u32[]{:S(2)}, u32[]{:S(2)}) async-start(f32[32,64,256]{2,1,0:T(8,128)} %get-tuple-element.17), calls=%async_computation | async-start | bytes 4194304 | tf_op jit(solution)/shard_map/all_to_all | solution.py:424
  55.4 14.9 %collective-permute-start.2 = (f32[32,32,128]{2,1,0:T(8,128)}, f32[32,32,128]{2,1,0:T(8,128)S(1)}, u32[]{:S(2)}, u32[]{:S(2)}) collective-permute-start(f32[32,32,128]{2,1,0:T(8,128)} %get-tuple-element.16), channel_id=1, source_target_pairs={{0,96},{32,64},{64,32},{96,0},{1,97},{33,65},{65,33},{97,1},{2,98}... | collective-permute-start | bytes 1572872 | tf_op jit(solution)/shard_map/ppermute | solution.py:427
  70.4 0.8 copy-start.6
  88.2 8.1 %copy-start.3 = (f32[32,32,256]{2,1,0:T(8,128)S(1)}, f32[32,32,256]{2,1,0:T(8,128)}, u32[]{:S(2)}) copy-start(f32[32,32,256]{2,1,0:T(8,128)} %get-tuple-element.19) | copy-start | bytes 3145732
  88.2 42.3 %all-to-all-start.1 = ((f32[32,64,256]{2,1,0:T(8,128)}), f32[32,64,256]{2,1,0:T(8,128)S(1)}, u32[]{:S(2)}, u32[]{:S(2)}) async-start(f32[32,64,256]{2,1,0:T(8,128)} %place_early.1), calls=%async_computation.1 | async-start | bytes 4194304 | tf_op jit(solution)/shard_map/all_to_all | solution.py:424
  96.3 26.1 %collective-permute-start.3 = (f32[32,32,256]{2,1,0:T(8,128)S(1)}, f32[32,32,256]{2,1,0:T(8,128)}, u32[]{:S(2)}, u32[]{:S(2)}) collective-permute-start(f32[32,32,256]{2,1,0:T(8,128)S(1)} %copy-done.3), channel_id=1, source_target_pairs={{0,96},{32,64},{64,32},{96,0},{1,97},{33,65},{65,33},{97,1},{2,98}... | collective-permute-start | bytes 3145736 | tf_op jit(solution)/shard_map/ppermute | solution.py:427
  130.5 11.6 %copy-start.2 = (f32[32,64,256]{2,1,0:T(8,128)}, f32[32,64,256]{2,1,0:T(8,128)S(1)}, u32[]{:S(2)}) copy-start(f32[32,64,256]{2,1,0:T(8,128)S(1)} %all-to-all-done.1.both_in.b_in) | copy-start | bytes 6291460
  130.5 29.5 %all-to-all-start.3 = ((f32[32,32,256]{2,1,0:T(8,128)}), f32[32,32,256]{2,1,0:T(8,128)S(1)}, u32[]{:S(2)}, u32[]{:S(2)}) async-start(f32[32,32,256]{2,1,0:T(8,128)} %correlate.3), calls=%async_computation.3 | async-start | bytes 2097152 | tf_op jit(solution)/shard_map/all_to_all | solution.py:424
  139.4 14.7 %collective-permute-start.4 = (f32[32,32,128]{2,1,0:T(8,128)}, f32[32,32,128]{2,1,0:T(8,128)S(1)}, u32[]{:S(2)}, u32[]{:S(2)}) collective-permute-start(f32[32,32,128]{2,1,0:T(8,128)} %slice.11), channel_id=1, source_target_pairs={{0,96},{32,64},{64,32},{96,0},{1,97},{33,65},{65,33},{97,1},{2,98}... | collective-permute-start | bytes 1572872 | tf_op jit(solution)/shard_map/ppermute | solution.py:427
  154.1 0.8 copy-start.7
  160.0 8.1 %copy-start = (s32[64,128]{1,0:T(8,128)S(1)}, s32[64,128]{1,0:T(8,128)}, u32[]{:S(2)}) copy-start(s32[64,128]{1,0:T(8,128)} %get-tuple-element.21.column) | copy-start | bytes 98308
  160.0 8.1 %copy-start.1 = (s32[64,128]{1,0:T(8,128)S(1)}, s32[64,128]{1,0:T(8,128)}, u32[]{:S(2)}) copy-start(s32[64,128]{1,0:T(8,128)} %get-tuple-element.14.column) | copy-start | bytes 98308
  160.0 25.0 %all-to-all-start.2 = ((f32[32,32,256]{2,1,0:T(8,128)}), f32[32,32,256]{2,1,0:T(8,128)S(1)}, u32[]{:S(2)}, u32[]{:S(2)}) async-start(f32[32,32,256]{2,1,0:T(8,128)} %correlate.5), calls=%async_computation.2 | async-start | bytes 2097152 | tf_op jit(solution)/shard_map/all_to_all | solution.py:424

commit v5 on v4

--- a/solution.py
+++ b/solution.py
@@ -56,8 +56,9 @@
     )(a, b, a, b)
 
 
-def gather_kernel(count, upper, own, other, identity, mirror, rows, out, places, *rest, base):
-    early, (packed, order, mapped, table, sems, row_sems) = rest[:-6], rest[-6:]
+def gather_kernel(
+    count, upper, own, other, identity, mirror, rows, out, places, packed, order, mapped, table, sems, row_sems, *, base
+):
     width = out.shape[-1]
     per = width // 128
     here = pl.ds(base, PARTS * width)
@@ -121,27 +122,23 @@
             block = k * BATCH + b
             w = b % per * 128
             live = lane + (block * 128 + base) < count[0]
-            values = jnp.where(live, blocks[b][:64], 0.0)
-            out[block // per, :, w : w + 128] = values
-            if early and w == 0:
-                early[0][block // per] = values[32:]
+            out[block // per, :, w : w + 128] = jnp.where(live, blocks[b][:64], 0.0)
             places[pl.ds(block, 1), :] = blocks[b][64:65].astype(jnp.int32)
         return 0
 
     lax.fori_loop(0, PARTS * per // BATCH, batch, 0)
 
 
-def gather(lists, rows, base, width, early):
+def gather(lists, rows, base, width):
     items = PARTS * width
     return pl.pallas_call(
         functools.partial(gather_kernel, base=base),
         in_specs=[SMEM, SMEM, ANY, ANY, ANY, ANY, ANY],
-        out_specs=[VMEM] * (3 if early else 2),
+        out_specs=[VMEM, VMEM],
         out_shape=[
             jax.ShapeDtypeStruct((PARTS, 64, width), F32),
             jax.ShapeDtypeStruct((items // 128, 128), jnp.int32),
-            jax.ShapeDtypeStruct((PARTS, 32, 128), F32),
-        ][: 3 if early else 2],
+        ],
         scratch_shapes=[
             pltpu.VMEM((BATCH * 128, 128), F32),
             pltpu.SMEM((items,), jnp.int32),
@@ -154,26 +151,6 @@
         cost_estimate=cost(items * 2000, items * 5000),
         name="gather",
     )(*lists, rows)
-
-
-def place_kernel(_, early, both, sem):
-    copy = pltpu.make_async_copy(early, both.at[:, 32:, :128], sem)
-    copy.start()
-    copy.wait()
-
-
-def place_early(both, early):
-    return pl.pallas_call(
-        place_kernel,
-        in_specs=[ANY, ANY],
-        out_specs=ANY,
-        out_shape=jax.ShapeDtypeStruct(both.shape, F32),
-        input_output_aliases={0: 0},
-        scratch_shapes=[pltpu.SemaphoreType.DMA],
-        compiler_params=params(),
-        cost_estimate=cost(1 << 20, 2 << 20),
-        name="place_early",
-    )(both, early)
 
 
 def tables():
@@ -244,19 +221,17 @@
     )(matrix, turn, both)
 
 
-def correlate_kernel(matrix_in, turn_in, spectrum_in, b_in, *rest, lanes):
-    result, matrix, turn, spectrum, b_ref, out, sems = rest[-7:]
-    b_lanes = slice(None) if b_in.shape[-1] == out.shape[-1] else lanes
+def correlate_kernel(matrix_in, turn_in, spectrum_in, b_in, out, matrix, turn, spectrum, b_ref, sems):
     loads = [
-        pltpu.make_async_copy(b_in.at[:, b_in.shape[1] - 32 :, b_lanes], b_ref, sems.at[0]),
+        pltpu.make_async_copy(b_in, b_ref, sems.at[0]),
         pltpu.make_async_copy(matrix_in, matrix, sems.at[1]),
-        pltpu.make_async_copy(spectrum_in.at[:, :, :, lanes], spectrum, sems.at[2]),
+        pltpu.make_async_copy(spectrum_in, spectrum, sems.at[2]),
         pltpu.make_async_copy(turn_in, turn, sems.at[3]),
     ]
     for load in loads:
         load.start()
-    for load in loads:
-        load.wait()
+    loads[0].wait()
+    loads[1].wait()
     scale = 1.0 / (1024.0 * math.sqrt(ENERGIES))
     tile = min(TILE, out.shape[-1])
     for w in range(0, out.shape[-1], tile):
@@ -268,10 +243,14 @@
             re = (re0 + re1, re0 - im1, re0 - re1, re0 + im1)[r]
             im = (im0 + im1, im0 + re1, im0 - im1, im0 - re1)[r]
             if r:
+                if w == 0 and r == 1:
+                    loads[3].wait()
                 c, s = turned(turn, r, part)
                 re, im = re * c - im * s, im * c + re * s
             cos_re, cos_im, sin_re, sin_im = product(matrix, re, im)
             b_re, b_im = cos_re - sin_im, cos_im + sin_re
+            if w == 0 and r == 0:
+                loads[2].wait()
             a_re, a_im = spectrum[r, 0, :, part], spectrum[r, 1, :, part]
             cos_re, cos_im, sin_re, sin_im = product(
                 matrix, a_re * b_re - a_im * b_im, a_re * b_im + a_im * b_re
@@ -294,33 +273,26 @@
         out[16:, :16, part] = (high_im * scale).reshape(shape)
         out[:16, 16:, part] = (low_re * -scale).reshape(shape)
         out[16:, 16:, part] = (high_re * -scale).reshape(shape)
-    save = pltpu.make_async_copy(out, result.at[:, :, lanes], sems.at[0])
-    save.start()
-    save.wait()
-
-
-def correlate(matrix, turn, spectrum, b, lanes, into=None):
-    width = spectrum.shape[-1]
-    part = lanes.stop - lanes.start
-    more = () if into is None else (into,)
+
+
+def correlate(matrix, turn, spectrum, b):
+    width = b.shape[-1]
     return pl.pallas_call(
-        functools.partial(correlate_kernel, lanes=lanes),
-        in_specs=[ANY] * (4 + len(more)),
-        out_specs=ANY,
+        correlate_kernel,
+        in_specs=[ANY] * 4,
+        out_specs=VMEM,
         out_shape=jax.ShapeDtypeStruct((PARTS, 32, width), F32),
-        input_output_aliases={4: 0} if more else {},
         scratch_shapes=[
             pltpu.VMEM(matrix.shape, BF16),
             pltpu.VMEM(turn.shape, F32),
-            pltpu.VMEM((4, 2, 256, part), F32),
-            pltpu.VMEM((PARTS, 32, part), F32),
-            pltpu.VMEM((PARTS, 32, part), F32),
+            pltpu.VMEM(spectrum.shape, F32),
+            pltpu.VMEM(b.shape, F32),
             pltpu.SemaphoreType.DMA((4,)),
         ],
         compiler_params=params(),
-        cost_estimate=cost(part * 2 * 4 * 512 * 768 * 4, part * 12288),
+        cost_estimate=cost(width * 2 * 4 * 512 * 768 * 4, width * 12288),
         name="correlate",
-    )(matrix, turn, spectrum, b, *more)
+    )(matrix, turn, spectrum, b)
 
 
 def scatter_rows(row_of, column, values, out, packed):
@@ -418,7 +390,6 @@
     lists = (live_count, upper, live_columns, other_live, identity, other_mirror)
     matrix, turn = tables()
     matrix, turn = jnp.asarray(matrix), jnp.asarray(turn)
-    first, second = slice(0, 128), slice(128, 256)
 
     def swap(values):
         return lax.all_to_all(values, "energy", 0, 0, tiled=True)
@@ -427,22 +398,18 @@
         return lax.ppermute(values, "slab", across)
 
     rows = column_rows(g_lesser, g_greater)
-    picked0, columns0 = gather(lists, rows, 0, WIDTHS[0], False)
-    picked1, columns1, early = gather(lists, rows, PARTS * WIDTHS[0], WIDTHS[1], True)
-    early = cross(early)
+    picked0, columns0 = gather(lists, rows, 0, WIDTHS[0])
+    picked1, columns1 = gather(lists, rows, PARTS * WIDTHS[0], WIDTHS[1])
     arrived0 = swap(picked0)
     lesser0, greater0 = arrived0[:, :32], arrived0[:, 32:]
-    early, greater0 = lax.optimization_barrier((early, greater0))
     mirrored0 = cross(greater0)
-    arrived1 = swap(place_early(picked1, early))
+    arrived1 = swap(picked1)
     spectrum0 = lesser_spectrum(matrix, turn, lesser0)
-    result0 = correlate(matrix, turn, spectrum0, mirrored0, slice(0, 256))
-    arrived1, result0 = lax.optimization_barrier((arrived1, result0))
-    mirrored1 = cross(arrived1[:, 32:, second])
-    polar0 = swap(result0)
+    arrived1, spectrum0 = lax.optimization_barrier((arrived1, spectrum0))
+    mirrored1 = cross(arrived1[:, 32:])
+    polar0 = swap(correlate(matrix, turn, spectrum0, mirrored0))
     spectrum1 = lesser_spectrum(matrix, turn, arrived1)
-    result1 = correlate(matrix, turn, spectrum1, arrived1, first)
-    polar1 = swap(correlate(matrix, turn, spectrum1, mirrored1, second, result1))
+    polar1 = swap(correlate(matrix, turn, spectrum1, mirrored1))
     slots = scatter(columns0, polar0, None)
     return scatter(columns1, polar1, slots)
 

time: 200 us -> 173 us (0.86)
  Pallas kernels: 117 us -> 97.7 us
  starting transfers between devices: 45.4 us -> 33.5 us
  waiting for transfers between devices: 31.9 us -> 36.1 us
    all_to_all x4, waiting for transfers between devices: 11.4 us -> 33.4 us  [swap(): return lax.all_to_all(values, 'energy', 0, 0, tiled=True)]
    pallas_call x4 -> x2, Pallas kernels: 35.2 us -> 16.5 us  [correlate(): pl.pallas_call(correlate_kernel, in_specs=[ANY] * 4, out_specs=VMEM, out_...]
    ppermute x3 -> x2, waiting for transfers between devices: 20.5 us -> 2.74 us  [cross(): return lax.ppermute(values, 'slab', across)]
    all_to_all x4, starting transfers between devices: 33.4 us -> 24.2 us  [swap(): return lax.all_to_all(values, 'energy', 0, 0, tiled=True)]
    ppermute x3 -> x2, starting transfers between devices: 8.42 us -> 5.73 us  [cross(): return lax.ppermute(values, 'slab', across)]
  transfers between devices with their start and end apart: 9 -> 8, of which waited for: 5 -> 5; matrix products, arithmetic and copies ran while one was open for 1% -> 1% of each run, Pallas kernels for 34% -> 39%
where the time goes in v5:
time: 173 us
  Pallas kernels  97.7 us (56%)
  waiting for transfers between devices  36.1 us (21%)
  starting transfers between devices  33.5 us (19%)
  local copies, waits for them, and re-layouts  4.18 us (2%)
    all_to_all x4, waiting for transfers between devices, swap(): return lax.all_to_all(values, 'energy', 0, 0, tiled=True)  33.4 us
    pallas_call x2, Pallas kernels, gather(): pl.pallas_call(functools.partial(gather_kernel, base=base), in_specs=[SME...  33.1 us
    pallas_call x2, Pallas kernels, scatter(): pl.pallas_call(scatter_first_kernel if first else scatter_last_kernel, in...  28.6 us
    all_to_all x4, starting transfers between devices, swap(): return lax.all_to_all(values, 'energy', 0, 0, tiled=True)  24.2 us
    pallas_call x2, Pallas kernels, correlate(): pl.pallas_call(correlate_kernel, in_specs=[ANY] * 4, out_specs=VMEM, out_...  16.5 us
    pallas_call x2, Pallas kernels, lesser_spectrum(): pl.pallas_call(lesser_kernel, in_specs=[VMEM, VMEM, ANY], out_specs=VMEM,...  11.6 us
    pallas_call x1, Pallas kernels, column_rows(): pl.pallas_call(rows_kernel, grid=(steps,), in_specs=[low, low, high, high...  7.83 us
    ppermute x2, starting transfers between devices, cross(): return lax.ppermute(values, 'slab', across)  5.73 us
  transfers between devices with their start and end apart: 8, of which 5 were waited for; matrix products, arithmetic and copies ran while one was open for 1% of the time, Pallas kernels for 39%

profile of v5, /device:TPU:1, one launch (start us, length us, event | category | flops | bytes accessed | tf_op | source)
XLA Modules:
  0.0 172.6 jit_solution(15030033428977804376)
XLA Ops:
  0.0 3.6 %collective-permute-start.1 = (s32[32768]{0:T(1024)}, s32[32768]{0:T(1024)S(1)}, u32[]{:S(2)}, u32[]{:S(2)}) collective-permute-start(s32[32768]{0:T(1024)} %param.12), channel_id=1, source_target_pairs={{0,96},{32,64},{64,32},{96,0},{1,97},{33,65},{65,33},{97,1},{2,98}... | collective-permute-start | bytes 393224 | tf_op jit(solution)/shard_map/ppermute | solution.py:387
  3.6 0.0 collective-permute-start
  4.2 7.8 %column_rows.1.rows = f32[16384,128]{1,0:T(8,128)} custom-call(f32[2,16,32768]{2,1,0:T(8,128)} %a_high.1, f32[2,16,32768]{2,1,0:T(8,128)} %b_high.1, f32[2,16,32768]{2,1,0:T(8,128)} %a_high.1, f32[2,16,32768]{2,1,0:T(8,128)} %b_high.1), custom_call_target="tpu_custom_call" | custom-call | flops 1048576 | bytes 25165824 | tf_op jit(solution)/shard_map/column_rows/pallas_call | solution.py:47
  12.1 0.0 collective-permute-done.1.mirror
  12.1 0.0 copy-start.2
  12.1 0.0 collective-permute-done.other
  12.1 0.0 copy-start.3
  12.1 0.7 call_exported.0.identity
  12.8 0.0 copy-done.2
  12.8 0.0 copy-done.3
  12.8 16.6 %gather.3 = (f32[32,64,256]{2,1,0:T(8,128)}, s32[64,128]{1,0:T(8,128)}) custom-call(s32[1]{0:T(128)S(6)} %copy.9.count, s32[1]{0:T(128)} %bitcast.upper, s32[32768]{0:T(1024)} %own.3, s32[32768]{0:T(1024)} %copy-done.3, s32[32768]{0:T(1024)} %call_exported.0.identity, s32[32768]{0:T(1024)} %copy-done.2, f32[16384,128]{1,0:T(8,128)} %column_rows.1.rows), custom_call_target="tpu_custom_call" | custom-call | flops 16384000 | bytes 40960000 | tf_op jit(solution)/shard_map/gather/pallas_call | solution.py:134
  29.5 9.1 %all-to-all-start.1 = ((f32[32,64,256]{2,1,0:T(8,128)}), f32[32,64,256]{2,1,0:T(8,128)S(1)}, u32[]{:S(2)}, u32[]{:S(2)}) async-start(f32[32,64,256]{2,1,0:T(8,128)} %get-tuple-element.13), calls=%async_computation.1 | async-start | bytes 4194304 | tf_op jit(solution)/shard_map/all_to_all | solution.py:395
  38.6 16.5 %gather.2 = (f32[32,64,256]{2,1,0:T(8,128)}, s32[64,128]{1,0:T(8,128)}) custom-call(s32[1]{0:T(128)S(6)} %copy.9.count, s32[1]{0:T(128)} %bitcast.upper, s32[32768]{0:T(1024)} %own.3, s32[32768]{0:T(1024)} %copy-done.3, s32[32768]{0:T(1024)} %call_exported.0.identity, s32[32768]{0:T(1024)} %copy-done.2, f32[16384,128]{1,0:T(8,128)} %column_rows.1.rows), custom_call_target="tpu_custom_call" | custom-call | flops 16384000 | bytes 40960000 | tf_op jit(solution)/shard_map/gather/pallas_call | solution.py:134
  55.1 11.8 %all-to-all-done.1 = f32[32,64,256]{2,1,0:T(8,128)S(1)} async-done(((f32[32,64,256]{2,1,0:T(8,128)}), f32[32,64,256]{2,1,0:T(8,128)S(1)}, u32[]{:S(2)}, u32[]{:S(2)}) %all-to-all-start.1) | async-done | bytes 2097184 | tf_op jit(solution)/shard_map/all_to_all | solution.py:395
  66.8 5.2 %all-to-all-start = ((f32[32,64,256]{2,1,0:T(8,128)}), f32[32,64,256]{2,1,0:T(8,128)}, u32[]{:S(2)}, u32[]{:S(2)}) async-start(f32[32,64,256]{2,1,0:T(8,128)} %get-tuple-element.12), calls=%async_computation | async-start | bytes 4194304 | tf_op jit(solution)/shard_map/all_to_all | solution.py:395
  72.1 1.2 fusion
  73.2 2.7 %collective-permute-start.3 = (f32[32,32,256]{2,1,0:T(8,128)S(1)}, f32[32,32,256]{2,1,0:T(8,128)S(1)}, u32[]{:S(2)}, u32[]{:S(2)}) collective-permute-start(f32[32,32,256]{2,1,0:T(8,128)S(1)} %get-tuple-element.17), channel_id=1, source_target_pairs={{0,96},{32,64},{64,32},{96,0},{1,97},{33,65},{65,33},{97,1},{2,98}... | collective-permute-start | bytes 3145736 | tf_op jit(solution)/shard_map/ppermute | solution.py:398
  76.0 5.8 %lesser_spectrum.2.spectrum_in = f32[4,2,256,256]{3,2,1,0:T(8,128)} custom-call(bf16[512,768]{1,0:T(8,128)(2,1)} %constant.20.clone.matrix.matrix_in, f32[3,2,256,128]{3,2,1,0:T(8,128)} %constant.21.clone.turn.turn_in, f32[32,32,256]{2,1,0:T(8,128)} %get-tuple-element.18.both_in), custom_call_target="tpu_custom_call" | custom-call | flops 1610612736 | bytes 3145728 | tf_op jit(solution)/shard_map/lesser_spectrum/pallas_call | solution.py:212
  81.8 18.7 %all-to-all-done.both_in = f32[32,64,256]{2,1,0:T(8,128)} async-done(((f32[32,64,256]{2,1,0:T(8,128)}), f32[32,64,256]{2,1,0:T(8,128)}, u32[]{:S(2)}, u32[]{:S(2)}) %all-to-all-start) | async-done | bytes 2097184 | tf_op jit(solution)/shard_map/all_to_all | solution.py:395
  100.5 1.3 slice.10
  101.8 3.0 %collective-permute-start.2 = (f32[32,32,256]{2,1,0:T(8,128)S(1)}, f32[32,32,256]{2,1,0:T(8,128)}, u32[]{:S(2)}, u32[]{:S(2)}) collective-permute-start(f32[32,32,256]{2,1,0:T(8,128)S(1)} %slice.10), channel_id=1, source_target_pairs={{0,96},{32,64},{64,32},{96,0},{1,97},{33,65},{65,33},{97,1},{2,98}... | collective-permute-start | bytes 3145736 | tf_op jit(solution)/shard_map/ppermute | solution.py:398
  104.8 0.0 collective-permute-done.3.b_in
  104.8 0.0 copy-start.4
  104.8 1.0 copy-done.4
  105.8 8.2 %correlate.3 = f32[32,32,256]{2,1,0:T(8,128)} custom-call(bf16[512,768]{1,0:T(8,128)(2,1)} %constant.20.clone.matrix.matrix_in, f32[3,2,256,128]{3,2,1,0:T(8,128)} %constant.21.clone.turn.turn_in, f32[4,2,256,256]{3,2,1,0:T(8,128)} %lesser_spectrum.2.spectrum_in, f32[32,32,256]{2,1,0:T(8,128)} %copy-done.4), custom_call_target="tpu_custom_call" | custom-call | flops 3221225472 | bytes 3145728 | tf_op jit(solution)/shard_map/correlate/pallas_call | solution.py:280
  114.0 4.7 %all-to-all-start.3 = ((f32[32,32,256]{2,1,0:T(8,128)}), f32[32,32,256]{2,1,0:T(8,128)S(1)}, u32[]{:S(2)}, u32[]{:S(2)}) async-start(f32[32,32,256]{2,1,0:T(8,128)} %correlate.3), calls=%async_computation.3 | async-start | bytes 2097152 | tf_op jit(solution)/shard_map/all_to_all | solution.py:395
  118.8 5.8 %lesser_spectrum.3.spectrum_in = f32[4,2,256,256]{3,2,1,0:T(8,128)} custom-call(bf16[512,768]{1,0:T(8,128)(2,1)} %constant.20.clone.matrix.matrix_in, f32[3,2,256,128]{3,2,1,0:T(8,128)} %constant.21.clone.turn.turn_in, f32[32,64,256]{2,1,0:T(8,128)} %all-to-all-done.both_in), custom_call_target="tpu_custom_call" | custom-call | flops 1610612736 | bytes 3145728 | tf_op jit(solution)/shard_map/lesser_spectrum/pallas_call | solution.py:212
  124.6 2.7 %collective-permute-done.2.b_in = f32[32,32,256]{2,1,0:T(8,128)} collective-permute-done((f32[32,32,256]{2,1,0:T(8,128)S(1)}, f32[32,32,256]{2,1,0:T(8,128)}, u32[]{:S(2)}, u32[]{:S(2)}) %collective-permute-start.2) | collective-permute-done | bytes 1048608 | tf_op jit(solution)/shard_map/ppermute | solution.py:398
  127.3 8.3 %correlate.2 = f32[32,32,256]{2,1,0:T(8,128)} custom-call(bf16[512,768]{1,0:T(8,128)(2,1)} %constant.20.clone.matrix.matrix_in, f32[3,2,256,128]{3,2,1,0:T(8,128)} %constant.21.clone.turn.turn_in, f32[4,2,256,256]{3,2,1,0:T(8,128)} %lesser_spectrum.3.spectrum_in, f32[32,32,256]{2,1,0:T(8,128)} %collective-permute-done.2.b_in), custom_call_target="tpu_custom_call" | custom-call | flops 3221225472 | bytes 3145728 | tf_op jit(solution)/shard_map/correlate/pallas_call | solution.py:280
  135.6 0.0 copy-start
  135.7 0.0 copy-start.1
  135.7 0.1 all-to-all-done.3.values
  135.8 5.2 %all-to-all-start.2 = ((f32[32,32,256]{2,1,0:T(8,128)}), f32[32,32,256]{2,1,0:T(8,128)S(1)}, u32[]{:S(2)}, u32[]{:S(2)}) async-start(f32[32,32,256]{2,1,0:T(8,128)} %correlate.2), calls=%async_computation.2 | async-start | bytes 2097152 | tf_op jit(solution)/shard_map/all_to_all | solution.py:395
  141.0 0.0 copy-done
  141.0 0.0 copy-done.1
  141.0 14.1 %scatter.2.before = f32[6,8192,128]{2,1,0:T(8,128)} custom-call(s32[8192]{0:T(1024)S(1)} %or_bitcast_fusion.row_of, s32[64,128]{1,0:T(8,128)S(1)} %copy-done, f32[32,32,256]{2,1,0:T(8,128)S(1)} %all-to-all-done.3.values), custom_call_target="tpu_custom_call" | custom-call | flops 8192000 | bytes 32768000 | tf_op jit(solution)/shard_map/scatter/pallas_call | solution.py:371
  155.2 2.8 %all-to-all-done.2.values = f32[32,32,256]{2,1,0:T(8,128)S(1)} async-done(((f32[32,32,256]{2,1,0:T(8,128)}), f32[32,32,256]{2,1,0:T(8,128)S(1)}, u32[]{:S(2)}, u32[]{:S(2)}) %all-to-all-start.2) | async-done | bytes 1048608 | tf_op jit(solution)/shard_map/all_to_all | solution.py:395
  158.0 14.4 %scatter.3 = f32[2,16,32768]{2,1,0:T(8,128)} custom-call(s32[8192]{0:T(1024)S(1)} %or_bitcast_fusion.1.row_of, s32[64,128]{1,0:T(8,128)S(1)} %copy-done.1, f32[32,32,256]{2,1,0:T(8,128)S(1)} %all-to-all-done.2.values, f32[6,8192,128]{2,1,0:T(8,128)} %scatter.2.before), custom_call_target="tpu_custom_call" | custom-call | flops 8192000 | bytes 32768000 | tf_op jit(solution)/shard_map/scatter/pallas_call | solution.py:371
  (2 shorter events, 0.0 us)
Async XLA Ops:
  0.0 12.1 %collective-permute-start.1 = (s32[32768]{0:T(1024)}, s32[32768]{0:T(1024)S(1)}, u32[]{:S(2)}, u32[]{:S(2)}) collective-permute-start(s32[32768]{0:T(1024)} %param.12), channel_id=1, source_target_pairs={{0,96},{32,64},{64,32},{96,0},{1,97},{33,65},{65,33},{97,1},{2,98}... | collective-permute-start | bytes 393224 | tf_op jit(solution)/shard_map/ppermute | solution.py:387
  3.6 8.5 %collective-permute-start = (s32[32768]{0:T(1024)}, s32[32768]{0:T(1024)S(1)}, u32[]{:S(2)}, u32[]{:S(2)}) collective-permute-start(s32[32768]{0:T(1024)} %own.3), channel_id=1, source_target_pairs={{0,96},{32,64},{64,32},{96,0},{1,97},{33,65},{65,33},{97,1},{2,98}... | collective-permute-start | bytes 393224 | tf_op jit(solution)/shard_map/ppermute | solution.py:388
  12.1 0.8 copy-start.2
  12.1 0.7 copy-start.3
  29.5 37.4 %all-to-all-start.1 = ((f32[32,64,256]{2,1,0:T(8,128)}), f32[32,64,256]{2,1,0:T(8,128)S(1)}, u32[]{:S(2)}, u32[]{:S(2)}) async-start(f32[32,64,256]{2,1,0:T(8,128)} %get-tuple-element.13), calls=%async_computation.1 | async-start | bytes 4194304 | tf_op jit(solution)/shard_map/all_to_all | solution.py:395
  66.8 33.7 %all-to-all-start = ((f32[32,64,256]{2,1,0:T(8,128)}), f32[32,64,256]{2,1,0:T(8,128)}, u32[]{:S(2)}, u32[]{:S(2)}) async-start(f32[32,64,256]{2,1,0:T(8,128)} %get-tuple-element.12), calls=%async_computation | async-start | bytes 4194304 | tf_op jit(solution)/shard_map/all_to_all | solution.py:395
  73.2 31.6 %collective-permute-start.3 = (f32[32,32,256]{2,1,0:T(8,128)S(1)}, f32[32,32,256]{2,1,0:T(8,128)S(1)}, u32[]{:S(2)}, u32[]{:S(2)}) collective-permute-start(f32[32,32,256]{2,1,0:T(8,128)S(1)} %get-tuple-element.17), channel_id=1, source_target_pairs={{0,96},{32,64},{64,32},{96,0},{1,97},{33,65},{65,33},{97,1},{2,98}... | collective-permute-start | bytes 3145736 | tf_op jit(solution)/shard_map/ppermute | solution.py:398
  101.8 25.5 %collective-permute-start.2 = (f32[32,32,256]{2,1,0:T(8,128)S(1)}, f32[32,32,256]{2,1,0:T(8,128)}, u32[]{:S(2)}, u32[]{:S(2)}) collective-permute-start(f32[32,32,256]{2,1,0:T(8,128)S(1)} %slice.10), channel_id=1, source_target_pairs={{0,96},{32,64},{64,32},{96,0},{1,97},{33,65},{65,33},{97,1},{2,98}... | collective-permute-start | bytes 3145736 | tf_op jit(solution)/shard_map/ppermute | solution.py:398
  104.8 1.0 copy-start.4
  114.0 21.7 %all-to-all-start.3 = ((f32[32,32,256]{2,1,0:T(8,128)}), f32[32,32,256]{2,1,0:T(8,128)S(1)}, u32[]{:S(2)}, u32[]{:S(2)}) async-start(f32[32,32,256]{2,1,0:T(8,128)} %correlate.3), calls=%async_computation.3 | async-start | bytes 2097152 | tf_op jit(solution)/shard_map/all_to_all | solution.py:395
  135.6 5.3 %copy-start = (s32[64,128]{1,0:T(8,128)S(1)}, s32[64,128]{1,0:T(8,128)}, u32[]{:S(2)}) copy-start(s32[64,128]{1,0:T(8,128)} %get-tuple-element.15.column) | copy-start | bytes 98308
  135.7 5.3 %copy-start.1 = (s32[64,128]{1,0:T(8,128)S(1)}, s32[64,128]{1,0:T(8,128)}, u32[]{:S(2)}) copy-start(s32[64,128]{1,0:T(8,128)} %get-tuple-element.11.column) | copy-start | bytes 98308
  135.8 22.2 %all-to-all-start.2 = ((f32[32,32,256]{2,1,0:T(8,128)}), f32[32,32,256]{2,1,0:T(8,128)S(1)}, u32[]{:S(2)}, u32[]{:S(2)}) async-start(f32[32,32,256]{2,1,0:T(8,128)} %correlate.2), calls=%async_computation.2 | async-start | bytes 2097152 | tf_op jit(solution)/shard_map/all_to_all | solution.py:395

commit v6 on v5

--- a/solution.py
+++ b/solution.py
@@ -21,7 +21,7 @@
 VMEM = pl.BlockSpec(memory_space=pltpu.VMEM)
 ANY = pl.BlockSpec(memory_space=pl.ANY)
 UNROLL = 32
-BATCH = 4
+BATCH = 8
 TILE = 256
 
 
@@ -33,7 +33,9 @@
     return pl.CostEstimate(flops=flops, bytes_accessed=bytes_accessed, transcendentals=0)
 
 
-def rows_kernel(a_low, b_low, a_high, b_high, rows):
+def rows_kernel(a_low, b_low, a_high, b_high, rows, numbers):
+    number = lax.broadcasted_iota(jnp.int32, numbers.shape, 0) * 128
+    numbers[...] = number + lax.broadcasted_iota(jnp.int32, numbers.shape, 1)
     for j in range(a_low.shape[-1] // 128):
         s = slice(j * 128, (j + 1) * 128)
         block = [ref[:, :, s].reshape(32, 128) for ref in (a_low, b_low, a_high, b_high)]
@@ -48,8 +50,14 @@
         rows_kernel,
         grid=(steps,),
         in_specs=[low, low, high, high],
-        out_specs=pl.BlockSpec((block, 128), lambda i: (i, 0)),
-        out_shape=jax.ShapeDtypeStruct((LIVE, 128), F32),
+        out_specs=[
+            pl.BlockSpec((block, 128), lambda i: (i, 0)),
+            pl.BlockSpec((SLOTS // 128, 128), lambda i: (0, 0)),
+        ],
+        out_shape=[
+            jax.ShapeDtypeStruct((LIVE, 128), F32),
+            jax.ShapeDtypeStruct((SLOTS // 128, 128), jnp.int32),
+        ],
         compiler_params=params(),
         cost_estimate=cost(1 << 20, 24 << 20),
         name="column_rows",
@@ -57,30 +65,38 @@
 
 
 def gather_kernel(
-    count, upper, own, other, identity, mirror, rows, out, places, packed, order, mapped, table, sems, row_sems, *, base
+    count, upper, own, other, identity, mirror, rows, out, places,
+    packed, list0, list1, mapped, table, map_sem, list_sems, row_sems, *, base
 ):
     width = out.shape[-1]
     per = width // 128
-    here = pl.ds(base, PARTS * width)
-    lists = [
-        pltpu.make_async_copy(identity, mapped, sems.at[0]),
-        pltpu.make_async_copy(own.at[here], order, sems.at[1]),
-    ]
-    other_lists = [
-        pltpu.make_async_copy(mirror, mapped, sems.at[0]),
-        pltpu.make_async_copy(other.at[here], order, sems.at[1]),
-    ]
+    lists = (list0, list1)
+    items = BATCH * 128
+    count_batches = PARTS * per // BATCH
+
+    def fetch(source, batch, h):
+        piece = pl.ds(pl.multiple_of(base + batch * items, items), items)
+        return pltpu.make_async_copy(source.at[piece], lists[h], list_sems.at[h])
+
+    def start(batch, h):
+        @pl.when(upper[0] == 0)
+        def _():
+            fetch(own, batch, h).start()
+
+        @pl.when(upper[0] != 0)
+        def _():
+            fetch(other, batch, h).start()
 
     @pl.when(upper[0] == 0)
     def _():
-        for copy in lists:
-            copy.start()
+        pltpu.make_async_copy(identity, mapped, map_sem).start()
 
     @pl.when(upper[0] != 0)
     def _():
-        for copy in other_lists:
-            copy.start()
-
+        pltpu.make_async_copy(mirror, mapped, map_sem).start()
+
+    start(0, 0)
+    start(1, 1)
     parts = row_sems.shape[0]
     span = LIVE // parts
     loads = []
@@ -107,26 +123,32 @@
             return 0
 
         lax.fori_loop(0, span // step, widen, 0)
-    for copy in lists:
-        copy.wait()
+    pltpu.make_async_copy(identity, mapped, map_sem).wait()
     lane = lax.broadcasted_iota(jnp.int32, (1, 128), 1)
 
-    def batch(k, _):
-        for r in range(0, BATCH * 128, UNROLL):
-            first = pl.multiple_of(k * (BATCH * 128) + r, UNROLL)
-            cols = [mapped[order[first + u]] for u in range(UNROLL)]
-            for u in range(UNROLL):
-                packed[r + u : r + u + 1, :] = table[pl.ds(cols[u], 1), :]
-        blocks = [packed[b * 128 : (b + 1) * 128, :].T for b in range(BATCH)]
-        for b in range(BATCH):
-            block = k * BATCH + b
-            w = b % per * 128
-            live = lane + (block * 128 + base) < count[0]
-            out[block // per, :, w : w + 128] = jnp.where(live, blocks[b][:64], 0.0)
-            places[pl.ds(block, 1), :] = blocks[b][64:65].astype(jnp.int32)
+    def pair(k, _):
+        for h in range(2):
+            batch = 2 * k + h
+            fetch(own, batch, h).wait()
+            for r in range(0, items, UNROLL):
+                cols = [mapped[lists[h][r + u]] for u in range(UNROLL)]
+                for u in range(UNROLL):
+                    packed[r + u : r + u + 1, :] = table[pl.ds(cols[u], 1), :]
+
+            @pl.when(batch + 2 < count_batches)
+            def _():
+                start(batch + 2, h)
+
+            blocks = [packed[b * 128 : (b + 1) * 128, :].T for b in range(BATCH)]
+            for b in range(BATCH):
+                block = batch * BATCH + b
+                w = b % per * 128
+                live = lane + (block * 128 + base) < count[0]
+                out[block // per, :, w : w + 128] = jnp.where(live, blocks[b][:64], 0.0)
+                places[pl.ds(block, 1), :] = blocks[b][64:65].astype(jnp.int32)
         return 0
 
-    lax.fori_loop(0, PARTS * per // BATCH, batch, 0)
+    lax.fori_loop(0, count_batches // 2, pair, 0)
 
 
 def gather(lists, rows, base, width):
@@ -141,9 +163,11 @@
         ],
         scratch_shapes=[
             pltpu.VMEM((BATCH * 128, 128), F32),
-            pltpu.SMEM((items,), jnp.int32),
+            pltpu.SMEM((BATCH * 128,), jnp.int32),
+            pltpu.SMEM((BATCH * 128,), jnp.int32),
             pltpu.SMEM((SLOTS,), jnp.int32),
             pltpu.VMEM((SLOTS, 128), F32),
+            pltpu.SemaphoreType.DMA,
             pltpu.SemaphoreType.DMA((2,)),
             pltpu.SemaphoreType.DMA((4,)),
         ],
@@ -222,16 +246,20 @@
 
 
 def correlate_kernel(matrix_in, turn_in, spectrum_in, b_in, out, matrix, turn, spectrum, b_ref, sems):
-    loads = [
+    first = [
         pltpu.make_async_copy(b_in, b_ref, sems.at[0]),
         pltpu.make_async_copy(matrix_in, matrix, sems.at[1]),
-        pltpu.make_async_copy(spectrum_in, spectrum, sems.at[2]),
-        pltpu.make_async_copy(turn_in, turn, sems.at[3]),
     ]
-    for load in loads:
+    loads = [pltpu.make_async_copy(spectrum_in.at[r], spectrum.at[r], sems.at[3 + r]) for r in range(4)]
+    angles = pltpu.make_async_copy(turn_in, turn, sems.at[2])
+    for load in first:
         load.start()
-    loads[0].wait()
-    loads[1].wait()
+    for load in first:
+        load.wait()
+    loads[0].start()
+    angles.start()
+    for load in loads[1:]:
+        load.start()
     scale = 1.0 / (1024.0 * math.sqrt(ENERGIES))
     tile = min(TILE, out.shape[-1])
     for w in range(0, out.shape[-1], tile):
@@ -244,13 +272,13 @@
             im = (im0 + im1, im0 + re1, im0 - im1, im0 - re1)[r]
             if r:
                 if w == 0 and r == 1:
-                    loads[3].wait()
+                    angles.wait()
                 c, s = turned(turn, r, part)
                 re, im = re * c - im * s, im * c + re * s
             cos_re, cos_im, sin_re, sin_im = product(matrix, re, im)
             b_re, b_im = cos_re - sin_im, cos_im + sin_re
-            if w == 0 and r == 0:
-                loads[2].wait()
+            if w == 0:
+                loads[r].wait()
             a_re, a_im = spectrum[r, 0, :, part], spectrum[r, 1, :, part]
             cos_re, cos_im, sin_re, sin_im = product(
                 matrix, a_re * b_re - a_im * b_im, a_re * b_im + a_im * b_re
@@ -287,7 +315,7 @@
             pltpu.VMEM(turn.shape, F32),
             pltpu.VMEM(spectrum.shape, F32),
             pltpu.VMEM(b.shape, F32),
-            pltpu.SemaphoreType.DMA((4,)),
+            pltpu.SemaphoreType.DMA((7,)),
         ],
         compiler_params=params(),
         cost_estimate=cost(width * 2 * 4 * 512 * 768 * 4, width * 12288),
@@ -295,43 +323,61 @@
     )(matrix, turn, spectrum, b)
 
 
-def scatter_rows(row_of, column, values, out, packed):
+def scatter_rows(row_of, column, values, out, packed, lists, list_sems):
     per = values.shape[-1] // 128
-
-    def batch(k, _):
-        blocks = []
-        for b in range(BATCH):
-            block = k * BATCH + b
-            w = b % per * 128
-            group = (column[pl.ds(block, 1), :] >> 7) & 3
-            data = values[block // per, :, w : w + 128]
-            blocks.append(jnp.concatenate([jnp.where(group == g, data, 0.0) for g in range(4)], 0).T)
-        for b in range(BATCH):
-            packed[b * 128 : (b + 1) * 128, :] = blocks[b]
-        for r in range(0, BATCH * 128, UNROLL):
-            first = pl.multiple_of(k * (BATCH * 128) + r, UNROLL)
-            rows = [row_of[first + u] for u in range(UNROLL)]
-            for u in range(UNROLL):
-                row = packed[r + u : r + u + 1, :]
-                pltpu.store(out.at[pl.ds(rows[u], 1), :], row, mask=row != 0.0)
+    items = BATCH * 128
+    count = PARTS * per // BATCH
+
+    def fetch(batch, h):
+        piece = pl.ds(pl.multiple_of(batch * items, items), items)
+        return pltpu.make_async_copy(row_of.at[piece], lists[h], list_sems.at[h])
+
+    fetch(0, 0).start()
+    fetch(1, 1).start()
+
+    def pair(k, _):
+        for h in range(2):
+            batch = 2 * k + h
+            blocks = []
+            for b in range(BATCH):
+                block = batch * BATCH + b
+                w = b % per * 128
+                group = (column[pl.ds(block, 1), :] >> 7) & 3
+                data = values[block // per, :, w : w + 128]
+                blocks.append(jnp.concatenate([jnp.where(group == g, data, 0.0) for g in range(4)], 0).T)
+            for b in range(BATCH):
+                packed[b * 128 : (b + 1) * 128, :] = blocks[b]
+            fetch(batch, h).wait()
+            for r in range(0, items, UNROLL):
+                rows = [lists[h][r + u] for u in range(UNROLL)]
+                for u in range(UNROLL):
+                    row = packed[r + u : r + u + 1, :]
+                    pltpu.store(out.at[pl.ds(rows[u], 1), :], row, mask=row != 0.0)
+
+            @pl.when(batch + 2 < count)
+            def _():
+                fetch(batch + 2, h).start()
+
         return 0
 
-    lax.fori_loop(0, PARTS * per // BATCH, batch, 0)
-
-
-def scatter_first_kernel(row_of, column, values, out, packed, slots, sem):
+    lax.fori_loop(0, count // 2, pair, 0)
+
+
+def scatter_first_kernel(row_of, column, values, out, packed, list0, list1, list_sems, slots, sem):
     slots[...] = jnp.zeros_like(slots)
-    scatter_rows(row_of, column, values, slots, packed)
+    scatter_rows(row_of, column, values, slots, packed, (list0, list1), list_sems)
     save = pltpu.make_async_copy(slots, out.at[0], sem)
     save.start()
     save.wait()
 
 
-def scatter_last_kernel(row_of, column, values, before, out, packed, slots, earlier, staged, in_sem, out_sem):
+def scatter_last_kernel(
+    row_of, column, values, before, out, packed, list0, list1, list_sems, slots, earlier, staged, in_sem, out_sem
+):
     load = pltpu.make_async_copy(before.at[0], earlier, in_sem)
     load.start()
     slots[...] = jnp.zeros_like(slots)
-    scatter_rows(row_of, column, values, slots, packed)
+    scatter_rows(row_of, column, values, slots, packed, (list0, list1), list_sems)
     load.wait()
     pieces = out_sem.shape[0]
     span = SLOTS // pieces
@@ -357,6 +403,9 @@
     first = before is None
     scratch = [
         pltpu.VMEM((BATCH * 128, 128), F32),
+        pltpu.SMEM((BATCH * 128,), jnp.int32),
+        pltpu.SMEM((BATCH * 128,), jnp.int32),
+        pltpu.SemaphoreType.DMA((2,)),
         pltpu.VMEM((SLOTS // 4, 128), F32),
     ]
     if first:
@@ -370,7 +419,7 @@
         ]
     return pl.pallas_call(
         scatter_first_kernel if first else scatter_last_kernel,
-        in_specs=[SMEM, VMEM, VMEM] + ([] if first else [ANY]),
+        in_specs=[ANY, VMEM, VMEM] + ([] if first else [ANY]),
         out_specs=ANY,
         out_shape=jax.ShapeDtypeStruct((6, SLOTS // 4, 128) if first else (2, 16, SLOTS), F32),
         scratch_shapes=scratch,
@@ -386,7 +435,8 @@
     upper = (lax.axis_index("slab") >= slabs // 2).astype(jnp.int32).reshape(1)
     other_mirror = lax.ppermute(mirror, "slab", across)
     other_live = lax.ppermute(live_columns, "slab", across)
-    identity = jnp.asarray(np.arange(SLOTS, dtype=np.int32))
+    rows, identity = column_rows(g_lesser, g_greater)
+    identity = identity.reshape(SLOTS)
     lists = (live_count, upper, live_columns, other_live, identity, other_mirror)
     matrix, turn = tables()
     matrix, turn = jnp.asarray(matrix), jnp.asarray(turn)
@@ -397,7 +447,6 @@
     def cross(values):
         return lax.ppermute(values, "slab", across)
 
-    rows = column_rows(g_lesser, g_greater)
     picked0, columns0 = gather(lists, rows, 0, WIDTHS[0])
     picked1, columns1 = gather(lists, rows, PARTS * WIDTHS[0], WIDTHS[1])
     arrived0 = swap(picked0)

time: 173 us -> 168 us (0.971)
  Pallas kernels: 97.7 us -> 86.4 us
  waiting for transfers between devices: 36.1 us -> 41.7 us
    pallas_call x2, Pallas kernels: 28.6 us -> 18.2 us  [scatter(): pl.pallas_call(scatter_first_kernel if first else scatter_last_kernel, in...]
    all_to_all x4, waiting for transfers between devices: 33.4 us -> 39.6 us  [swap(): return lax.all_to_all(values, 'energy', 0, 0, tiled=True)]
    pallas_call x2, Pallas kernels: 33.1 us -> 31 us  [gather(): pl.pallas_call(functools.partial(gather_kernel, base=base), in_specs=[SME...]
  transfers between devices with their start and end apart: 8 -> 8, of which waited for: 5 -> 5; matrix products, arithmetic and copies ran while one was open for 1% -> 1% of each run, Pallas kernels for 39% -> 37%
where the time goes in v6:
time: 168 us; the launch traced here: 167 us
  Pallas kernels  86.4 us (51%)
  waiting for transfers between devices  41.7 us (25%)
  starting transfers between devices  33.7 us (20%)
  local copies, waits for them, and re-layouts  4.16 us (2%)
    all_to_all x4, waiting for transfers between devices, swap(): return lax.all_to_all(values, 'energy', 0, 0, tiled=True)  39.6 us
    pallas_call x2, Pallas kernels, gather(): pl.pallas_call(functools.partial(gather_kernel, base=base), in_specs=[SME...  31 us
    all_to_all x4, starting transfers between devices, swap(): return lax.all_to_all(values, 'energy', 0, 0, tiled=True)  24.3 us
    pallas_call x2, Pallas kernels, scatter(): pl.pallas_call(scatter_first_kernel if first else scatter_last_kernel, in...  18.2 us
    pallas_call x2, Pallas kernels, correlate(): pl.pallas_call(correlate_kernel, in_specs=[ANY] * 4, out_specs=VMEM, out_...  17.8 us
    pallas_call x2, Pallas kernels, lesser_spectrum(): pl.pallas_call(lesser_kernel, in_specs=[VMEM, VMEM, ANY], out_specs=VMEM,...  11.6 us
    pallas_call x1, Pallas kernels, column_rows(): pl.pallas_call(rows_kernel, grid=(steps,), in_specs=[low, low, high, high...  7.84 us
    ppermute x2, starting transfers between devices, cross(): return lax.ppermute(values, 'slab', across)  5.72 us
  transfers between devices with their start and end apart: 8, of which 5 were waited for; matrix products, arithmetic and copies ran while one was open for 1% of the time, Pallas kernels for 37%

profile of v6, /device:TPU:1, one launch (start us, length us, event | category | flops | bytes accessed | tf_op | source)
XLA Modules:
  0.0 167.0 jit_solution(4105283380283251850)
XLA Ops:
  0.0 3.6 %collective-permute-start.1 = (s32[32768]{0:T(1024)}, s32[32768]{0:T(1024)S(1)}, u32[]{:S(2)}, u32[]{:S(2)}) collective-permute-start(s32[32768]{0:T(1024)} %param.11), channel_id=1, source_target_pairs={{0,96},{32,64},{64,32},{96,0},{1,97},{33,65},{65,33},{97,1},{2,98}... | collective-permute-start | bytes 393224 | tf_op jit(solution)/shard_map/ppermute | solution.py:436
  3.6 0.0 collective-permute-start
  4.2 7.8 %column_rows.1 = (f32[16384,128]{1,0:T(8,128)}, s32[256,128]{1,0:T(8,128)}) custom-call(f32[2,16,32768]{2,1,0:T(8,128)} %a_high.1, f32[2,16,32768]{2,1,0:T(8,128)} %b_high.1, f32[2,16,32768]{2,1,0:T(8,128)} %a_high.1, f32[2,16,32768]{2,1,0:T(8,128)} %b_high.1), custom_call_target="tpu_custom_call" | custom-call | flops 1048576 | bytes 25165824 | tf_op jit(solution)/shard_map/column_rows/pallas_call | solution.py:49
  12.1 0.0 collective-permute-done.1.mirror
  12.1 0.0 copy-start.2
  12.1 0.0 collective-permute-done.other
  12.1 0.0 copy-start.3
  12.1 0.6 copy-done.2
  12.7 0.1 copy-done.3
  12.8 15.5 %gather.3 = (f32[32,64,256]{2,1,0:T(8,128)}, s32[64,128]{1,0:T(8,128)}) custom-call(s32[1]{0:T(128)S(6)} %copy.8.count, s32[1]{0:T(128)} %bitcast.upper, s32[32768]{0:T(1024)} %own.3, s32[32768]{0:T(1024)} %copy-done.3, s32[32768]{0:T(1024)} %bitcast.6, s32[32768]{0:T(1024)} %copy-done.2, f32[16384,128]{1,0:T(8,128)} %get-tuple-element.14.rows), custom_call_target="tpu_custom_call" | custom-call | flops 16384000 | bytes 40960000 | tf_op jit(solution)/shard_map/gather/pallas_call | solution.py:156
  28.4 9.1 %all-to-all-start.1 = ((f32[32,64,256]{2,1,0:T(8,128)}), f32[32,64,256]{2,1,0:T(8,128)S(1)}, u32[]{:S(2)}, u32[]{:S(2)}) async-start(f32[32,64,256]{2,1,0:T(8,128)} %get-tuple-element.17), calls=%async_computation.1 | async-start | bytes 4194304 | tf_op jit(solution)/shard_map/all_to_all | solution.py:445
  37.4 15.5 %gather.2 = (f32[32,64,256]{2,1,0:T(8,128)}, s32[64,128]{1,0:T(8,128)}) custom-call(s32[1]{0:T(128)S(6)} %copy.8.count, s32[1]{0:T(128)} %bitcast.upper, s32[32768]{0:T(1024)} %own.3, s32[32768]{0:T(1024)} %copy-done.3, s32[32768]{0:T(1024)} %bitcast.7, s32[32768]{0:T(1024)} %copy-done.2, f32[16384,128]{1,0:T(8,128)} %get-tuple-element.14.rows), custom_call_target="tpu_custom_call" | custom-call | flops 16384000 | bytes 40960000 | tf_op jit(solution)/shard_map/gather/pallas_call | solution.py:156
  52.9 12.8 %all-to-all-done.1 = f32[32,64,256]{2,1,0:T(8,128)S(1)} async-done(((f32[32,64,256]{2,1,0:T(8,128)}), f32[32,64,256]{2,1,0:T(8,128)S(1)}, u32[]{:S(2)}, u32[]{:S(2)}) %all-to-all-start.1) | async-done | bytes 2097184 | tf_op jit(solution)/shard_map/all_to_all | solution.py:445
  65.7 5.2 %all-to-all-start = ((f32[32,64,256]{2,1,0:T(8,128)}), f32[32,64,256]{2,1,0:T(8,128)}, u32[]{:S(2)}, u32[]{:S(2)}) async-start(f32[32,64,256]{2,1,0:T(8,128)} %get-tuple-element.16), calls=%async_computation | async-start | bytes 4194304 | tf_op jit(solution)/shard_map/all_to_all | solution.py:445
  70.9 1.2 fusion
  72.1 2.7 %collective-permute-start.3 = (f32[32,32,256]{2,1,0:T(8,128)S(1)}, f32[32,32,256]{2,1,0:T(8,128)S(1)}, u32[]{:S(2)}, u32[]{:S(2)}) collective-permute-start(f32[32,32,256]{2,1,0:T(8,128)S(1)} %get-tuple-element.21), channel_id=1, source_target_pairs={{0,96},{32,64},{64,32},{96,0},{1,97},{33,65},{65,33},{97,1},{2,98}... | collective-permute-start | bytes 3145736 | tf_op jit(solution)/shard_map/ppermute | solution.py:448
  74.9 5.8 %lesser_spectrum.2.spectrum_in = f32[4,2,256,256]{3,2,1,0:T(8,128)} custom-call(bf16[512,768]{1,0:T(8,128)(2,1)} %constant.18.clone.matrix.matrix_in, f32[3,2,256,128]{3,2,1,0:T(8,128)} %constant.19.clone.turn.turn_in, f32[32,32,256]{2,1,0:T(8,128)} %get-tuple-element.22.both_in), custom_call_target="tpu_custom_call" | custom-call | flops 1610612736 | bytes 3145728 | tf_op jit(solution)/shard_map/lesser_spectrum/pallas_call | solution.py:236
  80.7 18.7 %all-to-all-done.both_in = f32[32,64,256]{2,1,0:T(8,128)} async-done(((f32[32,64,256]{2,1,0:T(8,128)}), f32[32,64,256]{2,1,0:T(8,128)}, u32[]{:S(2)}, u32[]{:S(2)}) %all-to-all-start) | async-done | bytes 2097184 | tf_op jit(solution)/shard_map/all_to_all | solution.py:445
  99.4 1.3 slice.10
  100.7 3.0 %collective-permute-start.2 = (f32[32,32,256]{2,1,0:T(8,128)S(1)}, f32[32,32,256]{2,1,0:T(8,128)}, u32[]{:S(2)}, u32[]{:S(2)}) collective-permute-start(f32[32,32,256]{2,1,0:T(8,128)S(1)} %slice.10), channel_id=1, source_target_pairs={{0,96},{32,64},{64,32},{96,0},{1,97},{33,65},{65,33},{97,1},{2,98}... | collective-permute-start | bytes 3145736 | tf_op jit(solution)/shard_map/ppermute | solution.py:448
  103.7 0.0 collective-permute-done.3.b_in
  103.7 0.0 copy-start.4
  103.7 1.0 copy-done.4
  104.6 8.9 %correlate.3 = f32[32,32,256]{2,1,0:T(8,128)} custom-call(bf16[512,768]{1,0:T(8,128)(2,1)} %constant.18.clone.matrix.matrix_in, f32[3,2,256,128]{3,2,1,0:T(8,128)} %constant.19.clone.turn.turn_in, f32[4,2,256,256]{3,2,1,0:T(8,128)} %lesser_spectrum.2.spectrum_in, f32[32,32,256]{2,1,0:T(8,128)} %copy-done.4), custom_call_target="tpu_custom_call" | custom-call | flops 3221225472 | bytes 3145728 | tf_op jit(solution)/shard_map/correlate/pallas_call | solution.py:308
  113.5 4.7 %all-to-all-start.3 = ((f32[32,32,256]{2,1,0:T(8,128)}), f32[32,32,256]{2,1,0:T(8,128)S(1)}, u32[]{:S(2)}, u32[]{:S(2)}) async-start(f32[32,32,256]{2,1,0:T(8,128)} %correlate.3), calls=%async_computation.3 | async-start | bytes 2097152 | tf_op jit(solution)/shard_map/all_to_all | solution.py:445
  118.3 5.8 %lesser_spectrum.3.spectrum_in = f32[4,2,256,256]{3,2,1,0:T(8,128)} custom-call(bf16[512,768]{1,0:T(8,128)(2,1)} %constant.18.clone.matrix.matrix_in, f32[3,2,256,128]{3,2,1,0:T(8,128)} %constant.19.clone.turn.turn_in, f32[32,64,256]{2,1,0:T(8,128)} %all-to-all-done.both_in), custom_call_target="tpu_custom_call" | custom-call | flops 1610612736 | bytes 3145728 | tf_op jit(solution)/shard_map/lesser_spectrum/pallas_call | solution.py:236
  124.1 2.1 %collective-permute-done.2.b_in = f32[32,32,256]{2,1,0:T(8,128)} collective-permute-done((f32[32,32,256]{2,1,0:T(8,128)S(1)}, f32[32,32,256]{2,1,0:T(8,128)}, u32[]{:S(2)}, u32[]{:S(2)}) %collective-permute-start.2) | collective-permute-done | bytes 1048608 | tf_op jit(solution)/shard_map/ppermute | solution.py:448
  126.2 8.9 %correlate.2 = f32[32,32,256]{2,1,0:T(8,128)} custom-call(bf16[512,768]{1,0:T(8,128)(2,1)} %constant.18.clone.matrix.matrix_in, f32[3,2,256,128]{3,2,1,0:T(8,128)} %constant.19.clone.turn.turn_in, f32[4,2,256,256]{3,2,1,0:T(8,128)} %lesser_spectrum.3.spectrum_in, f32[32,32,256]{2,1,0:T(8,128)} %collective-permute-done.2.b_in), custom_call_target="tpu_custom_call" | custom-call | flops 3221225472 | bytes 3145728 | tf_op jit(solution)/shard_map/correlate/pallas_call | solution.py:308
  135.1 0.0 copy-start
  135.2 0.0 copy-start.1
  135.2 0.1 all-to-all-done.3.values
  135.3 5.3 %all-to-all-start.2 = ((f32[32,32,256]{2,1,0:T(8,128)}), f32[32,32,256]{2,1,0:T(8,128)S(1)}, u32[]{:S(2)}, u32[]{:S(2)}) async-start(f32[32,32,256]{2,1,0:T(8,128)} %correlate.2), calls=%async_computation.2 | async-start | bytes 2097152 | tf_op jit(solution)/shard_map/all_to_all | solution.py:445
  140.6 0.0 copy-done
  140.6 0.0 copy-done.1
  140.7 8.9 %scatter.2.before = f32[6,8192,128]{2,1,0:T(8,128)} custom-call(s32[8192]{0:T(1024)S(1)} %or_bitcast_fusion.row_of, s32[64,128]{1,0:T(8,128)S(1)} %copy-done, f32[32,32,256]{2,1,0:T(8,128)S(1)} %all-to-all-done.3.values), custom_call_target="tpu_custom_call" | custom-call | flops 8192000 | bytes 32768000 | tf_op jit(solution)/shard_map/scatter/pallas_call | solution.py:420
  149.6 7.9 %all-to-all-done.2.values = f32[32,32,256]{2,1,0:T(8,128)S(1)} async-done(((f32[32,32,256]{2,1,0:T(8,128)}), f32[32,32,256]{2,1,0:T(8,128)S(1)}, u32[]{:S(2)}, u32[]{:S(2)}) %all-to-all-start.2) | async-done | bytes 1048608 | tf_op jit(solution)/shard_map/all_to_all | solution.py:445
  157.5 9.3 %scatter.3 = f32[2,16,32768]{2,1,0:T(8,128)} custom-call(s32[8192]{0:T(1024)S(1)} %or_bitcast_fusion.1.row_of, s32[64,128]{1,0:T(8,128)S(1)} %copy-done.1, f32[32,32,256]{2,1,0:T(8,128)S(1)} %all-to-all-done.2.values, f32[6,8192,128]{2,1,0:T(8,128)} %scatter.2.before), custom_call_target="tpu_custom_call" | custom-call | flops 8192000 | bytes 32768000 | tf_op jit(solution)/shard_map/scatter/pallas_call | solution.py:420
  (2 shorter events, 0.0 us)
Async XLA Ops:
  0.0 12.1 %collective-permute-start.1 = (s32[32768]{0:T(1024)}, s32[32768]{0:T(1024)S(1)}, u32[]{:S(2)}, u32[]{:S(2)}) collective-permute-start(s32[32768]{0:T(1024)} %param.11), channel_id=1, source_target_pairs={{0,96},{32,64},{64,32},{96,0},{1,97},{33,65},{65,33},{97,1},{2,98}... | collective-permute-start | bytes 393224 | tf_op jit(solution)/shard_map/ppermute | solution.py:436
  3.6 8.5 %collective-permute-start = (s32[32768]{0:T(1024)}, s32[32768]{0:T(1024)S(1)}, u32[]{:S(2)}, u32[]{:S(2)}) collective-permute-start(s32[32768]{0:T(1024)} %own.3), channel_id=1, source_target_pairs={{0,96},{32,64},{64,32},{96,0},{1,97},{33,65},{65,33},{97,1},{2,98}... | collective-permute-start | bytes 393224 | tf_op jit(solution)/shard_map/ppermute | solution.py:437
  12.1 0.7 copy-start.2
  12.1 0.7 copy-start.3
  28.4 37.4 %all-to-all-start.1 = ((f32[32,64,256]{2,1,0:T(8,128)}), f32[32,64,256]{2,1,0:T(8,128)S(1)}, u32[]{:S(2)}, u32[]{:S(2)}) async-start(f32[32,64,256]{2,1,0:T(8,128)} %get-tuple-element.17), calls=%async_computation.1 | async-start | bytes 4194304 | tf_op jit(solution)/shard_map/all_to_all | solution.py:445
  65.7 33.6 %all-to-all-start = ((f32[32,64,256]{2,1,0:T(8,128)}), f32[32,64,256]{2,1,0:T(8,128)}, u32[]{:S(2)}, u32[]{:S(2)}) async-start(f32[32,64,256]{2,1,0:T(8,128)} %get-tuple-element.16), calls=%async_computation | async-start | bytes 4194304 | tf_op jit(solution)/shard_map/all_to_all | solution.py:445
  72.1 31.6 %collective-permute-start.3 = (f32[32,32,256]{2,1,0:T(8,128)S(1)}, f32[32,32,256]{2,1,0:T(8,128)S(1)}, u32[]{:S(2)}, u32[]{:S(2)}) collective-permute-start(f32[32,32,256]{2,1,0:T(8,128)S(1)} %get-tuple-element.21), channel_id=1, source_target_pairs={{0,96},{32,64},{64,32},{96,0},{1,97},{33,65},{65,33},{97,1},{2,98}... | collective-permute-start | bytes 3145736 | tf_op jit(solution)/shard_map/ppermute | solution.py:448
  100.7 25.5 %collective-permute-start.2 = (f32[32,32,256]{2,1,0:T(8,128)S(1)}, f32[32,32,256]{2,1,0:T(8,128)}, u32[]{:S(2)}, u32[]{:S(2)}) collective-permute-start(f32[32,32,256]{2,1,0:T(8,128)S(1)} %slice.10), channel_id=1, source_target_pairs={{0,96},{32,64},{64,32},{96,0},{1,97},{33,65},{65,33},{97,1},{2,98}... | collective-permute-start | bytes 3145736 | tf_op jit(solution)/shard_map/ppermute | solution.py:448
  103.7 1.0 copy-start.4
  113.5 21.7 %all-to-all-start.3 = ((f32[32,32,256]{2,1,0:T(8,128)}), f32[32,32,256]{2,1,0:T(8,128)S(1)}, u32[]{:S(2)}, u32[]{:S(2)}) async-start(f32[32,32,256]{2,1,0:T(8,128)} %correlate.3), calls=%async_computation.3 | async-start | bytes 2097152 | tf_op jit(solution)/shard_map/all_to_all | solution.py:445
  135.1 5.5 %copy-start = (s32[64,128]{1,0:T(8,128)S(1)}, s32[64,128]{1,0:T(8,128)}, u32[]{:S(2)}) copy-start(s32[64,128]{1,0:T(8,128)} %get-tuple-element.19.column) | copy-start | bytes 98308
  135.2 5.5 %copy-start.1 = (s32[64,128]{1,0:T(8,128)S(1)}, s32[64,128]{1,0:T(8,128)}, u32[]{:S(2)}) copy-start(s32[64,128]{1,0:T(8,128)} %get-tuple-element.15.column) | copy-start | bytes 98308
  135.3 22.2 %all-to-all-start.2 = ((f32[32,32,256]{2,1,0:T(8,128)}), f32[32,32,256]{2,1,0:T(8,128)S(1)}, u32[]{:S(2)}, u32[]{:S(2)}) async-start(f32[32,32,256]{2,1,0:T(8,128)} %correlate.2), calls=%async_computation.2 | async-start | bytes 2097152 | tf_op jit(solution)/shard_map/all_to_all | solution.py:445

commit v7 on v6

--- a/solution.py
+++ b/solution.py
@@ -231,7 +231,7 @@
             spectrum[r, 1, :, lanes] = cos_im - sin_re
 
 
-def lesser_spectrum(matrix, turn, both):
+def lesser_spectrum(matrix, turn, both, limit):
     width = both.shape[-1]
     return pl.pallas_call(
         lesser_kernel,
@@ -239,27 +239,13 @@
         out_specs=VMEM,
         out_shape=jax.ShapeDtypeStruct((4, 2, 256, width), F32),
         scratch_shapes=[pltpu.VMEM((PARTS, 32, width), F32), pltpu.SemaphoreType.DMA],
-        compiler_params=params(),
+        compiler_params=params(limit << 20),
         cost_estimate=cost(width * 2 * 4 * 512 * 768 * 2, width * 12288),
         name="lesser_spectrum",
     )(matrix, turn, both)
 
 
-def correlate_kernel(matrix_in, turn_in, spectrum_in, b_in, out, matrix, turn, spectrum, b_ref, sems):
-    first = [
-        pltpu.make_async_copy(b_in, b_ref, sems.at[0]),
-        pltpu.make_async_copy(matrix_in, matrix, sems.at[1]),
-    ]
-    loads = [pltpu.make_async_copy(spectrum_in.at[r], spectrum.at[r], sems.at[3 + r]) for r in range(4)]
-    angles = pltpu.make_async_copy(turn_in, turn, sems.at[2])
-    for load in first:
-        load.start()
-    for load in first:
-        load.wait()
-    loads[0].start()
-    angles.start()
-    for load in loads[1:]:
-        load.start()
+def correlate_kernel(matrix, turn, spectrum, b_ref, out):
     scale = 1.0 / (1024.0 * math.sqrt(ENERGIES))
     tile = min(TILE, out.shape[-1])
     for w in range(0, out.shape[-1], tile):
@@ -271,14 +257,10 @@
             re = (re0 + re1, re0 - im1, re0 - re1, re0 + im1)[r]
             im = (im0 + im1, im0 + re1, im0 - im1, im0 - re1)[r]
             if r:
-                if w == 0 and r == 1:
-                    angles.wait()
                 c, s = turned(turn, r, part)
                 re, im = re * c - im * s, im * c + re * s
             cos_re, cos_im, sin_re, sin_im = product(matrix, re, im)
             b_re, b_im = cos_re - sin_im, cos_im + sin_re
-            if w == 0:
-                loads[r].wait()
             a_re, a_im = spectrum[r, 0, :, part], spectrum[r, 1, :, part]
             cos_re, cos_im, sin_re, sin_im = product(
                 matrix, a_re * b_re - a_im * b_im, a_re * b_im + a_im * b_re
@@ -303,21 +285,14 @@
         out[16:, 16:, part] = (high_re * -scale).reshape(shape)
 
 
-def correlate(matrix, turn, spectrum, b):
+def correlate(matrix, turn, spectrum, b, limit):
     width = b.shape[-1]
     return pl.pallas_call(
         correlate_kernel,
-        in_specs=[ANY] * 4,
+        in_specs=[VMEM] * 4,
         out_specs=VMEM,
         out_shape=jax.ShapeDtypeStruct((PARTS, 32, width), F32),
-        scratch_shapes=[
-            pltpu.VMEM(matrix.shape, BF16),
-            pltpu.VMEM(turn.shape, F32),
-            pltpu.VMEM(spectrum.shape, F32),
-            pltpu.VMEM(b.shape, F32),
-            pltpu.SemaphoreType.DMA((7,)),
-        ],
-        compiler_params=params(),
+        compiler_params=params(limit << 20),
         cost_estimate=cost(width * 2 * 4 * 512 * 768 * 4, width * 12288),
         name="correlate",
     )(matrix, turn, spectrum, b)
@@ -453,12 +428,12 @@
     lesser0, greater0 = arrived0[:, :32], arrived0[:, 32:]
     mirrored0 = cross(greater0)
     arrived1 = swap(picked1)
-    spectrum0 = lesser_spectrum(matrix, turn, lesser0)
+    spectrum0 = lesser_spectrum(matrix, turn, lesser0, 60)
     arrived1, spectrum0 = lax.optimization_barrier((arrived1, spectrum0))
     mirrored1 = cross(arrived1[:, 32:])
-    polar0 = swap(correlate(matrix, turn, spectrum0, mirrored0))
-    spectrum1 = lesser_spectrum(matrix, turn, arrived1)
-    polar1 = swap(correlate(matrix, turn, spectrum1, mirrored1))
+    polar0 = swap(correlate(matrix, turn, spectrum0, mirrored0, 50))
+    spectrum1 = lesser_spectrum(matrix, turn, arrived1, 50)
+    polar1 = swap(correlate(matrix, turn, spectrum1, mirrored1, 50))
     slots = scatter(columns0, polar0, None)
     return scatter(columns1, polar1, slots)
 

time: 168 us -> 167 us (level)
  Pallas kernels: 86.4 us -> 80.7 us
  local copies, waits for them, and re-layouts: 4.16 us -> 7 us
  waiting for transfers between devices: 41.7 us -> 44.3 us
    pallas_call x2, Pallas kernels: 17.8 us -> 14.7 us  [correlate(): pl.pallas_call(correlate_kernel, in_specs=[VMEM] * 4, out_specs=VMEM, out...]
    ppermute x2, waiting for transfers between devices: 2.11 us -> 4.97 us  [cross(): return lax.ppermute(values, 'slab', across)]
    pallas_call x2, Pallas kernels: 11.6 us -> 8.9 us  [lesser_spectrum(): pl.pallas_call(lesser_kernel, in_specs=[VMEM, VMEM, ANY], out_specs=VMEM,...]
  transfers between devices with their start and end apart: 8 -> 8, of which waited for: 5 -> 4; matrix products, arithmetic and copies ran while one was open for 1% -> 2% of each run, Pallas kernels for 37% -> 34%
where the time goes in v7:
time: 167 us; the launch traced here: 166 us
  Pallas kernels  80.7 us (48%)
  waiting for transfers between devices  44.3 us (27%)
  starting transfers between devices  33.5 us (20%)
  local copies, waits for them, and re-layouts  7 us (4%)
    all_to_all x4, waiting for transfers between devices, swap(): return lax.all_to_all(values, 'energy', 0, 0, tiled=True)  39.3 us
    pallas_call x2, Pallas kernels, gather(): pl.pallas_call(functools.partial(gather_kernel, base=base), in_specs=[SME...  31 us
    all_to_all x4, starting transfers between devices, swap(): return lax.all_to_all(values, 'energy', 0, 0, tiled=True)  24.4 us
    pallas_call x2, Pallas kernels, scatter(): pl.pallas_call(scatter_first_kernel if first else scatter_last_kernel, in...  18.2 us
    pallas_call x2, Pallas kernels, correlate(): pl.pallas_call(correlate_kernel, in_specs=[VMEM] * 4, out_specs=VMEM, out...  14.7 us
    pallas_call x2, Pallas kernels, lesser_spectrum(): pl.pallas_call(lesser_kernel, in_specs=[VMEM, VMEM, ANY], out_specs=VMEM,...  8.9 us
    pallas_call x1, Pallas kernels, column_rows(): pl.pallas_call(rows_kernel, grid=(steps,), in_specs=[low, low, high, high...  7.86 us
    ppermute x2, starting transfers between devices, cross(): return lax.ppermute(values, 'slab', across)  5.48 us
  transfers between devices with their start and end apart: 8, of which 4 were waited for; matrix products, arithmetic and copies ran while one was open for 2% of the time, Pallas kernels for 34%

profile of v7, /device:TPU:1, one launch (start us, length us, event | category | flops | bytes accessed | tf_op | source)
XLA Modules:
  0.0 166.4 jit_solution(8608755330242229966)
XLA Ops:
  0.0 3.6 %collective-permute-start.1 = (s32[32768]{0:T(1024)}, s32[32768]{0:T(1024)S(1)}, u32[]{:S(2)}, u32[]{:S(2)}) collective-permute-start(s32[32768]{0:T(1024)} %param.11), channel_id=1, source_target_pairs={{0,96},{32,64},{64,32},{96,0},{1,97},{33,65},{65,33},{97,1},{2,98}... | collective-permute-start | bytes 393224 | tf_op jit(solution)/shard_map/ppermute | solution.py:411
  3.6 0.0 collective-permute-start
  4.2 7.9 %column_rows.1 = (f32[16384,128]{1,0:T(8,128)}, s32[256,128]{1,0:T(8,128)}) custom-call(f32[2,16,32768]{2,1,0:T(8,128)} %a_high.1, f32[2,16,32768]{2,1,0:T(8,128)} %b_high.1, f32[2,16,32768]{2,1,0:T(8,128)} %a_high.1, f32[2,16,32768]{2,1,0:T(8,128)} %b_high.1), custom_call_target="tpu_custom_call" | custom-call | flops 1048576 | bytes 25165824 | tf_op jit(solution)/shard_map/column_rows/pallas_call | solution.py:49
  12.1 0.0 collective-permute-done.1.mirror
  12.1 0.0 copy-start.6
  12.1 0.0 collective-permute-done.other
  12.1 0.0 copy-start.7
  12.1 0.6 copy-done.6
  12.8 0.1 copy-done.7
  12.8 15.6 %gather.3 = (f32[32,64,256]{2,1,0:T(8,128)}, s32[64,128]{1,0:T(8,128)}) custom-call(s32[1]{0:T(128)S(6)} %copy.8.count, s32[1]{0:T(128)} %bitcast.upper, s32[32768]{0:T(1024)} %own.3, s32[32768]{0:T(1024)} %copy-done.7, s32[32768]{0:T(1024)} %bitcast.6, s32[32768]{0:T(1024)} %copy-done.6, f32[16384,128]{1,0:T(8,128)} %get-tuple-element.14.rows), custom_call_target="tpu_custom_call" | custom-call | flops 16384000 | bytes 40960000 | tf_op jit(solution)/shard_map/gather/pallas_call | solution.py:156
  28.4 9.1 %all-to-all-start.1 = ((f32[32,64,256]{2,1,0:T(8,128)}), f32[32,64,256]{2,1,0:T(8,128)S(1)}, u32[]{:S(2)}, u32[]{:S(2)}) async-start(f32[32,64,256]{2,1,0:T(8,128)} %get-tuple-element.17), calls=%async_computation.1 | async-start | bytes 4194304 | tf_op jit(solution)/shard_map/all_to_all | solution.py:420
  37.5 15.5 %gather.2 = (f32[32,64,256]{2,1,0:T(8,128)}, s32[64,128]{1,0:T(8,128)}) custom-call(s32[1]{0:T(128)S(6)} %copy.8.count, s32[1]{0:T(128)} %bitcast.upper, s32[32768]{0:T(1024)} %own.3, s32[32768]{0:T(1024)} %copy-done.7, s32[32768]{0:T(1024)} %bitcast.7, s32[32768]{0:T(1024)} %copy-done.6, f32[16384,128]{1,0:T(8,128)} %get-tuple-element.14.rows), custom_call_target="tpu_custom_call" | custom-call | flops 16384000 | bytes 40960000 | tf_op jit(solution)/shard_map/gather/pallas_call | solution.py:156
  52.9 12.8 %all-to-all-done.1 = f32[32,64,256]{2,1,0:T(8,128)S(1)} async-done(((f32[32,64,256]{2,1,0:T(8,128)}), f32[32,64,256]{2,1,0:T(8,128)S(1)}, u32[]{:S(2)}, u32[]{:S(2)}) %all-to-all-start.1) | async-done | bytes 2097184 | tf_op jit(solution)/shard_map/all_to_all | solution.py:420
  65.8 5.2 %all-to-all-start = ((f32[32,64,256]{2,1,0:T(8,128)}), f32[32,64,256]{2,1,0:T(8,128)}, u32[]{:S(2)}, u32[]{:S(2)}) async-start(f32[32,64,256]{2,1,0:T(8,128)} %get-tuple-element.16), calls=%async_computation | async-start | bytes 4194304 | tf_op jit(solution)/shard_map/all_to_all | solution.py:420
  71.0 1.4 fusion
  72.4 2.7 %collective-permute-start.3 = (f32[32,32,256]{2,1,0:T(8,128)}, f32[32,32,256]{2,1,0:T(8,128)S(1)}, u32[]{:S(2)}, u32[]{:S(2)}) collective-permute-start(f32[32,32,256]{2,1,0:T(8,128)} %get-tuple-element.21), channel_id=1, source_target_pairs={{0,96},{32,64},{64,32},{96,0},{1,97},{33,65},{65,33},{97,1},{2,98}... | collective-permute-start | bytes 3145736 | tf_op jit(solution)/shard_map/ppermute | solution.py:423
  75.2 5.8 %lesser_spectrum.2.spectrum = f32[4,2,256,256]{3,2,1,0:T(8,128)} custom-call(bf16[512,768]{1,0:T(8,128)(2,1)} %constant.18.clone.matrix, f32[3,2,256,128]{3,2,1,0:T(8,128)} %constant.19.clone.turn, f32[32,32,256]{2,1,0:T(8,128)} %get-tuple-element.22.both_in), custom_call_target="tpu_custom_call" | custom-call | flops 1610612736 | bytes 3145728 | tf_op jit(solution)/shard_map/lesser_spectrum/pallas_call | solution.py:236
  81.0 0.0 copy-start.2
  81.0 18.4 %all-to-all-done.both_in = f32[32,64,256]{2,1,0:T(8,128)} async-done(((f32[32,64,256]{2,1,0:T(8,128)}), f32[32,64,256]{2,1,0:T(8,128)}, u32[]{:S(2)}, u32[]{:S(2)}) %all-to-all-start) | async-done | bytes 2097184 | tf_op jit(solution)/shard_map/all_to_all | solution.py:420
  99.4 0.0 copy-start.3
  99.4 2.4 %slice.10 = f32[32,32,256]{2,1,0:T(8,128)} slice(f32[32,64,256]{2,1,0:T(8,128)} %all-to-all-done.both_in), slice={[0:32], [32:64], [0:256]} | slice | bytes 2097152 | tf_op jit(solution)/shard_map/slice | solution.py:433
  101.8 2.7 %collective-permute-start.2 = (f32[32,32,256]{2,1,0:T(8,128)}, f32[32,32,256]{2,1,0:T(8,128)S(1)}, u32[]{:S(2)}, u32[]{:S(2)}) collective-permute-start(f32[32,32,256]{2,1,0:T(8,128)} %slice.10), channel_id=1, source_target_pairs={{0,96},{32,64},{64,32},{96,0},{1,97},{33,65},{65,33},{97,1},{2,98}... | collective-permute-start | bytes 3145736 | tf_op jit(solution)/shard_map/ppermute | solution.py:423
  104.6 0.0 collective-permute-done.3.b_ref
  104.6 0.0 copy-done.2
  104.6 0.0 copy-done.3
  104.6 7.3 %correlate.3 = f32[32,32,256]{2,1,0:T(8,128)} custom-call(bf16[512,768]{1,0:T(8,128)(2,1)S(1)} %copy-done.3, f32[3,2,256,128]{3,2,1,0:T(8,128)S(1)} %copy-done.2, f32[4,2,256,256]{3,2,1,0:T(8,128)} %lesser_spectrum.2.spectrum, f32[32,32,256]{2,1,0:T(8,128)S(1)} %collective-permute-done.3.b_ref), custom_call_target="tpu_custom_call" | custom-call | flops 3221225472 | bytes 3145728 | tf_op jit(solution)/shard_map/correlate/pallas_call | solution.py:290
  111.9 4.7 %all-to-all-start.3 = ((f32[32,32,256]{2,1,0:T(8,128)}), f32[32,32,256]{2,1,0:T(8,128)S(1)}, u32[]{:S(2)}, u32[]{:S(2)}) async-start(f32[32,32,256]{2,1,0:T(8,128)} %correlate.3), calls=%async_computation.3 | async-start | bytes 2097152 | tf_op jit(solution)/shard_map/all_to_all | solution.py:420
  116.6 0.0 copy-start.4
  116.6 1.1 copy-done.4
  117.8 3.1 %lesser_spectrum.3.spectrum = f32[4,2,256,256]{3,2,1,0:T(8,128)S(1)} custom-call(bf16[512,768]{1,0:T(8,128)(2,1)S(1)} %copy-done.4, f32[3,2,256,128]{3,2,1,0:T(8,128)S(1)} %copy-done.2, f32[32,64,256]{2,1,0:T(8,128)} %all-to-all-done.both_in), custom_call_target="tpu_custom_call" | custom-call | flops 1610612736 | bytes 3145728 | tf_op jit(solution)/shard_map/lesser_spectrum/pallas_call | solution.py:236
  120.9 0.0 copy-start.5
  120.9 1.3 copy-done.5
  122.2 5.0 %collective-permute-done.2.b_ref = f32[32,32,256]{2,1,0:T(8,128)S(1)} collective-permute-done((f32[32,32,256]{2,1,0:T(8,128)}, f32[32,32,256]{2,1,0:T(8,128)S(1)}, u32[]{:S(2)}, u32[]{:S(2)}) %collective-permute-start.2) | collective-permute-done | bytes 1048608 | tf_op jit(solution)/shard_map/ppermute | solution.py:423
  127.2 7.4 %correlate.2 = f32[32,32,256]{2,1,0:T(8,128)} custom-call(bf16[512,768]{1,0:T(8,128)(2,1)S(1)} %copy-done.4, f32[3,2,256,128]{3,2,1,0:T(8,128)S(1)} %copy-done.2, f32[4,2,256,256]{3,2,1,0:T(8,128)} %copy-done.5, f32[32,32,256]{2,1,0:T(8,128)S(1)} %collective-permute-done.2.b_ref), custom_call_target="tpu_custom_call" | custom-call | flops 3221225472 | bytes 3145728 | tf_op jit(solution)/shard_map/correlate/pallas_call | solution.py:290
  134.6 0.0 copy-start
  134.6 0.0 copy-start.1
  134.6 0.0 all-to-all-done.3.values
  134.6 5.4 %all-to-all-start.2 = ((f32[32,32,256]{2,1,0:T(8,128)}), f32[32,32,256]{2,1,0:T(8,128)S(1)}, u32[]{:S(2)}, u32[]{:S(2)}) async-start(f32[32,32,256]{2,1,0:T(8,128)} %correlate.2), calls=%async_computation.2 | async-start | bytes 2097152 | tf_op jit(solution)/shard_map/all_to_all | solution.py:420
  140.0 0.0 copy-done
  140.0 0.0 copy-done.1
  140.1 8.9 %scatter.2.before = f32[6,8192,128]{2,1,0:T(8,128)} custom-call(s32[8192]{0:T(1024)S(1)} %or_bitcast_fusion.row_of, s32[64,128]{1,0:T(8,128)S(1)} %copy-done, f32[32,32,256]{2,1,0:T(8,128)S(1)} %all-to-all-done.3.values), custom_call_target="tpu_custom_call" | custom-call | flops 8192000 | bytes 32768000 | tf_op jit(solution)/shard_map/scatter/pallas_call | solution.py:395
  149.0 8.0 %all-to-all-done.2.values = f32[32,32,256]{2,1,0:T(8,128)S(1)} async-done(((f32[32,32,256]{2,1,0:T(8,128)}), f32[32,32,256]{2,1,0:T(8,128)S(1)}, u32[]{:S(2)}, u32[]{:S(2)}) %all-to-all-start.2) | async-done | bytes 1048608 | tf_op jit(solution)/shard_map/all_to_all | solution.py:420
  157.0 9.3 %scatter.3 = f32[2,16,32768]{2,1,0:T(8,128)} custom-call(s32[8192]{0:T(1024)S(1)} %or_bitcast_fusion.1.row_of, s32[64,128]{1,0:T(8,128)S(1)} %copy-done.1, f32[32,32,256]{2,1,0:T(8,128)S(1)} %all-to-all-done.2.values, f32[6,8192,128]{2,1,0:T(8,128)} %scatter.2.before), custom_call_target="tpu_custom_call" | custom-call | flops 8192000 | bytes 32768000 | tf_op jit(solution)/shard_map/scatter/pallas_call | solution.py:395
  (2 shorter events, 0.0 us)
Async XLA Ops:
  0.0 12.1 %collective-permute-start.1 = (s32[32768]{0:T(1024)}, s32[32768]{0:T(1024)S(1)}, u32[]{:S(2)}, u32[]{:S(2)}) collective-permute-start(s32[32768]{0:T(1024)} %param.11), channel_id=1, source_target_pairs={{0,96},{32,64},{64,32},{96,0},{1,97},{33,65},{65,33},{97,1},{2,98}... | collective-permute-start | bytes 393224 | tf_op jit(solution)/shard_map/ppermute | solution.py:411
  3.6 8.6 %collective-permute-start = (s32[32768]{0:T(1024)}, s32[32768]{0:T(1024)S(1)}, u32[]{:S(2)}, u32[]{:S(2)}) collective-permute-start(s32[32768]{0:T(1024)} %own.3), channel_id=1, source_target_pairs={{0,96},{32,64},{64,32},{96,0},{1,97},{33,65},{65,33},{97,1},{2,98}... | collective-permute-start | bytes 393224 | tf_op jit(solution)/shard_map/ppermute | solution.py:412
  12.1 0.7 copy-start.6
  12.1 0.7 copy-start.7
  28.4 37.4 %all-to-all-start.1 = ((f32[32,64,256]{2,1,0:T(8,128)}), f32[32,64,256]{2,1,0:T(8,128)S(1)}, u32[]{:S(2)}, u32[]{:S(2)}) async-start(f32[32,64,256]{2,1,0:T(8,128)} %get-tuple-element.17), calls=%async_computation.1 | async-start | bytes 4194304 | tf_op jit(solution)/shard_map/all_to_all | solution.py:420
  65.8 33.6 %all-to-all-start = ((f32[32,64,256]{2,1,0:T(8,128)}), f32[32,64,256]{2,1,0:T(8,128)}, u32[]{:S(2)}, u32[]{:S(2)}) async-start(f32[32,64,256]{2,1,0:T(8,128)} %get-tuple-element.16), calls=%async_computation | async-start | bytes 4194304 | tf_op jit(solution)/shard_map/all_to_all | solution.py:420
  72.4 32.1 %collective-permute-start.3 = (f32[32,32,256]{2,1,0:T(8,128)}, f32[32,32,256]{2,1,0:T(8,128)S(1)}, u32[]{:S(2)}, u32[]{:S(2)}) collective-permute-start(f32[32,32,256]{2,1,0:T(8,128)} %get-tuple-element.21), channel_id=1, source_target_pairs={{0,96},{32,64},{64,32},{96,0},{1,97},{33,65},{65,33},{97,1},{2,98}... | collective-permute-start | bytes 3145736 | tf_op jit(solution)/shard_map/ppermute | solution.py:423
  81.0 23.6 %copy-start.2 = (f32[3,2,256,128]{3,2,1,0:T(8,128)S(1)}, f32[3,2,256,128]{3,2,1,0:T(8,128)}, u32[]{:S(2)}) copy-start(f32[3,2,256,128]{3,2,1,0:T(8,128)} %constant.19.clone.turn) | copy-start | bytes 2359300
  99.4 5.1 %copy-start.3 = (bf16[512,768]{1,0:T(8,128)(2,1)S(1)}, bf16[512,768]{1,0:T(8,128)(2,1)}, u32[]{:S(2)}) copy-start(bf16[512,768]{1,0:T(8,128)(2,1)} %constant.18.clone.matrix) | copy-start | bytes 2359300
  101.8 25.4 %collective-permute-start.2 = (f32[32,32,256]{2,1,0:T(8,128)}, f32[32,32,256]{2,1,0:T(8,128)S(1)}, u32[]{:S(2)}, u32[]{:S(2)}) collective-permute-start(f32[32,32,256]{2,1,0:T(8,128)} %slice.10), channel_id=1, source_target_pairs={{0,96},{32,64},{64,32},{96,0},{1,97},{33,65},{65,33},{97,1},{2,98}... | collective-permute-start | bytes 3145736 | tf_op jit(solution)/shard_map/ppermute | solution.py:423
  111.9 22.7 %all-to-all-start.3 = ((f32[32,32,256]{2,1,0:T(8,128)}), f32[32,32,256]{2,1,0:T(8,128)S(1)}, u32[]{:S(2)}, u32[]{:S(2)}) async-start(f32[32,32,256]{2,1,0:T(8,128)} %correlate.3), calls=%async_computation.3 | async-start | bytes 2097152 | tf_op jit(solution)/shard_map/all_to_all | solution.py:420
  116.6 1.1 copy-start.4
  120.9 1.3 copy-start.5
  134.6 5.4 %copy-start = (s32[64,128]{1,0:T(8,128)S(1)}, s32[64,128]{1,0:T(8,128)}, u32[]{:S(2)}) copy-start(s32[64,128]{1,0:T(8,128)} %get-tuple-element.19.column) | copy-start | bytes 98308
  134.6 5.5 %copy-start.1 = (s32[64,128]{1,0:T(8,128)S(1)}, s32[64,128]{1,0:T(8,128)}, u32[]{:S(2)}) copy-start(s32[64,128]{1,0:T(8,128)} %get-tuple-element.15.column) | copy-start | bytes 98308
  134.6 22.4 %all-to-all-start.2 = ((f32[32,32,256]{2,1,0:T(8,128)}), f32[32,32,256]{2,1,0:T(8,128)S(1)}, u32[]{:S(2)}, u32[]{:S(2)}) async-start(f32[32,32,256]{2,1,0:T(8,128)} %correlate.2), calls=%async_computation.2 | async-start | bytes 2097152 | tf_op jit(solution)/shard_map/all_to_all | solution.py:420

commit v8 on v7

--- a/solution.py
+++ b/solution.py
@@ -65,7 +65,7 @@
 
 
 def gather_kernel(
-    count, upper, own, other, identity, mirror, rows, out, places,
+    count, upper, own, other, identity, rows, out, places,
     packed, list0, list1, mapped, table, map_sem, list_sems, row_sems, *, base
 ):
     width = out.shape[-1]
@@ -74,8 +74,8 @@
     items = BATCH * 128
     count_batches = PARTS * per // BATCH
 
-    def fetch(source, batch, h):
-        piece = pl.ds(pl.multiple_of(base + batch * items, items), items)
+    def fetch(source, batch, h, skip=0):
+        piece = pl.ds(pl.multiple_of(skip + base + batch * items, items), items)
         return pltpu.make_async_copy(source.at[piece], lists[h], list_sems.at[h])
 
     def start(batch, h):
@@ -85,7 +85,7 @@
 
         @pl.when(upper[0] != 0)
         def _():
-            fetch(other, batch, h).start()
+            fetch(other, batch, h, SLOTS).start()
 
     @pl.when(upper[0] == 0)
     def _():
@@ -93,7 +93,7 @@
 
     @pl.when(upper[0] != 0)
     def _():
-        pltpu.make_async_copy(mirror, mapped, map_sem).start()
+        pltpu.make_async_copy(other.at[pl.ds(0, SLOTS)], mapped, map_sem).start()
 
     start(0, 0)
     start(1, 1)
@@ -155,7 +155,7 @@
     items = PARTS * width
     return pl.pallas_call(
         functools.partial(gather_kernel, base=base),
-        in_specs=[SMEM, SMEM, ANY, ANY, ANY, ANY, ANY],
+        in_specs=[SMEM, SMEM, ANY, ANY, ANY, ANY],
         out_specs=[VMEM, VMEM],
         out_shape=[
             jax.ShapeDtypeStruct((PARTS, 64, width), F32),
@@ -408,11 +408,10 @@
     slabs = lax.axis_size("slab")
     across = [(s, slabs - 1 - s) for s in range(slabs)]
     upper = (lax.axis_index("slab") >= slabs // 2).astype(jnp.int32).reshape(1)
-    other_mirror = lax.ppermute(mirror, "slab", across)
-    other_live = lax.ppermute(live_columns, "slab", across)
+    other = lax.ppermute(jnp.concatenate([mirror, live_columns]), "slab", across)
     rows, identity = column_rows(g_lesser, g_greater)
     identity = identity.reshape(SLOTS)
-    lists = (live_count, upper, live_columns, other_live, identity, other_mirror)
+    lists = (live_count, upper, live_columns, other, identity)
     matrix, turn = tables()
     matrix, turn = jnp.asarray(matrix), jnp.asarray(turn)
 

time: 167 us -> 168 us (level)
  starting transfers between devices: 33.5 us -> 28.9 us
  waiting for transfers between devices: 44.3 us -> 48.7 us
    ppermute x2, starting transfers between devices: 5.48 us -> 0.91 us  [cross(): return lax.ppermute(values, 'slab', across)]
    all_to_all x4, waiting for transfers between devices: 39.3 us -> 41.5 us  [swap(): return lax.all_to_all(values, 'energy', 0, 0, tiled=True)]
    ppermute x2, waiting for transfers between devices: 4.97 us -> 7.11 us  [cross(): return lax.ppermute(values, 'slab', across)]
    ppermute x2 -> x1, starting transfers between devices: 3.6 us -> 3.64 us  [local(): lax.ppermute(jnp.concatenate([mirror, live_columns]), 'slab', across)]
  transfers between devices with their start and end apart: 8 -> 7, of which waited for: 4 -> 4; matrix products, arithmetic and copies ran while one was open for 2% -> 2% of each run, Pallas kernels for 34% -> 33%
where the time goes in v8:
time: 168 us; the launch traced here: 167 us
  Pallas kernels  80.7 us (48%)
  waiting for transfers between devices  48.7 us (29%)
  starting transfers between devices  28.9 us (17%)
  local copies, waits for them, and re-layouts  7.01 us (4%)
    all_to_all x4, waiting for transfers between devices, swap(): return lax.all_to_all(values, 'energy', 0, 0, tiled=True)  41.5 us
    pallas_call x2, Pallas kernels, gather(): pl.pallas_call(functools.partial(gather_kernel, base=base), in_specs=[SME...  31 us
    all_to_all x4, starting transfers between devices, swap(): return lax.all_to_all(values, 'energy', 0, 0, tiled=True)  24.3 us
    pallas_call x2, Pallas kernels, scatter(): pl.pallas_call(scatter_first_kernel if first else scatter_last_kernel, in...  18.2 us
    pallas_call x2, Pallas kernels, correlate(): pl.pallas_call(correlate_kernel, in_specs=[VMEM] * 4, out_specs=VMEM, out...  14.7 us
    pallas_call x2, Pallas kernels, lesser_spectrum(): pl.pallas_call(lesser_kernel, in_specs=[VMEM, VMEM, ANY], out_specs=VMEM,...  8.91 us
    pallas_call x1, Pallas kernels, column_rows(): pl.pallas_call(rows_kernel, grid=(steps,), in_specs=[low, low, high, high...  7.86 us
    ppermute x2, waiting for transfers between devices, cross(): return lax.ppermute(values, 'slab', across)  7.11 us
  transfers between devices with their start and end apart: 7, of which 4 were waited for; matrix products, arithmetic and copies ran while one was open for 2% of the time, Pallas kernels for 33%

profile of v8, /device:TPU:1, one launch (start us, length us, event | category | flops | bytes accessed | tf_op | source)
XLA Modules:
  0.0 167.2 jit_solution(11792895332003797590)
XLA Ops:
  0.0 1.0 pad_add_fusion
  1.0 3.6 %collective-permute-start = (s32[65536]{0:T(1024)S(1)}, s32[65536]{0:T(1024)S(1)}, u32[]{:S(2)}, u32[]{:S(2)}) collective-permute-start(s32[65536]{0:T(1024)S(1)} %pad_add_fusion), channel_id=1, source_target_pairs={{0,96},{32,64},{64,32},{96,0},{1,97},{33,65},{65,33},{97,1},{2,98}... | collective-permute-start | bytes 786440 | tf_op jit(solution)/shard_map/ppermute | solution.py:411
  5.3 7.9 %column_rows.1 = (f32[16384,128]{1,0:T(8,128)}, s32[256,128]{1,0:T(8,128)}) custom-call(f32[2,16,32768]{2,1,0:T(8,128)} %a_high.1, f32[2,16,32768]{2,1,0:T(8,128)} %b_high.1, f32[2,16,32768]{2,1,0:T(8,128)} %a_high.1, f32[2,16,32768]{2,1,0:T(8,128)} %b_high.1), custom_call_target="tpu_custom_call" | custom-call | flops 1048576 | bytes 25165824 | tf_op jit(solution)/shard_map/column_rows/pallas_call | solution.py:49
  13.1 0.0 collective-permute-done.other
  13.1 0.0 copy-start.6
  13.2 0.7 copy-done.6
  13.8 15.6 %gather.3 = (f32[32,64,256]{2,1,0:T(8,128)}, s32[64,128]{1,0:T(8,128)}) custom-call(s32[1]{0:T(128)S(6)} %copy.8.count, s32[1]{0:T(128)} %bitcast.upper, s32[32768]{0:T(1024)} %own.3, s32[65536]{0:T(1024)} %copy-done.6, s32[32768]{0:T(1024)} %bitcast.6, f32[16384,128]{1,0:T(8,128)} %get-tuple-element.14.rows), custom_call_target="tpu_custom_call" | custom-call | flops 16384000 | bytes 40960000 | tf_op jit(solution)/shard_map/gather/pallas_call | solution.py:156
  29.4 8.9 %all-to-all-start.1 = ((f32[32,64,256]{2,1,0:T(8,128)}), f32[32,64,256]{2,1,0:T(8,128)S(1)}, u32[]{:S(2)}, u32[]{:S(2)}) async-start(f32[32,64,256]{2,1,0:T(8,128)} %get-tuple-element.17), calls=%async_computation.1 | async-start | bytes 4194304 | tf_op jit(solution)/shard_map/all_to_all | solution.py:419
  38.3 15.5 %gather.2 = (f32[32,64,256]{2,1,0:T(8,128)}, s32[64,128]{1,0:T(8,128)}) custom-call(s32[1]{0:T(128)S(6)} %copy.8.count, s32[1]{0:T(128)} %bitcast.upper, s32[32768]{0:T(1024)} %own.3, s32[65536]{0:T(1024)} %copy-done.6, s32[32768]{0:T(1024)} %bitcast.7, f32[16384,128]{1,0:T(8,128)} %get-tuple-element.14.rows), custom_call_target="tpu_custom_call" | custom-call | flops 16384000 | bytes 40960000 | tf_op jit(solution)/shard_map/gather/pallas_call | solution.py:156
  53.8 12.8 %all-to-all-done.1 = f32[32,64,256]{2,1,0:T(8,128)S(1)} async-done(((f32[32,64,256]{2,1,0:T(8,128)}), f32[32,64,256]{2,1,0:T(8,128)S(1)}, u32[]{:S(2)}, u32[]{:S(2)}) %all-to-all-start.1) | async-done | bytes 2097184 | tf_op jit(solution)/shard_map/all_to_all | solution.py:419
  66.6 5.2 %all-to-all-start = ((f32[32,64,256]{2,1,0:T(8,128)}), f32[32,64,256]{2,1,0:T(8,128)}, u32[]{:S(2)}, u32[]{:S(2)}) async-start(f32[32,64,256]{2,1,0:T(8,128)} %get-tuple-element.16), calls=%async_computation | async-start | bytes 4194304 | tf_op jit(solution)/shard_map/all_to_all | solution.py:419
  71.8 1.5 fusion
  73.3 0.5 collective-permute-start.2
  73.7 5.8 %lesser_spectrum.2.spectrum = f32[4,2,256,256]{3,2,1,0:T(8,128)} custom-call(bf16[512,768]{1,0:T(8,128)(2,1)} %constant.18.clone.matrix, f32[3,2,256,128]{3,2,1,0:T(8,128)} %constant.19.clone.turn, f32[32,32,256]{2,1,0:T(8,128)} %get-tuple-element.22.both_in), custom_call_target="tpu_custom_call" | custom-call | flops 1610612736 | bytes 3145728 | tf_op jit(solution)/shard_map/lesser_spectrum/pallas_call | solution.py:236
  79.5 0.0 copy-start.2
  79.6 20.7 %all-to-all-done.both_in = f32[32,64,256]{2,1,0:T(8,128)} async-done(((f32[32,64,256]{2,1,0:T(8,128)}), f32[32,64,256]{2,1,0:T(8,128)}, u32[]{:S(2)}, u32[]{:S(2)}) %all-to-all-start) | async-done | bytes 2097184 | tf_op jit(solution)/shard_map/all_to_all | solution.py:419
  100.3 0.0 copy-start.3
  100.3 2.4 %slice.10 = f32[32,32,256]{2,1,0:T(8,128)} slice(f32[32,64,256]{2,1,0:T(8,128)} %all-to-all-done.both_in), slice={[0:32], [32:64], [0:256]} | slice | bytes 2097152 | tf_op jit(solution)/shard_map/slice | solution.py:432
  102.7 0.5 collective-permute-start.1
  103.1 0.0 collective-permute-done.2.b_ref
  103.1 0.0 copy-done.2
  103.1 0.0 copy-done.3
  103.1 7.3 %correlate.3 = f32[32,32,256]{2,1,0:T(8,128)} custom-call(bf16[512,768]{1,0:T(8,128)(2,1)S(1)} %copy-done.3, f32[3,2,256,128]{3,2,1,0:T(8,128)S(1)} %copy-done.2, f32[4,2,256,256]{3,2,1,0:T(8,128)} %lesser_spectrum.2.spectrum, f32[32,32,256]{2,1,0:T(8,128)S(1)} %collective-permute-done.2.b_ref), custom_call_target="tpu_custom_call" | custom-call | flops 3221225472 | bytes 3145728 | tf_op jit(solution)/shard_map/correlate/pallas_call | solution.py:290
  110.5 4.7 %all-to-all-start.3 = ((f32[32,32,256]{2,1,0:T(8,128)}), f32[32,32,256]{2,1,0:T(8,128)S(1)}, u32[]{:S(2)}, u32[]{:S(2)}) async-start(f32[32,32,256]{2,1,0:T(8,128)} %correlate.3), calls=%async_computation.3 | async-start | bytes 2097152 | tf_op jit(solution)/shard_map/all_to_all | solution.py:419
  115.2 0.0 copy-start.4
  115.2 1.1 copy-done.4
  116.3 3.1 %lesser_spectrum.3.spectrum = f32[4,2,256,256]{3,2,1,0:T(8,128)S(1)} custom-call(bf16[512,768]{1,0:T(8,128)(2,1)S(1)} %copy-done.4, f32[3,2,256,128]{3,2,1,0:T(8,128)S(1)} %copy-done.2, f32[32,64,256]{2,1,0:T(8,128)} %all-to-all-done.both_in), custom_call_target="tpu_custom_call" | custom-call | flops 1610612736 | bytes 3145728 | tf_op jit(solution)/shard_map/lesser_spectrum/pallas_call | solution.py:236
  119.4 0.0 copy-start.5
  119.5 1.3 copy-done.5
  120.8 7.1 %collective-permute-done.1.b_ref = f32[32,32,256]{2,1,0:T(8,128)S(1)} collective-permute-done((f32[32,32,256]{2,1,0:T(8,128)}, f32[32,32,256]{2,1,0:T(8,128)S(1)}, u32[]{:S(2)}, u32[]{:S(2)}) %collective-permute-start.1) | collective-permute-done | bytes 1048608 | tf_op jit(solution)/shard_map/ppermute | solution.py:422
  127.9 7.4 %correlate.2 = f32[32,32,256]{2,1,0:T(8,128)} custom-call(bf16[512,768]{1,0:T(8,128)(2,1)S(1)} %copy-done.4, f32[3,2,256,128]{3,2,1,0:T(8,128)S(1)} %copy-done.2, f32[4,2,256,256]{3,2,1,0:T(8,128)} %copy-done.5, f32[32,32,256]{2,1,0:T(8,128)S(1)} %collective-permute-done.1.b_ref), custom_call_target="tpu_custom_call" | custom-call | flops 3221225472 | bytes 3145728 | tf_op jit(solution)/shard_map/correlate/pallas_call | solution.py:290
  135.3 0.0 copy-start
  135.3 0.0 copy-start.1
  135.3 0.0 all-to-all-done.3.values
  135.3 5.5 %all-to-all-start.2 = ((f32[32,32,256]{2,1,0:T(8,128)}), f32[32,32,256]{2,1,0:T(8,128)S(1)}, u32[]{:S(2)}, u32[]{:S(2)}) async-start(f32[32,32,256]{2,1,0:T(8,128)} %correlate.2), calls=%async_computation.2 | async-start | bytes 2097152 | tf_op jit(solution)/shard_map/all_to_all | solution.py:419
  140.8 0.0 copy-done
  140.8 0.0 copy-done.1
  140.9 8.9 %scatter.2.before = f32[6,8192,128]{2,1,0:T(8,128)} custom-call(s32[8192]{0:T(1024)S(1)} %or_bitcast_fusion.row_of, s32[64,128]{1,0:T(8,128)S(1)} %copy-done, f32[32,32,256]{2,1,0:T(8,128)S(1)} %all-to-all-done.3.values), custom_call_target="tpu_custom_call" | custom-call | flops 8192000 | bytes 32768000 | tf_op jit(solution)/shard_map/scatter/pallas_call | solution.py:395
  149.8 8.0 %all-to-all-done.2.values = f32[32,32,256]{2,1,0:T(8,128)S(1)} async-done(((f32[32,32,256]{2,1,0:T(8,128)}), f32[32,32,256]{2,1,0:T(8,128)S(1)}, u32[]{:S(2)}, u32[]{:S(2)}) %all-to-all-start.2) | async-done | bytes 1048608 | tf_op jit(solution)/shard_map/all_to_all | solution.py:419
  157.8 9.3 %scatter.3 = f32[2,16,32768]{2,1,0:T(8,128)} custom-call(s32[8192]{0:T(1024)S(1)} %or_bitcast_fusion.1.row_of, s32[64,128]{1,0:T(8,128)S(1)} %copy-done.1, f32[32,32,256]{2,1,0:T(8,128)S(1)} %all-to-all-done.2.values, f32[6,8192,128]{2,1,0:T(8,128)} %scatter.2.before), custom_call_target="tpu_custom_call" | custom-call | flops 8192000 | bytes 32768000 | tf_op jit(solution)/shard_map/scatter/pallas_call | solution.py:395
  (2 shorter events, 0.0 us)
Async XLA Ops:
  1.0 12.2 %collective-permute-start = (s32[65536]{0:T(1024)S(1)}, s32[65536]{0:T(1024)S(1)}, u32[]{:S(2)}, u32[]{:S(2)}) collective-permute-start(s32[65536]{0:T(1024)S(1)} %pad_add_fusion), channel_id=1, source_target_pairs={{0,96},{32,64},{64,32},{96,0},{1,97},{33,65},{65,33},{97,1},{2,98}... | collective-permute-start | bytes 786440 | tf_op jit(solution)/shard_map/ppermute | solution.py:411
  13.1 0.7 copy-start.6
  29.4 37.2 %all-to-all-start.1 = ((f32[32,64,256]{2,1,0:T(8,128)}), f32[32,64,256]{2,1,0:T(8,128)S(1)}, u32[]{:S(2)}, u32[]{:S(2)}) async-start(f32[32,64,256]{2,1,0:T(8,128)} %get-tuple-element.17), calls=%async_computation.1 | async-start | bytes 4194304 | tf_op jit(solution)/shard_map/all_to_all | solution.py:419
  66.6 33.6 %all-to-all-start = ((f32[32,64,256]{2,1,0:T(8,128)}), f32[32,64,256]{2,1,0:T(8,128)}, u32[]{:S(2)}, u32[]{:S(2)}) async-start(f32[32,64,256]{2,1,0:T(8,128)} %get-tuple-element.16), calls=%async_computation | async-start | bytes 4194304 | tf_op jit(solution)/shard_map/all_to_all | solution.py:419
  73.3 29.8 %collective-permute-start.2 = (f32[32,32,256]{2,1,0:T(8,128)}, f32[32,32,256]{2,1,0:T(8,128)S(1)}, u32[]{:S(2)}, u32[]{:S(2)}) collective-permute-start(f32[32,32,256]{2,1,0:T(8,128)} %get-tuple-element.21), channel_id=1, source_target_pairs={{0,96},{32,64},{64,32},{96,0},{1,97},{33,65},{65,33},{97,1},{2,98}... | collective-permute-start | bytes 3145736 | tf_op jit(solution)/shard_map/ppermute | solution.py:422
  79.5 23.6 %copy-start.2 = (f32[3,2,256,128]{3,2,1,0:T(8,128)S(1)}, f32[3,2,256,128]{3,2,1,0:T(8,128)}, u32[]{:S(2)}) copy-start(f32[3,2,256,128]{3,2,1,0:T(8,128)} %constant.19.clone.turn) | copy-start | bytes 2359300
  100.3 2.9 %copy-start.3 = (bf16[512,768]{1,0:T(8,128)(2,1)S(1)}, bf16[512,768]{1,0:T(8,128)(2,1)}, u32[]{:S(2)}) copy-start(bf16[512,768]{1,0:T(8,128)(2,1)} %constant.18.clone.matrix) | copy-start | bytes 2359300
  102.7 25.2 %collective-permute-start.1 = (f32[32,32,256]{2,1,0:T(8,128)}, f32[32,32,256]{2,1,0:T(8,128)S(1)}, u32[]{:S(2)}, u32[]{:S(2)}) collective-permute-start(f32[32,32,256]{2,1,0:T(8,128)} %slice.10), channel_id=1, source_target_pairs={{0,96},{32,64},{64,32},{96,0},{1,97},{33,65},{65,33},{97,1},{2,98}... | collective-permute-start | bytes 3145736 | tf_op jit(solution)/shard_map/ppermute | solution.py:422
  110.5 24.8 %all-to-all-start.3 = ((f32[32,32,256]{2,1,0:T(8,128)}), f32[32,32,256]{2,1,0:T(8,128)S(1)}, u32[]{:S(2)}, u32[]{:S(2)}) async-start(f32[32,32,256]{2,1,0:T(8,128)} %correlate.3), calls=%async_computation.3 | async-start | bytes 2097152 | tf_op jit(solution)/shard_map/all_to_all | solution.py:419
  115.2 1.1 copy-start.4
  119.4 1.3 copy-start.5
  135.3 5.5 %copy-start = (s32[64,128]{1,0:T(8,128)S(1)}, s32[64,128]{1,0:T(8,128)}, u32[]{:S(2)}) copy-start(s32[64,128]{1,0:T(8,128)} %get-tuple-element.19.column) | copy-start | bytes 98308
  135.3 5.5 %copy-start.1 = (s32[64,128]{1,0:T(8,128)S(1)}, s32[64,128]{1,0:T(8,128)}, u32[]{:S(2)}) copy-start(s32[64,128]{1,0:T(8,128)} %get-tuple-element.15.column) | copy-start | bytes 98308
  135.3 22.5 %all-to-all-start.2 = ((f32[32,32,256]{2,1,0:T(8,128)}), f32[32,32,256]{2,1,0:T(8,128)S(1)}, u32[]{:S(2)}, u32[]{:S(2)}) async-start(f32[32,32,256]{2,1,0:T(8,128)} %correlate.2), calls=%async_computation.2 | async-start | bytes 2097152 | tf_op jit(solution)/shard_map/all_to_all | solution.py:419
